TPU v7x, 32 devices: a whole 2x2x4 slice. The times are simulated.
32 devices in a mesh: dp: 4 (over y, x), ctx: 2 (over core), exp: 4 (over z).
Axes of the slice: x: 2, y: 2, z: 4, core: 2. Of those that a mesh axis runs over, the one named last changes fastest.
Arguments:
- queries: bfloat16 [4, 256, 16, 576], P('dp', 'ctx', 'exp'), may hold values from -7 to 7
- out_grad: bfloat16 [4, 256, 16, 512], P('dp', 'ctx', 'exp'), may hold values from -6 to 6
- latent_keys: bfloat16 [4, 256, 576], P('dp', 'ctx'), may hold values from -9 to 9
- kv_gain: float32 [512], replicated, may hold values from 0.5 to 2
- query_groups: int32 [4, 2], P('dp'), may hold values from 0 to 1, each once within a row
Outputs:
- grad_queries: bfloat16 [4, 256, 16, 576], P('dp', 'ctx', 'exp')
- grad_keys: float32 [4, 2, 128, 576], P('dp', 'ctx', 'exp')
- grad_gain: float32 [512], replicated
Inputs may be any that keep to these rules, and one draw needn't show every extreme that they name: `query_groups`: each row names each group index once.
All inputs are finite; a program needn't handle non-finite values.
Results may differ from a plain program's by a relative error of at most 0.0049.
Values may be sent and summed in bfloat16 or wider, within the bound.
No kernel may reach another device: no remote copies, remote signals or barrier semaphores. Data moves between devices by JAX's collectives and lax.ppermute only.
A program may use at most 64 MiB of HBM per device.

v0:
```python
import math

import jax
import jax.numpy as jnp
from jax import lax
from jax.sharding import PartitionSpec as P

LATENT = 512


SOFTMAX_SCALE = (0.1 * math.log(40.0) + 1.0) ** 2 / math.sqrt(192.0)
MASKED_SCORE = -1e30


def body(queries, out_grad, latent_keys, kv_gain, query_groups):
    own_keys = latent_keys[0]
    rows_q, head_count, key_width = (queries.shape[1], queries.shape[2], queries.shape[3])
    rows_k = own_keys.shape[0]
    rows_all = rows_q * head_count
    query_rows = queries[0].reshape(rows_all, key_width)
    grad_rows = out_grad[0].reshape(rows_all, LATENT)
    group_now = query_groups[0, lax.axis_index("ctx")]
    offsets = jnp.arange(rows_q, dtype=jnp.int32)
    query_pos = jnp.repeat(group_now * rows_q + offsets, head_count)
    last_row = group_now * rows_q + rows_q - 1
    ctx_count = lax.axis_size("ctx")
    key_total = rows_k * ctx_count

    def score_block(key_piece):
        scores = (
            jnp.einsum("qd,kd->qk", query_rows, key_piece, preferred_element_type=jnp.float32)
            * SOFTMAX_SCALE
        )
        grad_prob = jnp.einsum(
            "qe,ke->qk", grad_rows, key_piece[:, :LATENT], preferred_element_type=jnp.float32
        )
        key_pos = jnp.arange(key_piece.shape[0], dtype=jnp.int32)
        visible = key_pos[None, :] <= query_pos[:, None]
        return (jnp.where(visible, scores, MASKED_SCORE), grad_prob, visible)

    def keep_state(current):
        return current

    stats_init = (
        jnp.full((rows_all,), MASKED_SCORE, jnp.float32),
        jnp.zeros((rows_all,), jnp.float32),
        jnp.zeros((rows_all,), jnp.float32),
    )
    key_piece = lax.all_gather(own_keys, "ctx", axis=0, tiled=True)

    def stats_update(current):
        row_max, row_sum, weighted = current
        scores, grad_prob, visible = score_block(key_piece)
        new_max = jnp.maximum(row_max, jnp.max(scores, axis=1))
        exponent = jnp.where(visible, jnp.exp(scores - new_max[:, None]), 0.0)
        return (new_max, jnp.sum(exponent, axis=1), jnp.sum(exponent * grad_prob, axis=1))

    row_max, row_sum, weighted = lax.cond(
        jnp.int32(0) <= last_row, stats_update, keep_state, stats_init
    )
    row_delta = weighted / row_sum
    grads_init = (
        jnp.zeros((rows_all, key_width), jnp.float32),
        jnp.zeros((key_total, key_width), jnp.float32),
    )
    grads_key_piece = lax.all_gather(own_keys, "ctx", axis=0, tiled=True)

    def grads_update(current):
        scores, grad_prob, visible = score_block(grads_key_piece)
        weights = jnp.where(visible, jnp.exp(scores - row_max[:, None]) / row_sum[:, None], 0.0)
        dscore = (weights * (grad_prob - row_delta[:, None])).astype(jnp.bfloat16)
        weights_low = weights.astype(jnp.bfloat16)
        grad_query = (
            jnp.dot(dscore, grads_key_piece, preferred_element_type=jnp.float32) * SOFTMAX_SCALE
        )
        key_part = (
            jnp.einsum("qk,qd->kd", dscore, query_rows, preferred_element_type=jnp.float32)
            * SOFTMAX_SCALE
        )
        value_part = jnp.einsum(
            "qk,qe->ke", weights_low, grad_rows, preferred_element_type=jnp.float32
        )
        key_part = key_part + jnp.pad(value_part, ((0, 0), (0, key_width - LATENT)))
        return (grad_query, key_part)

    grad_query, grad_keys = lax.cond(jnp.int32(0) <= last_row, grads_update, keep_state, grads_init)
    grad_queries = grad_query.astype(jnp.bfloat16).reshape(1, rows_q, head_count, key_width)
    exp_count = lax.axis_size("exp")
    share = rows_k // exp_count
    summed = lax.psum_scatter(grad_keys, ("ctx", "exp"), scatter_dimension=0, tiled=True).reshape(
        1, share, key_width
    )
    key_slice = lax.dynamic_slice_in_dim(own_keys, lax.axis_index("exp") * share, share, 0)
    gain_terms = jnp.sum(summed[0, :, :LATENT] * key_slice[:, :LATENT].astype(jnp.float32), axis=0)
    grad_gain = lax.psum(gain_terms, ("dp", "ctx", "exp")) / kv_gain
    return (grad_queries, summed.reshape(1, 1, share, key_width), grad_gain)


def solution(mesh):
    in_specs = (
        P("dp", "ctx", "exp", None),
        P("dp", "ctx", "exp", None),
        P("dp", "ctx", None),
        P(),
        P("dp", None),
    )
    out_specs = (P("dp", "ctx", "exp", None), P("dp", "ctx", "exp", None), P())
    return jax.shard_map(body, mesh=mesh, in_specs=in_specs, out_specs=out_specs, check_vma=False)
```

profile of v0, /device:TPU:0, one launch (start us, length us, event | category | flops | bytes accessed | tf_op | source)
XLA Modules:
  0.0 106.8 jit_solution(17918854650872762580)
XLA Ops:
  7.2 1.2 %fusion.19 = s32[1,1]{1,0:T(1,128)} fusion(s32[1,2]{1,0:T(1,128)} %param.13, s32[]{:T(128)S(6)} %select_n.21), kind=kLoop, calls=%fused_computation.33 | loop fusion | flops 1 | bytes 12 | tf_op jit(solution)/shard_map/mul | solution.py:25
  8.5 0.6 iota_add_fusion
  9.1 1.6 %copy.16 = bf16[1,128,4,576]{3,2,1,0:T(4,128)(2,1)S(1)} copy(bf16[1,128,4,576]{1,3,2,0:T(8,128)(2,1)} %param.9) | data formatting | bytes 1179648 | tf_op args[0]
  10.7 0.3 reshape_squeeze.6
  11.1 0.7 copy-done.2
  11.9 0.8 copy-done.1
  12.8 2.1 %all-gather = bf16[1,256,576]{2,1,0:T(8,128)(2,1)S(1)} all-gather(bf16[1,128,576]{2,1,0:T(8,128)(2,1)S(1)} %copy.17), channel_id=2, replica_groups=mesh['dp'=4,'ctx'=2,'exp'=4] {'ctx'}, dimensions={1}, use_global_device_ids=true | all-gather | bytes 442368 | tf_op jit(solution)/shard_map/all_gather | solution.py:66
  15.7 3.0 %conditional.2 = (f32[512]{0:T(512)}, f32[512]{0:T(512)S(1)}, f32[512]{0:T(512)S(1)}) conditional(s32[]{:T(128)} %convert_element_type.24, () %tuple.29, (s32[128,4]{1,0:T(8,128)S(1)}, bf16[512,576]{1,0:T(8,128)(2,1)S(1)}, bf16[256,576]{1,0:T(8,128)(2,1)S(1)}, bf16[512,512]{1,0:T(8,128)(2,1)S(1)}) %tuple.44), branch_computations={%region_0.0_spmd, %region_1.5_spmd} | conditional | flops 286915584 | bytes 3268632 | solution.py:58
  15.8 0.4 fusion.18
  16.2 0.6 broadcast_maximum_fusion
  16.8 1.1 fusion.1
  17.9 0.8 fusion.2
  18.7 4.0 %conditional.3 = (f32[256,576]{0,1:T(8,128)S(1)}, bf16[1,128,4,576]{1,3,2,0:T(8,128)(2,1)S(1)}) conditional(s32[]{:T(128)} %convert_element_type.24, () %tuple.28, (s32[128,4]{1,0:T(8,128)S(1)}, bf16[512,576]{1,0:T(8,128)(2,1)S(1)}, bf16[256,576]{1,0:T(8,128)(2,1)S(1)}, f32[512]{0:T(512)}, f32[512]{0:T(512)S(1)}, ...), branch_computations={%region_5.6_spmd, %region_6.7_spmd} | conditional | flops 723616256 | bytes 11225104 | solution.py:86
  18.8 1.1 %fusion.10 = f32[512,256]{1,0:T(8,128)S(1)} fusion(bf16[512,576]{1,0:T(8,128)(2,1)S(1)} %get-tuple-element.45, bf16[256,576]{1,0:T(8,128)(2,1)S(1)} %get-tuple-element.46, f32[512]{0:T(512)S(1)} %get-tuple-element.48, f32[512]{0:T(512)} %get-tuple-element.47, s32[512]{0:T(512)S(1)} %le.33), kind=kOutput, calls=%fused_computation.18 | convolution fusion | flops 151781376 | bytes 1415168 | tf_op jit(solution)/shard_map/cond/branch_1_fun/qd,kd->qk/dot_general | solution.py:31
  20.0 0.3 fusion.12
  20.3 0.3 fusion.13
  20.6 0.4 fusion.5
  21.0 0.4 fusion.4
  21.9 0.8 copy.23
  22.7 1.1 %copy.18 = f32[256,576]{1,0:T(8,128)} copy(f32[256,576]{0,1:T(8,128)S(1)} %get-tuple-element.63) | data formatting | bytes 1179648 | tf_op jit(solution)/shard_map/cond | solution.py:86
  24.0 35.5 %reduce-scatter.2.cloned.1.call-done = f32[32,576]{1,0:T(8,128)} async-done(((f32[256,576]{1,0:T(8,128)}), f32[32,576]{1,0:T(8,128)}) %reduce-scatter.2.cloned.1.call-update) | async-done | bytes 73744 | tf_op jit(solution)/shard_map/reduce_scatter | solution.py:90
  59.6 0.9 fusion.17
  60.4 38.9 %psum.7 = f32[512]{0:T(512)S(1)} all-reduce(f32[512]{0:T(512)S(1)} %fusion.17), channel_id=1, replica_groups=mesh['dp'=4,'ctx'=2,'exp'=4] {'dp','ctx','exp'}, use_global_device_ids=true, to_apply=%region_9.10 | all-reduce | flops 512 | bytes 4096 | tf_op jit(solution)/shard_map/psum | solution.py:95
  99.4 0.6 div.18
  (18 shorter events, 1.3 us)
Async XLA Ops:
  7.2 52.4 %reduce-scatter.2.cloned.1.call-start = ((), (), s32[]{:S(2)}) async-start(), calls=%async_computation.1 | async-start | bytes 737280 | tf_op jit(solution)/shard_map/reduce_scatter | solution.py:90
  10.7 1.0 copy-start.2
  11.8 0.9 copy-start.1
  22.7 1.1 %copy-start = (bf16[1,128,4,576]{1,3,2,0:T(8,128)(2,1)}, bf16[1,128,4,576]{1,3,2,0:T(8,128)(2,1)S(1)}, u32[]{:S(2)}) copy-start(bf16[1,128,4,576]{1,3,2,0:T(8,128)(2,1)S(1)} %get-tuple-element.70) | copy-start | bytes 1769476
  23.8 75.6 %copy-start.3 = (f32[512]{0:T(512)S(1)}, f32[512]{0:T(512)}, u32[]{:S(2)}) copy-start(f32[512]{0:T(512)} %param.12) | copy-start | bytes 6148
Sparse Core Ops, SparseCore 0:
  23.9 35.6 reduce-scatter.1
where the time goes:
time: 107 us
  blocking collectives  41 us (38%)
  waiting for transfers between devices  35.5 us (33%)
  between operations  14.8 us (14%)
  local copies, waits for them, and re-layouts  6.55 us (6%)
  other arithmetic  4.74 us (4%)
  matrix products  4.02 us (4%)
    psum x1, blocking collectives, body(): grad_gain = lax.psum(gain_terms, ('dp', 'ctx', 'exp')) / kv_gain  38.9 us
    reduce_scatter x1, waiting for transfers between devices, body(): lax.psum_scatter(grad_keys, ('ctx', 'exp'), scatter_dimension=0, tiled=True)  35.5 us
    unnamed x10, local copies, waits for them, and re-layouts  3.24 us
  transfers between devices with their start and end apart: 1, of which 1 were waited for; matrix products, arithmetic and copies ran while one was open for 0% of the time, Pallas kernels for 0%

commit v1 on v0

v1 whole, which is shorter than its diff:
```python
import math

import jax
import jax.numpy as jnp
from jax import lax
from jax.experimental import pallas as pl
from jax.experimental.pallas import tpu as pltpu
from jax.sharding import PartitionSpec as P

LATENT = 512
SOFTMAX_SCALE = (0.1 * math.log(40.0) + 1.0) ** 2 / math.sqrt(192.0)
MASKED_SCORE = -1e30
TAIL = 64
TAIL_ROWS = LATENT // TAIL

NT = (((1,), (1,)), ((), ()))
F32, BF16 = jnp.float32, jnp.bfloat16


def shift(value, axis, step):
    size = lax.axis_size(axis)
    return lax.ppermute(value, axis, [(i, (i - step) % size) for i in range(size)])


EXP_STEPS = ((2, 3, 1, 0), (3, 2, 0, 1), (1, 0, 3, 2))
DP_STEPS = ((1, 3, 0, 2), (2, 0, 3, 1), (3, 2, 1, 0))


def exchange_steps(steps, size):
    if size == 4:
        return steps
    return tuple(tuple((i + k) % size for i in range(size)) for k in range(1, size))


def target_of(place, step):
    size = len(step)
    if size != 4:
        return lax.rem(place + step[0], size)
    target = jnp.int32(step[0])
    for i in range(1, size):
        target = jnp.where(place == i, step[i], target)
    return target


def send_step(value, axis, step):
    return lax.ppermute(value, axis, list(enumerate(step)))


def dot(a, b):
    return jnp.dot(a, b, preferred_element_type=F32)


def dot_nt(a, b):
    return lax.dot_general(a, b, NT, preferred_element_type=F32)


def gain_tail(gain):
    high = gain.astype(BF16).astype(F32)
    return jnp.concatenate(
        [
            part[:, r * TAIL : (r + 1) * TAIL]
            for part in (high, gain - high)
            for r in range(TAIL_ROWS)
        ],
        axis=0,
    ).astype(BF16)


def tail_gain(tail):
    tail = tail[:TAIL_ROWS] + tail[TAIL_ROWS:]
    return jnp.concatenate([tail[r : r + 1] for r in range(TAIL_ROWS)], axis=1)


def write_tail(ref, tail):
    rows, width = ref.shape
    if rows > 2 * TAIL_ROWS:
        ref[2 * TAIL_ROWS :, width - TAIL :] = jnp.zeros((rows - 2 * TAIL_ROWS, TAIL), BF16)
    ref[: 2 * TAIL_ROWS, width - TAIL :] = tail


def block_scores(keys, queries_t, grads, first_key, query_pos):
    scores = dot(keys, queries_t) * SOFTMAX_SCALE
    grad_prob = dot_nt(keys[:, :LATENT], grads)
    key_pos = first_key + lax.broadcasted_iota(jnp.int32, scores.shape, 0)
    return jnp.where(key_pos <= query_pos, scores, MASKED_SCORE), grad_prob


def own_scores_kernel(
    groups_hbm, kv_gain_hbm, q_hbm, g_hbm, key_hbm,
    queries_ref, grads_ref, keys_ref, scores_ref, grad_prob_ref, query_pos_ref, kv_gain_ref,
    groups, g_ref, key_ref, copied,
):
    heads, _, rows_q = q_hbm.shape
    rows_k = key_ref.shape[1]
    q_copies = [
        pltpu.make_async_copy(
            q_hbm.at[h], queries_ref.at[:, pl.ds(h * rows_q, rows_q)], copied.at[4 + h]
        )
        for h in range(heads)
    ]
    key_copy = pltpu.make_async_copy(key_hbm, key_ref, copied.at[0])
    groups_copy = pltpu.make_async_copy(groups_hbm, groups, copied.at[1])
    g_copy = pltpu.make_async_copy(g_hbm, g_ref, copied.at[2])
    gain_copy = pltpu.make_async_copy(kv_gain_hbm, kv_gain_ref, copied.at[3])
    for copy in (key_copy, groups_copy, g_copy, *q_copies, gain_copy):
        copy.start()

    key_copy.wait()
    keys = key_ref[...].T
    keys_ref[...] = keys
    g_copy.wait()
    grads = jnp.swapaxes(g_ref[...], 0, 1).reshape(heads * rows_q, LATENT)
    grads_ref[...] = grads
    groups_copy.wait()
    place = lax.axis_index("ctx")
    query_pos = groups[0, place] * rows_q + lax.rem(
        lax.broadcasted_iota(jnp.int32, (1, heads * rows_q), 1), rows_q
    )
    query_pos_ref[...] = query_pos
    for copy in q_copies:
        copy.wait()
    scores_ref[...], grad_prob_ref[...] = block_scores(
        keys, queries_ref[...], grads, place * rows_k, query_pos
    )
    gain_copy.wait()


def softmax_kernel(ctx_count, *refs):
    queries_ref, grads_ref, keys_ref, scores_ref, grad_prob_ref, query_pos_ref = refs[:6]
    peer_refs = refs[6 : 5 + ctx_count]
    dscore_ref, own_ref, gain_ref = refs[5 + ctx_count : 8 + ctx_count]
    send_refs = refs[8 + ctx_count :]
    rows_k = keys_ref.shape[0]
    place = lax.axis_index("ctx")
    queries_t = queries_ref[...]
    grads = grads_ref[...]

    keys = [keys_ref[...]] + [ref[...].T for ref in peer_refs]
    blocks = [(scores_ref[...], grad_prob_ref[...])]
    for b in range(1, ctx_count):
        first_key = lax.rem(place + b, ctx_count) * rows_k
        blocks.append(block_scores(keys[b], queries_t, grads, first_key, query_pos_ref[...]))
    scores = jnp.concatenate([block[0] for block in blocks], axis=0)
    grad_prob = jnp.concatenate([block[1] for block in blocks], axis=0)
    row_max = jnp.max(scores, axis=0, keepdims=True)
    exponent = jnp.where(scores > MASKED_SCORE, jnp.exp(scores - row_max), 0.0)
    weights = exponent * (1.0 / jnp.sum(exponent, axis=0, keepdims=True))
    row_delta = jnp.sum(weights * grad_prob, axis=0, keepdims=True)
    dscore = (weights * (grad_prob - row_delta)).astype(BF16)
    weights_low = weights.astype(BF16)
    dscore_ref[...] = dscore

    key_part = dot_nt(dscore, queries_t) * SOFTMAX_SCALE
    latent_part = key_part[:, :LATENT] + dot(weights_low, grads)
    all_keys = jnp.concatenate(keys, axis=0)[:, :LATENT]
    gain = jnp.sum(latent_part * all_keys.astype(F32), axis=0, keepdims=True)
    gain_ref[...] = gain
    tail = gain_tail(gain)
    width = key_part.shape[1]
    for b in range(ctx_count):
        rows = slice(b * rows_k, (b + 1) * rows_k)
        target = own_ref if b == 0 else send_refs[b - 1]
        target[:, :LATENT] = latent_part[rows].astype(target.dtype)
        target[:, LATENT:width] = key_part[rows, LATENT:].astype(target.dtype)
        if b:
            write_tail(target, tail)


def grad_queries_kernel(*refs):
    dscore_ref, *key_refs, dq_ref = refs
    heads, _, rows_q = dq_ref.shape
    keys_t = jnp.concatenate([ref[...] for ref in key_refs], axis=1)
    dq_t = dot(keys_t, dscore_ref[...]) * SOFTMAX_SCALE
    for h in range(heads):
        dq_ref[h] = dq_t[:, h * rows_q : (h + 1) * rows_q].astype(BF16)


def pair_kernel(ctx_count, exp_count, *refs):
    own_ref, gain_ref = refs[:2]
    recv_refs = refs[2 : 1 + ctx_count]
    kept_ref, gain_out = refs[1 + ctx_count : 3 + ctx_count]
    send_refs = refs[3 + ctx_count : -1]
    total = refs[-1]
    share, width = kept_ref.shape
    value = own_ref[...]
    gain = gain_ref[...]
    for ref in recv_refs:
        value = value + ref[:, :width].astype(F32)
        gain = gain + tail_gain(ref[: 2 * TAIL_ROWS, width:].astype(F32))
    total[...] = value.reshape(total.shape)
    gain_out[...] = gain
    tail = gain_tail(gain)
    place = lax.axis_index("exp")
    kept_ref[...] = total[place]
    for step, ref in zip(exchange_steps(EXP_STEPS, exp_count), send_refs):
        if ref.shape[0] > share:
            ref[...] = jnp.zeros(ref.shape, ref.dtype)
        ref[:share, :width] = total[target_of(place, step)].astype(BF16)
        write_tail(ref, tail)


def gain_kernel(*refs):
    gain_ref, *recv_refs, gain_out = refs
    tail = jnp.zeros((2 * TAIL_ROWS, TAIL), F32)
    for ref in recv_refs:
        tail = tail + ref[: 2 * TAIL_ROWS, ref.shape[1] - TAIL :].astype(F32)
    gain_out[...] = gain_ref[...] + tail_gain(tail)


def final_kernel(gain_count, *refs):
    gain_refs = refs[:gain_count]
    kv_gain_ref, kept_ref, *recv_refs, out_ref, gain_out = refs[gain_count:]
    share, width = kept_ref.shape
    rows = kept_ref[...]
    for ref in recv_refs:
        rows = rows + ref[:share, :width].astype(F32)
    out_ref[...] = rows
    gain = gain_refs[0][...]
    for ref in gain_refs[1:]:
        gain = gain + ref[...]
    gain_out[...] = gain / kv_gain_ref[...]


def call(kernel, out_shapes, operands, flops, scratch=(), fetch=False):
    space = pl.ANY if fetch else pltpu.VMEM
    size = sum(x.size * x.dtype.itemsize for x in (*operands, *out_shapes))
    if fetch:
        out_shapes = [pltpu.VMEM(x.shape, x.dtype) for x in out_shapes]
    return pl.pallas_call(
        kernel,
        out_shape=list(out_shapes),
        in_specs=[pl.BlockSpec(memory_space=space)] * len(operands),
        out_specs=[pl.BlockSpec(memory_space=pltpu.VMEM)] * len(out_shapes),
        scratch_shapes=list(scratch),
        compiler_params=pltpu.CompilerParams(vmem_limit_bytes=(56 if fetch else 48) * 2**20),
        cost_estimate=pl.CostEstimate(flops=flops, bytes_accessed=size, transcendentals=0),
    )(*operands)


def body(queries, out_grad, latent_keys, kv_gain, query_groups):
    ctx_count = lax.axis_size("ctx")
    exp_count = lax.axis_size("exp")
    _, rows_q, heads, width = queries.shape
    rows_k = latent_keys.shape[1]
    share = rows_k // exp_count
    keys_all = rows_k * ctx_count
    rows_all = rows_q * heads
    both = width + LATENT

    def f32(*shape):
        return jax.ShapeDtypeStruct(shape, F32)

    def bf16(*shape):
        return jax.ShapeDtypeStruct(shape, BF16)

    own_keys = latent_keys[0].T
    peer_keys = [shift(own_keys, "ctx", b) for b in range(1, ctx_count)]

    *prepared, query_pos, kv_gain_row = call(
        own_scores_kernel,
        [
            bf16(width, rows_all),
            bf16(rows_all, LATENT),
            bf16(rows_k, width),
            f32(rows_k, rows_all),
            f32(rows_k, rows_all),
            jax.ShapeDtypeStruct((1, rows_all), jnp.int32),
            f32(1, LATENT),
        ],
        [
            query_groups,
            kv_gain.reshape(1, LATENT),
            jnp.transpose(queries[0], (1, 2, 0)),
            out_grad[0],
            own_keys,
        ],
        2 * rows_all * rows_k * both,
        [
            pltpu.SMEM(query_groups.shape, jnp.int32),
            pltpu.VMEM((rows_q, heads, LATENT), BF16),
            pltpu.VMEM((width, rows_k), BF16),
            pltpu.SemaphoreType.DMA((4 + heads,)),
        ],
        fetch=True,
    )
    dscore, own, gain, *sends = call(
        lambda *refs: softmax_kernel(ctx_count, *refs),
        [bf16(keys_all, rows_all), f32(rows_k, width), f32(1, LATENT)]
        + [bf16(rows_k, width + TAIL)] * (ctx_count - 1),
        [*prepared, query_pos, *peer_keys],
        2 * rows_all * (2 * keys_all - rows_k) * both,
    )
    received = [shift(sends[b - 1], "ctx", -b) for b in range(1, ctx_count)]
    (dq_t,) = call(
        grad_queries_kernel,
        [bf16(heads, width, rows_q)],
        [dscore, own_keys, *peer_keys],
        2 * rows_all * keys_all * width,
    )
    message = bf16(max(share, 2 * TAIL_ROWS), width + TAIL)
    exp_steps = exchange_steps(EXP_STEPS, exp_count)
    kept, gain, *sends = call(
        lambda *refs: pair_kernel(ctx_count, exp_count, *refs),
        [f32(share, width), f32(1, LATENT)] + [message] * len(exp_steps),
        [own, gain, *received],
        rows_k * width * ctx_count,
        [pltpu.VMEM((exp_count, share, width), F32)],
    )
    received = [send_step(send, "exp", step) for send, step in zip(sends, exp_steps)]
    (gain,) = call(gain_kernel, [f32(1, LATENT)], [gain, *received], LATENT * exp_count)
    gains = [gain] + [
        send_step(gain, "dp", step)
        for step in reversed(exchange_steps(DP_STEPS, lax.axis_size("dp")))
    ]
    grad_keys, grad_gain = call(
        lambda *refs: final_kernel(len(gains), *refs),
        [f32(share, width), f32(1, LATENT)],
        [*gains, kv_gain_row, kept, *received],
        share * width * exp_count,
    )
    grad_queries = jnp.transpose(dq_t, (2, 0, 1))[None]
    return (grad_queries, grad_keys[None, None], grad_gain.reshape(LATENT))


def solution(mesh):
    in_specs = (
        P("dp", "ctx", "exp", None),
        P("dp", "ctx", "exp", None),
        P("dp", "ctx", None),
        P(),
        P("dp", None),
    )
    out_specs = (P("dp", "ctx", "exp", None), P("dp", "ctx", "exp", None), P())
    return jax.shard_map(body, mesh=mesh, in_specs=in_specs, out_specs=out_specs, check_vma=False)
```

time: 107 us -> 22.3 us (0.21)
  blocking collectives: 41 us -> 0 us
  waiting for transfers between devices: 35.5 us -> 5.89 us
  between operations: 14.8 us -> 0.66 us
  starting transfers between devices: 0.04 us -> 10.5 us
  local copies, waits for them, and re-layouts: 6.55 us -> 0.01 us
  Pallas kernels: 0 us -> 5.12 us
  other arithmetic: 4.74 us -> 0 us
  matrix products: 4.02 us -> 0 us
    psum x1 -> x0, blocking collectives: 38.9 us -> none  [body(): grad_gain = lax.psum(gain_terms, ('dp', 'ctx', 'exp')) / kv_gain]
    reduce_scatter x1 -> x0, waiting for transfers between devices: 35.5 us -> none  [body(): lax.psum_scatter(grad_keys, ('ctx', 'exp'), scatter_dimension=0, tiled=True)]
    ppermute x0 -> x8, starting transfers between devices: none -> 10.5 us  [the longest x6 9.94 us: send_step(): return lax.ppermute(value, axis, list(enumerate(step)))]
    ppermute x0 -> x8, waiting for transfers between devices: none -> 5.89 us  [the longest x6 4.56 us: send_step(): return lax.ppermute(value, axis, list(enumerate(step)))]
    pallas_call x0 -> x6, Pallas kernels: none -> 5.12 us  [call(): pl.pallas_call(kernel, out_shape=list(out_shapes), in_specs=[pl.BlockSpec...]
    dot_general x7 -> x0, matrix products: 4.02 us -> none  [the longest x2 1.56 us: score_block(): jnp.einsum('qd,kd->qk', query_rows, key_piece, preferred_element_type=jnp...]
    unnamed x10 -> x2, local copies, waits for them, and re-layouts: 3.24 us -> 0.01 us
    all_gather x1 -> x0, blocking collectives: 2.13 us -> none  [body(): grads_key_piece = lax.all_gather(own_keys, 'ctx', axis=0, tiled=True)]
  transfers between devices with their start and end apart: 1 -> 8, of which waited for: 1 -> 4; matrix products, arithmetic and copies ran while one was open for 0% -> 0% of each run, Pallas kernels for 0% -> 13%
where the time goes in v1:
time: 22.3 us; the launch traced here: 22.2 us
  starting transfers between devices  10.5 us (47%)
  waiting for transfers between devices  5.89 us (26%)
  Pallas kernels  5.12 us (23%)
  between operations  0.66 us (3%)
    ppermute x6, starting transfers between devices, send_step(): return lax.ppermute(value, axis, list(enumerate(step)))  9.94 us
    pallas_call x6, Pallas kernels, call(): pl.pallas_call(kernel, out_shape=list(out_shapes), in_specs=[pl.BlockSpec...  5.12 us
    ppermute x6, waiting for transfers between devices, send_step(): return lax.ppermute(value, axis, list(enumerate(step)))  4.56 us
    ppermute x2, waiting for transfers between devices, shift(): lax.ppermute(value, axis, [(i, (i - step) % size) for i in range(size)])  1.34 us
    ppermute x2, starting transfers between devices, shift(): lax.ppermute(value, axis, [(i, (i - step) % size) for i in range(size)])  0.59 us
  transfers between devices with their start and end apart: 8, of which 4 were waited for; matrix products, arithmetic and copies ran while one was open for 0% of the time, Pallas kernels for 13%

profile of v1, /device:TPU:0, one launch (start us, length us, event | category | flops | bytes accessed | tf_op | source)
XLA Modules:
  0.0 22.2 jit_solution(5754020989646790881)
XLA Ops:
  0.6 0.5 %collective-permute-start = (bf16[576,128]{1,0:T(8,128)(2,1)}, bf16[576,128]{1,0:T(8,128)(2,1)S(1)}, u32[]{:S(2)}, u32[]{:S(2)}) collective-permute-start(bf16[576,128]{1,0:T(8,128)(2,1)} %bitcast.13), channel_id=1, source_target_pairs={{0,4},{4,0},{1,5},{5,1},{2,6},{6,2},{3,7},{7,3},{8,12},{12,8},{9,1... | collective-permute-start | bytes 442376 | tf_op jit(solution)/shard_map/ppermute | solution.py:22
  1.1 1.8 %shard_map.76 = (bf16[576,512]{1,0:T(8,128)(2,1)S(1)}, bf16[512,512]{1,0:T(8,128)(2,1)S(1)}, bf16[128,576]{1,0:T(8,128)(2,1)S(1)}, f32[128,512]{1,0:T(8,128)S(1)...) custom-call(s32[1,2]{1,0:T(1,128)} %groups_hbm.1, f32[1,512]{1,0:T(1,128)} %bitcast.19, ...), custom_call_target="tpu_custom_call" | custom-call | flops 142606336 | bytes 3053576 | tf_op jit(solution)/shard_map/pallas_call | solution.py:229
  2.9 0.0 collective-permute-done.refs_6_.refs_2_
  3.0 1.2 %shard_map.77 = (bf16[256,512]{1,0:T(8,128)(2,1)S(1)}, f32[128,576]{1,0:T(8,128)S(1)}, f32[1,512]{1,0:T(1,128)S(1)}, bf16[128,640]{1,0:T(8,128)(2,1)S(1)}) custom-call(bf16[576,512]{1,0:T(8,128)(2,1)S(1)} %get-tuple-element.21.refs_0_, bf16[512,512]{1,0:T(8,128)(2,1)S(1)} %get-tuple-element.22.refs_1_, bf16[128,576]{1,0:T(8,128)(2,1)S(1)} %get-tuple-element.23.refs_2_, ...), custom_call_target="tpu_custom_call" | custom-call | flops 427819008 | bytes 2658304 | tf_op jit(solution)/shard_map/pallas_call | solution.py:229
  4.2 0.1 collective-permute-start.1
  4.2 1.3 %collective-permute-done.1.refs_2_ = bf16[128,640]{1,0:T(8,128)(2,1)S(1)} collective-permute-done((bf16[128,640]{1,0:T(8,128)(2,1)S(1)}, bf16[128,640]{1,0:T(8,128)(2,1)S(1)}, u32[]{:S(2)}, u32[]{:S(2)}) %collective-permute-start.1) | collective-permute-done | bytes 163872 | tf_op jit(solution)/shard_map/ppermute | solution.py:22
  5.6 0.0 copy-start
  5.6 0.2 %shard_map.79 = (f32[32,576]{1,0:T(8,128)S(1)}, f32[1,512]{1,0:T(1,128)S(1)}, bf16[32,640]{1,0:T(8,128)(2,1)S(1)}, bf16[32,640]{1,0:T(8,128)(2,1)S(1)}, bf16[32,640]{1,0:T(8,128)(2,1)S(1)}) custom-call(f32[128,576]{1,0:T(8,128)S(1)} %get-tuple-element.28.refs_0_, f32[1,512]{1,0:T(1,128)S(1)} %get-tuple-element.29.refs_1_, ...), custom_call_target="tpu_custom_call" | custom-call | flops 147456 | bytes 659456 | tf_op jit(solution)/shard_map/pallas_call | solution.py:229
  5.8 3.8 %collective-permute-start.2 = (bf16[32,640]{1,0:T(8,128)(2,1)S(1)}, bf16[32,640]{1,0:T(8,128)(2,1)S(1)}, u32[]{:S(2)}, u32[]{:S(2)}) collective-permute-start(bf16[32,640]{1,0:T(8,128)(2,1)S(1)} %get-tuple-element.32), channel_id=1, source_target_pairs={{0,2},{1,3},{2,1},{3,0},{4,6},{5,7},{6,5},{7,4},{8,10},{9,11},{10,... | collective-permute-start | bytes 122888 | tf_op jit(solution)/shard_map/ppermute | solution.py:46
  9.6 1.1 %collective-permute-start.3 = (bf16[32,640]{1,0:T(8,128)(2,1)S(1)}, bf16[32,640]{1,0:T(8,128)(2,1)S(1)}, u32[]{:S(2)}, u32[]{:S(2)}) collective-permute-start(bf16[32,640]{1,0:T(8,128)(2,1)S(1)} %get-tuple-element.33), channel_id=1, source_target_pairs={{0,3},{1,2},{2,0},{3,1},{4,7},{5,6},{6,4},{7,5},{8,11},{9,10},{10,... | collective-permute-start | bytes 122888 | tf_op jit(solution)/shard_map/ppermute | solution.py:46
  10.7 0.5 %collective-permute-start.4 = (bf16[32,640]{1,0:T(8,128)(2,1)S(1)}, bf16[32,640]{1,0:T(8,128)(2,1)S(1)}, u32[]{:S(2)}, u32[]{:S(2)}) collective-permute-start(bf16[32,640]{1,0:T(8,128)(2,1)S(1)} %get-tuple-element.34), channel_id=1, source_target_pairs={{0,1},{1,0},{2,3},{3,2},{4,5},{5,4},{6,7},{7,6},{8,9},{9,8},{10,11... | collective-permute-start | bytes 122888 | tf_op jit(solution)/shard_map/ppermute | solution.py:46
  11.2 1.6 %collective-permute-done.2.refs_1_.refs_6_ = bf16[32,640]{1,0:T(8,128)(2,1)S(1)} collective-permute-done((bf16[32,640]{1,0:T(8,128)(2,1)S(1)}, bf16[32,640]{1,0:T(8,128)(2,1)S(1)}, u32[]{:S(2)}, u32[]{:S(2)}) %collective-permute-start.2) | collective-permute-done | bytes 40992 | tf_op jit(solution)/shard_map/ppermute | solution.py:46
  12.8 2.1 %collective-permute-done.3.refs_2_.refs_7_ = bf16[32,640]{1,0:T(8,128)(2,1)S(1)} collective-permute-done((bf16[32,640]{1,0:T(8,128)(2,1)S(1)}, bf16[32,640]{1,0:T(8,128)(2,1)S(1)}, u32[]{:S(2)}, u32[]{:S(2)}) %collective-permute-start.3) | collective-permute-done | bytes 40992 | tf_op jit(solution)/shard_map/ppermute | solution.py:46
  14.9 0.0 collective-permute-done.4.refs_3_.refs_8_
  14.9 0.1 shard_map.80.refs_0_
  15.0 1.6 %collective-permute-start.7 = (f32[1,512]{1,0:T(1,128)S(1)}, f32[1,512]{1,0:T(1,128)S(1)}, u32[]{:S(2)}, u32[]{:S(2)}) collective-permute-start(f32[1,512]{1,0:T(1,128)S(1)} %shard_map.80.refs_0_), channel_id=1, source_target_pairs={{0,8},{8,24},{16,0},{24,16},{1,9},{9,25},{17,1},{25,17},{2,10},{10... | collective-permute-start | bytes 6152 | tf_op jit(solution)/shard_map/ppermute | solution.py:46
  16.6 0.4 %collective-permute-start.6 = (f32[1,512]{1,0:T(1,128)S(1)}, f32[1,512]{1,0:T(1,128)S(1)}, u32[]{:S(2)}, u32[]{:S(2)}) collective-permute-start(f32[1,512]{1,0:T(1,128)S(1)} %shard_map.80.refs_0_), channel_id=1, source_target_pairs={{0,16},{8,0},{16,24},{24,8},{1,17},{9,1},{17,25},{25,9},{2,18},{10... | collective-permute-start | bytes 6152 | tf_op jit(solution)/shard_map/ppermute | solution.py:46
  17.0 2.6 %collective-permute-start.5 = (f32[1,512]{1,0:T(1,128)S(1)}, f32[1,512]{1,0:T(1,128)S(1)}, u32[]{:S(2)}, u32[]{:S(2)}) collective-permute-start(f32[1,512]{1,0:T(1,128)S(1)} %shard_map.80.refs_0_), channel_id=1, source_target_pairs={{0,24},{8,16},{16,8},{24,0},{1,25},{9,17},{17,9},{25,1},{2,26},{10... | collective-permute-start | bytes 6152 | tf_op jit(solution)/shard_map/ppermute | solution.py:46
  19.6 0.0 copy-done
  19.6 1.1 %shard_map.78 = bf16[4,576,128]{2,1,0:T(8,128)(2,1)} custom-call(bf16[256,512]{1,0:T(8,128)(2,1)S(1)} %get-tuple-element.27.refs_0_, bf16[576,128]{1,0:T(8,128)(2,1)S(1)} %bitcast.15, bf16[576,128]{1,0:T(8,128)(2,1)S(1)} %collective-permute-done.refs_6_.refs_2_), custom_call_target="tpu_custom_call" | custom-call | flops 150994944 | bytes 1146880 | tf_op jit(solution)/shard_map/pallas_call | solution.py:229
  20.7 0.0 collective-permute-done.7.refs_3_
  20.7 0.0 collective-permute-done.6.refs_2_
  20.7 0.8 %collective-permute-done.5.refs_1_ = f32[1,512]{1,0:T(1,128)S(1)} collective-permute-done((f32[1,512]{1,0:T(1,128)S(1)}, f32[1,512]{1,0:T(1,128)S(1)}, u32[]{:S(2)}, u32[]{:S(2)}) %collective-permute-start.5) | collective-permute-done | bytes 2080 | tf_op jit(solution)/shard_map/ppermute | solution.py:46
  21.5 0.7 %shard_map.81 = (f32[32,576]{1,0:T(8,128)}, f32[1,512]{1,0:T(1,128)}) custom-call(f32[1,512]{1,0:T(1,128)S(1)} %shard_map.80.refs_0_, f32[1,512]{1,0:T(1,128)S(1)} %collective-permute-done.5.refs_1_, f32[1,512]{1,0:T(1,128)S(1)} %collective-permute-done.6.refs_2_, f32[1,512]{1,0:T(1,128)S(1)} %collective-permute-done.7.refs_3_, ...), custom_call_target="tpu_custom_call" | custom-call | flops 73728 | bytes 282624 | tf_op jit(solution)/shard_map/pallas_call | solution.py:229
Async XLA Ops:
  0.6 2.3 %collective-permute-start = (bf16[576,128]{1,0:T(8,128)(2,1)}, bf16[576,128]{1,0:T(8,128)(2,1)S(1)}, u32[]{:S(2)}, u32[]{:S(2)}) collective-permute-start(bf16[576,128]{1,0:T(8,128)(2,1)} %bitcast.13), channel_id=1, source_target_pairs={{0,4},{4,0},{1,5},{5,1},{2,6},{6,2},{3,7},{7,3},{8,12},{12,8},{9,1... | collective-permute-start | bytes 442376 | tf_op jit(solution)/shard_map/ppermute | solution.py:22
  4.2 1.4 %collective-permute-start.1 = (bf16[128,640]{1,0:T(8,128)(2,1)S(1)}, bf16[128,640]{1,0:T(8,128)(2,1)S(1)}, u32[]{:S(2)}, u32[]{:S(2)}) collective-permute-start(bf16[128,640]{1,0:T(8,128)(2,1)S(1)} %get-tuple-element.30), channel_id=1, source_target_pairs={{0,4},{4,0},{1,5},{5,1},{2,6},{6,2},{3,7},{7,3},{8,12},{12,8},{9,1... | collective-permute-start | bytes 491528 | tf_op jit(solution)/shard_map/ppermute | solution.py:22
  5.6 14.0 %copy-start = (bf16[1,128,576]{1,2,0:T(8,128)(2,1)S(1)}, bf16[1,128,576]{1,2,0:T(8,128)(2,1)}, u32[]{:S(2)}) copy-start(bf16[1,128,576]{1,2,0:T(8,128)(2,1)} %param.7) | copy-start | bytes 442372
  5.8 7.0 %collective-permute-start.2 = (bf16[32,640]{1,0:T(8,128)(2,1)S(1)}, bf16[32,640]{1,0:T(8,128)(2,1)S(1)}, u32[]{:S(2)}, u32[]{:S(2)}) collective-permute-start(bf16[32,640]{1,0:T(8,128)(2,1)S(1)} %get-tuple-element.32), channel_id=1, source_target_pairs={{0,2},{1,3},{2,1},{3,0},{4,6},{5,7},{6,5},{7,4},{8,10},{9,11},{10,... | collective-permute-start | bytes 122888 | tf_op jit(solution)/shard_map/ppermute | solution.py:46
  9.6 5.4 %collective-permute-start.3 = (bf16[32,640]{1,0:T(8,128)(2,1)S(1)}, bf16[32,640]{1,0:T(8,128)(2,1)S(1)}, u32[]{:S(2)}, u32[]{:S(2)}) collective-permute-start(bf16[32,640]{1,0:T(8,128)(2,1)S(1)} %get-tuple-element.33), channel_id=1, source_target_pairs={{0,3},{1,2},{2,0},{3,1},{4,7},{5,6},{6,4},{7,5},{8,11},{9,10},{10,... | collective-permute-start | bytes 122888 | tf_op jit(solution)/shard_map/ppermute | solution.py:46
  10.7 4.3 %collective-permute-start.4 = (bf16[32,640]{1,0:T(8,128)(2,1)S(1)}, bf16[32,640]{1,0:T(8,128)(2,1)S(1)}, u32[]{:S(2)}, u32[]{:S(2)}) collective-permute-start(bf16[32,640]{1,0:T(8,128)(2,1)S(1)} %get-tuple-element.34), channel_id=1, source_target_pairs={{0,1},{1,0},{2,3},{3,2},{4,5},{5,4},{6,7},{7,6},{8,9},{9,8},{10,11... | collective-permute-start | bytes 122888 | tf_op jit(solution)/shard_map/ppermute | solution.py:46
  15.0 5.7 %collective-permute-start.7 = (f32[1,512]{1,0:T(1,128)S(1)}, f32[1,512]{1,0:T(1,128)S(1)}, u32[]{:S(2)}, u32[]{:S(2)}) collective-permute-start(f32[1,512]{1,0:T(1,128)S(1)} %shard_map.80.refs_0_), channel_id=1, source_target_pairs={{0,8},{8,24},{16,0},{24,16},{1,9},{9,25},{17,1},{25,17},{2,10},{10... | collective-permute-start | bytes 6152 | tf_op jit(solution)/shard_map/ppermute | solution.py:46
  16.6 4.1 %collective-permute-start.6 = (f32[1,512]{1,0:T(1,128)S(1)}, f32[1,512]{1,0:T(1,128)S(1)}, u32[]{:S(2)}, u32[]{:S(2)}) collective-permute-start(f32[1,512]{1,0:T(1,128)S(1)} %shard_map.80.refs_0_), channel_id=1, source_target_pairs={{0,16},{8,0},{16,24},{24,8},{1,17},{9,1},{17,25},{25,9},{2,18},{10... | collective-permute-start | bytes 6152 | tf_op jit(solution)/shard_map/ppermute | solution.py:46
  17.0 4.5 %collective-permute-start.5 = (f32[1,512]{1,0:T(1,128)S(1)}, f32[1,512]{1,0:T(1,128)S(1)}, u32[]{:S(2)}, u32[]{:S(2)}) collective-permute-start(f32[1,512]{1,0:T(1,128)S(1)} %shard_map.80.refs_0_), channel_id=1, source_target_pairs={{0,24},{8,16},{16,8},{24,0},{1,25},{9,17},{17,9},{25,1},{2,26},{10... | collective-permute-start | bytes 6152 | tf_op jit(solution)/shard_map/ppermute | solution.py:46

commit v2 on v1

--- a/solution.py
+++ b/solution.py
@@ -167,7 +167,8 @@
 
 
 def grad_queries_kernel(*refs):
-    dscore_ref, *key_refs, dq_ref = refs
+    dscore_ref, *key_refs, dq_ref, mark_ref = refs
+    mark_ref[...] = jnp.zeros(mark_ref.shape, F32)
     heads, _, rows_q = dq_ref.shape
     keys_t = jnp.concatenate([ref[...] for ref in key_refs], axis=1)
     dq_t = dot(keys_t, dscore_ref[...]) * SOFTMAX_SCALE
@@ -200,24 +201,32 @@
 
 
 def gain_kernel(*refs):
-    gain_ref, *recv_refs, gain_out = refs
+    gain_ref, _, *recv_refs, gain_out = refs
     tail = jnp.zeros((2 * TAIL_ROWS, TAIL), F32)
     for ref in recv_refs:
         tail = tail + ref[: 2 * TAIL_ROWS, ref.shape[1] - TAIL :].astype(F32)
     gain_out[...] = gain_ref[...] + tail_gain(tail)
 
 
-def final_kernel(gain_count, *refs):
-    gain_refs = refs[:gain_count]
-    kv_gain_ref, kept_ref, *recv_refs, out_ref, gain_out = refs[gain_count:]
+def sum_kernel(*refs):
+    *gain_refs, gain_out = refs
+    gain = gain_refs[0][...]
+    for ref in gain_refs[1:]:
+        gain = gain + ref[...]
+    gain_out[...] = gain
+
+
+def final_kernel(total_count, *refs):
+    total_refs = refs[:total_count]
+    kv_gain_ref, kept_ref, *recv_refs, out_ref, gain_out = refs[total_count:]
     share, width = kept_ref.shape
     rows = kept_ref[...]
     for ref in recv_refs:
         rows = rows + ref[:share, :width].astype(F32)
     out_ref[...] = rows
-    gain = gain_refs[0][...]
-    for ref in gain_refs[1:]:
-        gain = gain + ref[...]
+    gain = total_refs[0][...]
+    if total_count > 1:
+        gain = jnp.where(lax.axis_index("ctx") == 0, total_refs[1][...], gain)
     gain_out[...] = gain / kv_gain_ref[...]
 
 
@@ -291,9 +300,9 @@
         2 * rows_all * (2 * keys_all - rows_k) * both,
     )
     received = [shift(sends[b - 1], "ctx", -b) for b in range(1, ctx_count)]
-    (dq_t,) = call(
+    dq_t, mark = call(
         grad_queries_kernel,
-        [bf16(heads, width, rows_q)],
+        [bf16(heads, width, rows_q), f32(1, 128)],
         [dscore, own_keys, *peer_keys],
         2 * rows_all * keys_all * width,
     )
@@ -307,15 +316,27 @@
         [pltpu.VMEM((exp_count, share, width), F32)],
     )
     received = [send_step(send, "exp", step) for send, step in zip(sends, exp_steps)]
-    (gain,) = call(gain_kernel, [f32(1, LATENT)], [gain, *received], LATENT * exp_count)
+    (gain,) = call(gain_kernel, [f32(1, LATENT)], [gain, mark, *received], LATENT * exp_count)
+
+    dp_steps = exchange_steps(DP_STEPS, lax.axis_size("dp"))
     gains = [gain] + [
-        send_step(gain, "dp", step)
-        for step in reversed(exchange_steps(DP_STEPS, lax.axis_size("dp")))
+        lax.ppermute(
+            gain,
+            ("dp", "ctx"),
+            [
+                (i * ctx_count + c, (to if c or ctx_count != 2 else i) * ctx_count + c)
+                for i, to in enumerate(step)
+                for c in range(ctx_count)
+            ],
+        )
+        for step in reversed(dp_steps)
     ]
+    (gain,) = call(sum_kernel, [f32(1, LATENT)], gains, LATENT * len(gains))
+    totals = [gain] + [shift(gain, "ctx", 1)] * (ctx_count == 2)
     grad_keys, grad_gain = call(
-        lambda *refs: final_kernel(len(gains), *refs),
+        lambda *refs: final_kernel(len(totals), *refs),
         [f32(share, width), f32(1, LATENT)],
-        [*gains, kv_gain_row, kept, *received],
+        [*totals, kv_gain_row, kept, *received],
         share * width * exp_count,
     )
     grad_queries = jnp.transpose(dq_t, (2, 0, 1))[None]

time: 22.3 us -> 26.1 us (1.17)
  starting transfers between devices: 10.5 us -> 15.3 us
  waiting for transfers between devices: 5.89 us -> 4.79 us
    ppermute x2 -> x3, starting transfers between devices: 0.59 us -> 7.97 us  [shift(): lax.ppermute(value, axis, [(i, (i - step) % size) for i in range(size)])]
    ppermute x6 -> x3, starting transfers between devices: 9.94 us -> 5.35 us  [send_step(): return lax.ppermute(value, axis, list(enumerate(step)))]
    ppermute x0 -> x3, starting transfers between devices: none -> 1.98 us  [body(): lax.ppermute(gain, ('dp', 'ctx'), [(i * ctx_count + c, (to if c or ctx_co...]
    ppermute x6 -> x3, waiting for transfers between devices: 4.56 us -> 2.63 us  [send_step(): return lax.ppermute(value, axis, list(enumerate(step)))]
    ppermute x2 -> x3, waiting for transfers between devices: 1.34 us -> 2.16 us  [shift(): lax.ppermute(value, axis, [(i, (i - step) % size) for i in range(size)])]
    pallas_call x6 -> x7, Pallas kernels: 5.12 us -> 5.13 us  [call(): pl.pallas_call(kernel, out_shape=list(out_shapes), in_specs=[pl.BlockSpec...]
  transfers between devices with their start and end apart: 8 -> 9, of which waited for: 4 -> 4; matrix products, arithmetic and copies ran while one was open for 0% -> 0% of each run, Pallas kernels for 13% -> 11%
where the time goes in v2:
time: 26.1 us; the launch traced here: 25.9 us
  starting transfers between devices  15.3 us (59%)
  Pallas kernels  5.13 us (20%)
  waiting for transfers between devices  4.79 us (18%)
  between operations  0.71 us (3%)
    ppermute x3, starting transfers between devices, shift(): lax.ppermute(value, axis, [(i, (i - step) % size) for i in range(size)])  7.97 us
    ppermute x3, starting transfers between devices, send_step(): return lax.ppermute(value, axis, list(enumerate(step)))  5.35 us
    pallas_call x7, Pallas kernels, call(): pl.pallas_call(kernel, out_shape=list(out_shapes), in_specs=[pl.BlockSpec...  5.13 us
    ppermute x3, waiting for transfers between devices, send_step(): return lax.ppermute(value, axis, list(enumerate(step)))  2.63 us
    ppermute x3, waiting for transfers between devices, shift(): lax.ppermute(value, axis, [(i, (i - step) % size) for i in range(size)])  2.16 us
    ppermute x3, starting transfers between devices, body(): lax.ppermute(gain, ('dp', 'ctx'), [(i * ctx_count + c, (to if c or ctx_co...  1.98 us
  transfers between devices with their start and end apart: 9, of which 4 were waited for; matrix products, arithmetic and copies ran while one was open for 0% of the time, Pallas kernels for 11%

profile of v2, /device:TPU:0, one launch (start us, length us, event | category | flops | bytes accessed | tf_op | source)
XLA Modules:
  0.0 25.9 jit_solution(7513592863870974532)
XLA Ops:
  0.6 0.5 %collective-permute-start = (bf16[576,128]{1,0:T(8,128)(2,1)}, bf16[576,128]{1,0:T(8,128)(2,1)S(1)}, u32[]{:S(2)}, u32[]{:S(2)}) collective-permute-start(bf16[576,128]{1,0:T(8,128)(2,1)} %bitcast.13), channel_id=1, source_target_pairs={{0,4},{4,0},{1,5},{5,1},{2,6},{6,2},{3,7},{7,3},{8,12},{12,8},{9,1... | collective-permute-start | bytes 442376 | tf_op jit(solution)/shard_map/ppermute | solution.py:22
  1.1 1.8 %shard_map.76 = (bf16[576,512]{1,0:T(8,128)(2,1)S(1)}, bf16[512,512]{1,0:T(8,128)(2,1)S(1)}, bf16[128,576]{1,0:T(8,128)(2,1)S(1)}, f32[128,512]{1,0:T(8,128)S(1)...) custom-call(s32[1,2]{1,0:T(1,128)} %groups_hbm.1, f32[1,512]{1,0:T(1,128)} %bitcast.18, ...), custom_call_target="tpu_custom_call" | custom-call | flops 142606336 | bytes 3053576 | tf_op jit(solution)/shard_map/pallas_call | solution.py:238
  2.9 0.0 collective-permute-done.refs_6_.refs_2_
  3.0 1.2 %shard_map.77 = (bf16[256,512]{1,0:T(8,128)(2,1)S(1)}, f32[128,576]{1,0:T(8,128)S(1)}, f32[1,512]{1,0:T(1,128)S(1)}, bf16[128,640]{1,0:T(8,128)(2,1)S(1)}) custom-call(bf16[576,512]{1,0:T(8,128)(2,1)S(1)} %get-tuple-element.23.refs_0_, bf16[512,512]{1,0:T(8,128)(2,1)S(1)} %get-tuple-element.24.refs_1_, bf16[128,576]{1,0:T(8,128)(2,1)S(1)} %get-tuple-element.25.refs_2_, ...), custom_call_target="tpu_custom_call" | custom-call | flops 427819008 | bytes 2658304 | tf_op jit(solution)/shard_map/pallas_call | solution.py:238
  4.2 0.1 collective-permute-start.1
  4.2 1.3 %collective-permute-done.1.refs_2_ = bf16[128,640]{1,0:T(8,128)(2,1)S(1)} collective-permute-done((bf16[128,640]{1,0:T(8,128)(2,1)S(1)}, bf16[128,640]{1,0:T(8,128)(2,1)S(1)}, u32[]{:S(2)}, u32[]{:S(2)}) %collective-permute-start.1) | collective-permute-done | bytes 163872 | tf_op jit(solution)/shard_map/ppermute | solution.py:22
  5.6 0.2 shard_map.79
  5.8 3.8 %collective-permute-start.2 = (bf16[32,640]{1,0:T(8,128)(2,1)S(1)}, bf16[32,640]{1,0:T(8,128)(2,1)S(1)}, u32[]{:S(2)}, u32[]{:S(2)}) collective-permute-start(bf16[32,640]{1,0:T(8,128)(2,1)S(1)} %get-tuple-element.36), channel_id=1, source_target_pairs={{0,2},{1,3},{2,1},{3,0},{4,6},{5,7},{6,5},{7,4},{8,10},{9,11},{10,... | collective-permute-start | bytes 122888 | tf_op jit(solution)/shard_map/ppermute | solution.py:46
  9.6 1.1 %collective-permute-start.3 = (bf16[32,640]{1,0:T(8,128)(2,1)S(1)}, bf16[32,640]{1,0:T(8,128)(2,1)S(1)}, u32[]{:S(2)}, u32[]{:S(2)}) collective-permute-start(bf16[32,640]{1,0:T(8,128)(2,1)S(1)} %get-tuple-element.37), channel_id=1, source_target_pairs={{0,3},{1,2},{2,0},{3,1},{4,7},{5,6},{6,4},{7,5},{8,11},{9,10},{10,... | collective-permute-start | bytes 122888 | tf_op jit(solution)/shard_map/ppermute | solution.py:46
  10.7 0.5 %collective-permute-start.4 = (bf16[32,640]{1,0:T(8,128)(2,1)S(1)}, bf16[32,640]{1,0:T(8,128)(2,1)S(1)}, u32[]{:S(2)}, u32[]{:S(2)}) collective-permute-start(bf16[32,640]{1,0:T(8,128)(2,1)S(1)} %get-tuple-element.38), channel_id=1, source_target_pairs={{0,1},{1,0},{2,3},{3,2},{4,5},{5,4},{6,7},{7,6},{8,9},{9,8},{10,11... | collective-permute-start | bytes 122888 | tf_op jit(solution)/shard_map/ppermute | solution.py:46
  11.2 1.1 %shard_map.78 = (bf16[4,576,128]{2,1,0:T(8,128)(2,1)}, f32[1,128]{1,0:T(1,128)S(1)}) custom-call(bf16[256,512]{1,0:T(8,128)(2,1)S(1)} %get-tuple-element.29.refs_0_, bf16[576,128]{1,0:T(8,128)(2,1)S(1)} %bitcast.15, bf16[576,128]{1,0:T(8,128)(2,1)S(1)} %collective-permute-done.refs_6_.refs_2_), custom_call_target="tpu_custom_call" | custom-call | flops 150994944 | bytes 1147392 | tf_op jit(solution)/shard_map/pallas_call | solution.py:238
  12.3 0.5 %collective-permute-done.2.refs_2_.refs_4_ = bf16[32,640]{1,0:T(8,128)(2,1)S(1)} collective-permute-done((bf16[32,640]{1,0:T(8,128)(2,1)S(1)}, bf16[32,640]{1,0:T(8,128)(2,1)S(1)}, u32[]{:S(2)}, u32[]{:S(2)}) %collective-permute-start.2) | collective-permute-done | bytes 40992 | tf_op jit(solution)/shard_map/ppermute | solution.py:46
  12.8 2.1 %collective-permute-done.3.refs_3_.refs_5_ = bf16[32,640]{1,0:T(8,128)(2,1)S(1)} collective-permute-done((bf16[32,640]{1,0:T(8,128)(2,1)S(1)}, bf16[32,640]{1,0:T(8,128)(2,1)S(1)}, u32[]{:S(2)}, u32[]{:S(2)}) %collective-permute-start.3) | collective-permute-done | bytes 40992 | tf_op jit(solution)/shard_map/ppermute | solution.py:46
  14.9 0.0 collective-permute-done.4.refs_4_.refs_6_
  14.9 0.1 shard_map.80.refs_0_
  15.0 0.7 %collective-permute-start.7 = (f32[1,512]{1,0:T(1,128)S(1)}, f32[1,512]{1,0:T(1,128)S(1)}, u32[]{:S(2)}, u32[]{:S(2)}) collective-permute-start(f32[1,512]{1,0:T(1,128)S(1)} %shard_map.80.refs_0_), channel_id=1, source_target_pairs={{0,0},{4,12},{8,8},{12,28},{16,16},{20,4},{24,24},{28,20},{1,1},{5... | collective-permute-start | bytes 6152 | tf_op jit(solution)/shard_map/ppermute | solution.py:323
  15.7 0.7 %collective-permute-start.6 = (f32[1,512]{1,0:T(1,128)S(1)}, f32[1,512]{1,0:T(1,128)S(1)}, u32[]{:S(2)}, u32[]{:S(2)}) collective-permute-start(f32[1,512]{1,0:T(1,128)S(1)} %shard_map.80.refs_0_), channel_id=1, source_target_pairs={{0,0},{4,20},{8,8},{12,4},{16,16},{20,28},{24,24},{28,12},{1,1},{5... | collective-permute-start | bytes 6152 | tf_op jit(solution)/shard_map/ppermute | solution.py:323
  16.3 0.7 %collective-permute-start.5 = (f32[1,512]{1,0:T(1,128)S(1)}, f32[1,512]{1,0:T(1,128)S(1)}, u32[]{:S(2)}, u32[]{:S(2)}) collective-permute-start(f32[1,512]{1,0:T(1,128)S(1)} %shard_map.80.refs_0_), channel_id=1, source_target_pairs={{0,0},{4,28},{8,8},{12,20},{16,16},{20,12},{24,24},{28,4},{1,1},{5... | collective-permute-start | bytes 6152 | tf_op jit(solution)/shard_map/ppermute | solution.py:323
  17.0 0.0 collective-permute-done.7.refs_3_
  17.0 0.0 collective-permute-done.6.refs_2_
  17.0 0.0 collective-permute-done.5.refs_1_
  17.1 7.4 %collective-permute-start.8 = (f32[1,512]{1,0:T(1,128)S(1)}, f32[1,512]{1,0:T(1,128)S(1)}, u32[]{:S(2)}, u32[]{:S(2)}) collective-permute-start(f32[1,512]{1,0:T(1,128)S(1)} %shard_map.81.refs_0_), channel_id=1, source_target_pairs={{0,4},{4,0},{1,5},{5,1},{2,6},{6,2},{3,7},{7,3},{8,12},{12,8},{9,1... | collective-permute-start | bytes 6152 | tf_op jit(solution)/shard_map/ppermute | solution.py:22
  24.4 0.8 %collective-permute-done.8.refs_1_ = f32[1,512]{1,0:T(1,128)S(1)} collective-permute-done((f32[1,512]{1,0:T(1,128)S(1)}, f32[1,512]{1,0:T(1,128)S(1)}, u32[]{:S(2)}, u32[]{:S(2)}) %collective-permute-start.8) | collective-permute-done | bytes 2080 | tf_op jit(solution)/shard_map/ppermute | solution.py:22
  25.3 0.7 %shard_map.82 = (f32[32,576]{1,0:T(8,128)}, f32[1,512]{1,0:T(1,128)}) custom-call(f32[1,512]{1,0:T(1,128)S(1)} %shard_map.81.refs_0_, f32[1,512]{1,0:T(1,128)S(1)} %collective-permute-done.8.refs_1_, f32[1,512]{1,0:T(1,128)S(1)} %get-tuple-element.39.refs_2_, f32[32,576]{1,0:T(8,128)S(1)} %get-tuple-element.40.refs_3_, ...), custom_call_target="tpu_custom_call" | custom-call | flops 73728 | bytes 278528 | tf_op jit(solution)/shard_map/pallas_call | solution.py:238
  (3 shorter events, 0.0 us)
Async XLA Ops:
  0.6 2.3 %collective-permute-start = (bf16[576,128]{1,0:T(8,128)(2,1)}, bf16[576,128]{1,0:T(8,128)(2,1)S(1)}, u32[]{:S(2)}, u32[]{:S(2)}) collective-permute-start(bf16[576,128]{1,0:T(8,128)(2,1)} %bitcast.13), channel_id=1, source_target_pairs={{0,4},{4,0},{1,5},{5,1},{2,6},{6,2},{3,7},{7,3},{8,12},{12,8},{9,1... | collective-permute-start | bytes 442376 | tf_op jit(solution)/shard_map/ppermute | solution.py:22
  4.2 1.4 %collective-permute-start.1 = (bf16[128,640]{1,0:T(8,128)(2,1)S(1)}, bf16[128,640]{1,0:T(8,128)(2,1)S(1)}, u32[]{:S(2)}, u32[]{:S(2)}) collective-permute-start(bf16[128,640]{1,0:T(8,128)(2,1)S(1)} %get-tuple-element.33), channel_id=1, source_target_pairs={{0,4},{4,0},{1,5},{5,1},{2,6},{6,2},{3,7},{7,3},{8,12},{12,8},{9,1... | collective-permute-start | bytes 491528 | tf_op jit(solution)/shard_map/ppermute | solution.py:22
  5.6 5.6 %copy-start = (bf16[1,128,576]{1,2,0:T(8,128)(2,1)S(1)}, bf16[1,128,576]{1,2,0:T(8,128)(2,1)}, u32[]{:S(2)}) copy-start(bf16[1,128,576]{1,2,0:T(8,128)(2,1)} %param.7) | copy-start | bytes 442372
  5.8 7.0 %collective-permute-start.2 = (bf16[32,640]{1,0:T(8,128)(2,1)S(1)}, bf16[32,640]{1,0:T(8,128)(2,1)S(1)}, u32[]{:S(2)}, u32[]{:S(2)}) collective-permute-start(bf16[32,640]{1,0:T(8,128)(2,1)S(1)} %get-tuple-element.36), channel_id=1, source_target_pairs={{0,2},{1,3},{2,1},{3,0},{4,6},{5,7},{6,5},{7,4},{8,10},{9,11},{10,... | collective-permute-start | bytes 122888 | tf_op jit(solution)/shard_map/ppermute | solution.py:46
  9.6 5.4 %collective-permute-start.3 = (bf16[32,640]{1,0:T(8,128)(2,1)S(1)}, bf16[32,640]{1,0:T(8,128)(2,1)S(1)}, u32[]{:S(2)}, u32[]{:S(2)}) collective-permute-start(bf16[32,640]{1,0:T(8,128)(2,1)S(1)} %get-tuple-element.37), channel_id=1, source_target_pairs={{0,3},{1,2},{2,0},{3,1},{4,7},{5,6},{6,4},{7,5},{8,11},{9,10},{10,... | collective-permute-start | bytes 122888 | tf_op jit(solution)/shard_map/ppermute | solution.py:46
  10.7 4.3 %collective-permute-start.4 = (bf16[32,640]{1,0:T(8,128)(2,1)S(1)}, bf16[32,640]{1,0:T(8,128)(2,1)S(1)}, u32[]{:S(2)}, u32[]{:S(2)}) collective-permute-start(bf16[32,640]{1,0:T(8,128)(2,1)S(1)} %get-tuple-element.38), channel_id=1, source_target_pairs={{0,1},{1,0},{2,3},{3,2},{4,5},{5,4},{6,7},{7,6},{8,9},{9,8},{10,11... | collective-permute-start | bytes 122888 | tf_op jit(solution)/shard_map/ppermute | solution.py:46
  15.0 2.0 %collective-permute-start.7 = (f32[1,512]{1,0:T(1,128)S(1)}, f32[1,512]{1,0:T(1,128)S(1)}, u32[]{:S(2)}, u32[]{:S(2)}) collective-permute-start(f32[1,512]{1,0:T(1,128)S(1)} %shard_map.80.refs_0_), channel_id=1, source_target_pairs={{0,0},{4,12},{8,8},{12,28},{16,16},{20,4},{24,24},{28,20},{1,1},{5... | collective-permute-start | bytes 6152 | tf_op jit(solution)/shard_map/ppermute | solution.py:323
  15.7 1.4 %collective-permute-start.6 = (f32[1,512]{1,0:T(1,128)S(1)}, f32[1,512]{1,0:T(1,128)S(1)}, u32[]{:S(2)}, u32[]{:S(2)}) collective-permute-start(f32[1,512]{1,0:T(1,128)S(1)} %shard_map.80.refs_0_), channel_id=1, source_target_pairs={{0,0},{4,20},{8,8},{12,4},{16,16},{20,28},{24,24},{28,12},{1,1},{5... | collective-permute-start | bytes 6152 | tf_op jit(solution)/shard_map/ppermute | solution.py:323
  16.3 0.7 %collective-permute-start.5 = (f32[1,512]{1,0:T(1,128)S(1)}, f32[1,512]{1,0:T(1,128)S(1)}, u32[]{:S(2)}, u32[]{:S(2)}) collective-permute-start(f32[1,512]{1,0:T(1,128)S(1)} %shard_map.80.refs_0_), channel_id=1, source_target_pairs={{0,0},{4,28},{8,8},{12,20},{16,16},{20,12},{24,24},{28,4},{1,1},{5... | collective-permute-start | bytes 6152 | tf_op jit(solution)/shard_map/ppermute | solution.py:323
  17.1 8.2 %collective-permute-start.8 = (f32[1,512]{1,0:T(1,128)S(1)}, f32[1,512]{1,0:T(1,128)S(1)}, u32[]{:S(2)}, u32[]{:S(2)}) collective-permute-start(f32[1,512]{1,0:T(1,128)S(1)} %shard_map.81.refs_0_), channel_id=1, source_target_pairs={{0,4},{4,0},{1,5},{5,1},{2,6},{6,2},{3,7},{7,3},{8,12},{12,8},{9,1... | collective-permute-start | bytes 6152 | tf_op jit(solution)/shard_map/ppermute | solution.py:22

commit v3 on v1

--- a/solution.py
+++ b/solution.py
@@ -12,6 +12,7 @@
 MASKED_SCORE = -1e30
 TAIL = 64
 TAIL_ROWS = LATENT // TAIL
+G_PARTS = 4
 
 NT = (((1,), (1,)), ((), ()))
 F32, BF16 = jnp.float32, jnp.bfloat16
@@ -22,28 +23,51 @@
     return lax.ppermute(value, axis, [(i, (i - step) % size) for i in range(size)])
 
 
-EXP_STEPS = ((2, 3, 1, 0), (3, 2, 0, 1), (1, 0, 3, 2))
-DP_STEPS = ((1, 3, 0, 2), (2, 0, 3, 1), (3, 2, 1, 0))
-
-
-def exchange_steps(steps, size):
-    if size == 4:
-        return steps
+EXP_STEPS = (
+    (4, 5, 0, 7, 6, 1, 2, 3),
+    (1, 2, 3, 0, 5, 7, 4, 6),
+    (3, 0, 1, 2, 7, 6, 5, 4),
+    (2, 3, 6, 1, 0, 4, 7, 5),
+)
+DP_STEPS = ((2, 6, 1, 4, 3, 7, 0, 5), (6, 2, 5, 1, 7, 4, 3, 0), (5, 3, 7, 6, 1, 0, 4, 2))
+
+
+def ring_steps(size):
     return tuple(tuple((i + k) % size for i in range(size)) for k in range(1, size))
 
 
-def target_of(place, step):
-    size = len(step)
-    if size != 4:
-        return lax.rem(place + step[0], size)
+def exp_steps(exp_count, ctx_count):
+    if (exp_count, ctx_count) == (4, 2):
+        return EXP_STEPS
+    return [
+        [c * exp_count + to for c in range(ctx_count) for to in step]
+        for step in ring_steps(exp_count)
+    ]
+
+
+def dp_pairs(dp_count, ctx_count):
+    if (dp_count, ctx_count) == (4, 2):
+        return [
+            [(k % 4 * 2 + k // 4, to % 4 * 2 + to // 4) for k, to in enumerate(step)]
+            for step in DP_STEPS
+        ]
+    return [
+        [(i * ctx_count + c, to * ctx_count + c) for i, to in enumerate(step) for c in range(ctx_count)]
+        for step in ring_steps(dp_count)
+    ]
+
+
+def target_of(core, place, step, exp_count):
+    if step not in EXP_STEPS:
+        return lax.rem(place + step[0], exp_count), True
     target = jnp.int32(step[0])
-    for i in range(1, size):
-        target = jnp.where(place == i, step[i], target)
-    return target
-
-
-def send_step(value, axis, step):
-    return lax.ppermute(value, axis, list(enumerate(step)))
+    for k in range(1, len(step)):
+        target = jnp.where(core * exp_count + place == k, step[k], target)
+    return lax.rem(target, exp_count), target // exp_count == core
+
+
+def send_step(value, step):
+    return lax.ppermute(value, ("ctx", "exp"), list(enumerate(step)))
 
 
 def dot(a, b):
@@ -78,11 +102,14 @@
     ref[: 2 * TAIL_ROWS, width - TAIL :] = tail
 
 
-def block_scores(keys, queries_t, grads, first_key, query_pos):
-    scores = dot(keys, queries_t) * SOFTMAX_SCALE
-    grad_prob = dot_nt(keys[:, :LATENT], grads)
-    key_pos = first_key + lax.broadcasted_iota(jnp.int32, scores.shape, 0)
-    return jnp.where(key_pos <= query_pos, scores, MASKED_SCORE), grad_prob
+def tail_blocks(share):
+    step = min(share, 2 * TAIL_ROWS)
+    return [(j, slice(j * step, (j + 1) * step), step) for j in range(2 * TAIL_ROWS // step)]
+
+
+def masked(products, first_key, query_pos):
+    key_pos = first_key + lax.broadcasted_iota(jnp.int32, products.shape, 0)
+    return jnp.where(key_pos <= query_pos, products * SOFTMAX_SCALE, MASKED_SCORE)
 
 
 def own_scores_kernel(
@@ -94,23 +121,34 @@
     rows_k = key_ref.shape[1]
     q_copies = [
         pltpu.make_async_copy(
-            q_hbm.at[h], queries_ref.at[:, pl.ds(h * rows_q, rows_q)], copied.at[4 + h]
+            q_hbm.at[h], queries_ref.at[:, pl.ds(h * rows_q, rows_q)], copied.at[3 + h]
         )
         for h in range(heads)
     ]
     key_copy = pltpu.make_async_copy(key_hbm, key_ref, copied.at[0])
     groups_copy = pltpu.make_async_copy(groups_hbm, groups, copied.at[1])
-    g_copy = pltpu.make_async_copy(g_hbm, g_ref, copied.at[2])
-    gain_copy = pltpu.make_async_copy(kv_gain_hbm, kv_gain_ref, copied.at[3])
-    for copy in (key_copy, groups_copy, g_copy, *q_copies, gain_copy):
+    part = rows_q // G_PARTS
+    g_copies = [
+        pltpu.make_async_copy(
+            g_hbm.at[pl.ds(p * part, part)],
+            g_ref.at[pl.ds(p * part, part)],
+            copied.at[3 + heads + p],
+        )
+        for p in range(G_PARTS)
+    ]
+    gain_copy = pltpu.make_async_copy(kv_gain_hbm, kv_gain_ref, copied.at[2])
+    for copy in (*g_copies, key_copy, *q_copies, groups_copy, gain_copy):
         copy.start()
 
+    for p, copy in enumerate(g_copies):
+        copy.wait()
+        heads_first = jnp.swapaxes(g_ref[pl.ds(p * part, part)], 0, 1)
+        for h in range(heads):
+            grads_ref[pl.ds(h * rows_q + p * part, part), :] = heads_first[h]
     key_copy.wait()
     keys = key_ref[...].T
     keys_ref[...] = keys
-    g_copy.wait()
-    grads = jnp.swapaxes(g_ref[...], 0, 1).reshape(heads * rows_q, LATENT)
-    grads_ref[...] = grads
+    grad_prob_ref[...] = dot_nt(keys[:, :LATENT], grads_ref[...])
     groups_copy.wait()
     place = lax.axis_index("ctx")
     query_pos = groups[0, place] * rows_q + lax.rem(
@@ -119,9 +157,7 @@
     query_pos_ref[...] = query_pos
     for copy in q_copies:
         copy.wait()
-    scores_ref[...], grad_prob_ref[...] = block_scores(
-        keys, queries_ref[...], grads, place * rows_k, query_pos
-    )
+    scores_ref[...] = masked(dot(keys, queries_ref[...]), place * rows_k, query_pos)
     gain_copy.wait()
 
 
@@ -139,11 +175,12 @@
     blocks = [(scores_ref[...], grad_prob_ref[...])]
     for b in range(1, ctx_count):
         first_key = lax.rem(place + b, ctx_count) * rows_k
-        blocks.append(block_scores(keys[b], queries_t, grads, first_key, query_pos_ref[...]))
+        scores = masked(dot(keys[b], queries_t), first_key, query_pos_ref[...])
+        blocks.append((scores, dot_nt(keys[b][:, :LATENT], grads)))
     scores = jnp.concatenate([block[0] for block in blocks], axis=0)
     grad_prob = jnp.concatenate([block[1] for block in blocks], axis=0)
     row_max = jnp.max(scores, axis=0, keepdims=True)
-    exponent = jnp.where(scores > MASKED_SCORE, jnp.exp(scores - row_max), 0.0)
+    exponent = jnp.exp(scores - row_max)
     weights = exponent * (1.0 / jnp.sum(exponent, axis=0, keepdims=True))
     row_delta = jnp.sum(weights * grad_prob, axis=0, keepdims=True)
     dscore = (weights * (grad_prob - row_delta)).astype(BF16)
@@ -156,18 +193,23 @@
     gain = jnp.sum(latent_part * all_keys.astype(F32), axis=0, keepdims=True)
     gain_ref[...] = gain
     tail = gain_tail(gain)
-    width = key_part.shape[1]
+    blocks, share, width = own_ref.shape
     for b in range(ctx_count):
         rows = slice(b * rows_k, (b + 1) * rows_k)
         target = own_ref if b == 0 else send_refs[b - 1]
-        target[:, :LATENT] = latent_part[rows].astype(target.dtype)
-        target[:, LATENT:width] = key_part[rows, LATENT:].astype(target.dtype)
+        latent_rows = latent_part[rows].reshape(blocks, share, LATENT)
+        rope_rows = key_part[rows, LATENT:].reshape(blocks, share, width - LATENT)
+        target[:, :, :LATENT] = latent_rows.astype(target.dtype)
+        target[:, :, LATENT:width] = rope_rows.astype(target.dtype)
         if b:
-            write_tail(target, tail)
+            target[:, :, width:] = jnp.zeros((blocks, share, TAIL), BF16)
+            for j, part, step in tail_blocks(share):
+                target[j, :step, width:] = tail[part]
 
 
 def grad_queries_kernel(*refs):
-    dscore_ref, *key_refs, dq_ref = refs
+    dscore_ref, *key_refs, dq_ref, mark_ref = refs
+    mark_ref[...] = jnp.zeros(mark_ref.shape, F32)
     heads, _, rows_q = dq_ref.shape
     keys_t = jnp.concatenate([ref[...] for ref in key_refs], axis=1)
     dq_t = dot(keys_t, dscore_ref[...]) * SOFTMAX_SCALE
@@ -175,48 +217,57 @@
         dq_ref[h] = dq_t[:, h * rows_q : (h + 1) * rows_q].astype(BF16)
 
 
-def pair_kernel(ctx_count, exp_count, *refs):
+def pair_kernel(ctx_count, *refs):
     own_ref, gain_ref = refs[:2]
     recv_refs = refs[2 : 1 + ctx_count]
     kept_ref, gain_out = refs[1 + ctx_count : 3 + ctx_count]
-    send_refs = refs[3 + ctx_count : -1]
-    total = refs[-1]
-    share, width = kept_ref.shape
-    value = own_ref[...]
+    send_refs = refs[3 + ctx_count :]
+    exp_count, share, width = own_ref.shape
+
+    def block(i):
+        rows = own_ref[i]
+        for ref in recv_refs:
+            rows = rows + ref[i, :, :width].astype(F32)
+        return rows
+
     gain = gain_ref[...]
     for ref in recv_refs:
-        value = value + ref[:, :width].astype(F32)
-        gain = gain + tail_gain(ref[: 2 * TAIL_ROWS, width:].astype(F32))
-    total[...] = value.reshape(total.shape)
+        tail = [ref[j, :step, width:] for j, _, step in tail_blocks(share)]
+        gain = gain + tail_gain(jnp.concatenate(tail, axis=0).astype(F32))
     gain_out[...] = gain
     tail = gain_tail(gain)
-    place = lax.axis_index("exp")
-    kept_ref[...] = total[place]
-    for step, ref in zip(exchange_steps(EXP_STEPS, exp_count), send_refs):
+    core, place = lax.axis_index("ctx"), lax.axis_index("exp")
+    kept_ref[...] = block(place)
+    for step, ref in zip(exp_steps(exp_count, ctx_count), send_refs):
+        target, sends = target_of(core, place, step, exp_count)
         if ref.shape[0] > share:
             ref[...] = jnp.zeros(ref.shape, ref.dtype)
-        ref[:share, :width] = total[target_of(place, step)].astype(BF16)
-        write_tail(ref, tail)
+        rows = block(target)
+        ref[:share, :width] = jnp.where(sends, rows, jnp.zeros_like(rows)).astype(BF16)
+        write_tail(ref, jnp.where(sends, tail, jnp.zeros_like(tail)))
 
 
 def gain_kernel(*refs):
-    gain_ref, *recv_refs, gain_out = refs
+    gain_ref, _, *recv_refs, gain_out = refs
     tail = jnp.zeros((2 * TAIL_ROWS, TAIL), F32)
     for ref in recv_refs:
         tail = tail + ref[: 2 * TAIL_ROWS, ref.shape[1] - TAIL :].astype(F32)
     gain_out[...] = gain_ref[...] + tail_gain(tail)
 
 
-def final_kernel(gain_count, *refs):
-    gain_refs = refs[:gain_count]
-    kv_gain_ref, kept_ref, *recv_refs, out_ref, gain_out = refs[gain_count:]
+def rows_kernel(*refs):
+    _, kept_ref, *recv_refs, out_ref = refs
     share, width = kept_ref.shape
     rows = kept_ref[...]
     for ref in recv_refs:
         rows = rows + ref[:share, :width].astype(F32)
     out_ref[...] = rows
-    gain = gain_refs[0][...]
-    for ref in gain_refs[1:]:
+
+
+def final_kernel(*refs):
+    kv_gain_ref, gain_ref, *recv_refs, gain_out = refs
+    gain = gain_ref[...]
+    for ref in recv_refs:
         gain = gain + ref[...]
     gain_out[...] = gain / kv_gain_ref[...]
 
@@ -279,44 +330,42 @@
             pltpu.SMEM(query_groups.shape, jnp.int32),
             pltpu.VMEM((rows_q, heads, LATENT), BF16),
             pltpu.VMEM((width, rows_k), BF16),
-            pltpu.SemaphoreType.DMA((4 + heads,)),
+            pltpu.SemaphoreType.DMA((3 + heads + G_PARTS,)),
         ],
         fetch=True,
     )
     dscore, own, gain, *sends = call(
         lambda *refs: softmax_kernel(ctx_count, *refs),
-        [bf16(keys_all, rows_all), f32(rows_k, width), f32(1, LATENT)]
-        + [bf16(rows_k, width + TAIL)] * (ctx_count - 1),
+        [bf16(keys_all, rows_all), f32(exp_count, share, width), f32(1, LATENT)]
+        + [bf16(exp_count, share, width + TAIL)] * (ctx_count - 1),
         [*prepared, query_pos, *peer_keys],
         2 * rows_all * (2 * keys_all - rows_k) * both,
     )
     received = [shift(sends[b - 1], "ctx", -b) for b in range(1, ctx_count)]
-    (dq_t,) = call(
+    dq_t, mark = call(
         grad_queries_kernel,
-        [bf16(heads, width, rows_q)],
+        [bf16(heads, width, rows_q), f32(1, 128)],
         [dscore, own_keys, *peer_keys],
         2 * rows_all * keys_all * width,
     )
     message = bf16(max(share, 2 * TAIL_ROWS), width + TAIL)
-    exp_steps = exchange_steps(EXP_STEPS, exp_count)
+    steps = exp_steps(exp_count, ctx_count)
     kept, gain, *sends = call(
-        lambda *refs: pair_kernel(ctx_count, exp_count, *refs),
-        [f32(share, width), f32(1, LATENT)] + [message] * len(exp_steps),
+        lambda *refs: pair_kernel(ctx_count, *refs),
+        [f32(share, width), f32(1, LATENT)] + [message] * len(steps),
         [own, gain, *received],
         rows_k * width * ctx_count,
-        [pltpu.VMEM((exp_count, share, width), F32)],
-    )
-    received = [send_step(send, "exp", step) for send, step in zip(sends, exp_steps)]
-    (gain,) = call(gain_kernel, [f32(1, LATENT)], [gain, *received], LATENT * exp_count)
-    gains = [gain] + [
-        send_step(gain, "dp", step)
-        for step in reversed(exchange_steps(DP_STEPS, lax.axis_size("dp")))
-    ]
-    grad_keys, grad_gain = call(
-        lambda *refs: final_kernel(len(gains), *refs),
-        [f32(share, width), f32(1, LATENT)],
-        [*gains, kv_gain_row, kept, *received],
-        share * width * exp_count,
+    )
+    received = [send_step(send, step) for send, step in zip(sends, steps)]
+    (gain,) = call(gain_kernel, [f32(1, LATENT)], [gain, mark, *received], LATENT * exp_count)
+
+    pairs = dp_pairs(lax.axis_size("dp"), ctx_count)
+    gains = [lax.ppermute(gain, ("dp", "ctx"), step) for step in reversed(pairs)]
+    (grad_keys,) = call(
+        rows_kernel, [f32(share, width)], [gain, kept, *received], share * width * exp_count
+    )
+    (grad_gain,) = call(
+        final_kernel, [f32(1, LATENT)], [kv_gain_row, gain, *gains], LATENT * len(gains)
     )
     grad_queries = jnp.transpose(dq_t, (2, 0, 1))[None]
     return (grad_queries, grad_keys[None, None], grad_gain.reshape(LATENT))

time: 22.3 us -> 20.3 us (0.910)
  waiting for transfers between devices: 5.89 us -> 3.05 us
  Pallas kernels: 5.12 us -> 5.79 us
    ppermute x6 -> x7, waiting for transfers between devices: 4.56 us -> 1.71 us  [the longest x4 0.87 us: send_step(): return lax.ppermute(value, ('ctx', 'exp'), list(enumerate(step)))]
    pallas_call x6 -> x7, Pallas kernels: 5.12 us -> 5.79 us  [call(): pl.pallas_call(kernel, out_shape=list(out_shapes), in_specs=[pl.BlockSpec...]
    ppermute x6 -> x7, starting transfers between devices: 9.94 us -> 10 us  [the longest x4 5.85 us: send_step(): return lax.ppermute(value, ('ctx', 'exp'), list(enumerate(step)))]
  transfers between devices with their start and end apart: 8 -> 9, of which waited for: 4 -> 4; matrix products, arithmetic and copies ran while one was open for 0% -> 0% of each run, Pallas kernels for 13% -> 18%
where the time goes in v3:
time: 20.3 us; the launch traced here: 20.1 us
  starting transfers between devices  10.6 us (52%)
  Pallas kernels  5.79 us (29%)
  waiting for transfers between devices  3.05 us (15%)
  between operations  0.66 us (3%)
    ppermute x4, starting transfers between devices, send_step(): return lax.ppermute(value, ('ctx', 'exp'), list(enumerate(step)))  5.85 us
    pallas_call x7, Pallas kernels, call(): pl.pallas_call(kernel, out_shape=list(out_shapes), in_specs=[pl.BlockSpec...  5.79 us
    ppermute x3, starting transfers between devices, body(): lax.ppermute(gain, ('dp', 'ctx'), step)  4.18 us
    ppermute x2, waiting for transfers between devices, shift(): lax.ppermute(value, axis, [(i, (i - step) % size) for i in range(size)])  1.34 us
    ppermute x4, waiting for transfers between devices, send_step(): return lax.ppermute(value, ('ctx', 'exp'), list(enumerate(step)))  0.87 us
    ppermute x3, waiting for transfers between devices, body(): lax.ppermute(gain, ('dp', 'ctx'), step)  0.84 us
    ppermute x2, starting transfers between devices, shift(): lax.ppermute(value, axis, [(i, (i - step) % size) for i in range(size)])  0.58 us
  transfers between devices with their start and end apart: 9, of which 4 were waited for; matrix products, arithmetic and copies ran while one was open for 0% of the time, Pallas kernels for 18%

profile of v3, /device:TPU:0, one launch (start us, length us, event | category | flops | bytes accessed | tf_op | source)
XLA Modules:
  0.0 20.1 jit_solution(381010276673330633)
XLA Ops:
  0.6 0.5 %collective-permute-start = (bf16[576,128]{1,0:T(8,128)(2,1)}, bf16[576,128]{1,0:T(8,128)(2,1)S(1)}, u32[]{:S(2)}, u32[]{:S(2)}) collective-permute-start(bf16[576,128]{1,0:T(8,128)(2,1)} %bitcast.13), channel_id=1, source_target_pairs={{0,4},{4,0},{1,5},{5,1},{2,6},{6,2},{3,7},{7,3},{8,12},{12,8},{9,1... | collective-permute-start | bytes 442376 | tf_op jit(solution)/shard_map/ppermute | solution.py:23
  1.1 1.9 %shard_map.76 = (bf16[576,512]{1,0:T(8,128)(2,1)S(1)}, bf16[512,512]{1,0:T(8,128)(2,1)S(1)}, bf16[128,576]{1,0:T(8,128)(2,1)S(1)}, f32[128,512]{1,0:T(8,128)S(1)...) custom-call(s32[1,2]{1,0:T(1,128)} %groups_hbm.1, f32[1,512]{1,0:T(1,128)} %bitcast.19, ...), custom_call_target="tpu_custom_call" | custom-call | flops 142606336 | bytes 3053576 | tf_op jit(solution)/shard_map/pallas_call | solution.py:280
  3.0 0.0 collective-permute-done.refs_6_.refs_2_
  3.0 1.2 %shard_map.77 = (bf16[256,512]{1,0:T(8,128)(2,1)S(1)}, f32[4,32,576]{2,1,0:T(8,128)S(1)}, f32[1,512]{1,0:T(1,128)S(1)}, bf16[4,32,640]{2,1,0:T(8,128)(2,1)S(1)}) custom-call(bf16[576,512]{1,0:T(8,128)(2,1)S(1)} %get-tuple-element.22.refs_0_, bf16[512,512]{1,0:T(8,128)(2,1)S(1)} %get-tuple-element.23.refs_1_, bf16[128,576]{1,0:T(8,128)(2,1)S(1)} %get-tuple-element.24.refs_2_, ...), custom_call_target="tpu_custom_call" | custom-call | flops 427819008 | bytes 2658304 | tf_op jit(solution)/shard_map/pallas_call | solution.py:280
  4.3 0.1 collective-permute-start.1
  4.3 1.3 %collective-permute-done.1.refs_2_ = bf16[4,32,640]{2,1,0:T(8,128)(2,1)S(1)} collective-permute-done((bf16[4,32,640]{2,1,0:T(8,128)(2,1)S(1)}, bf16[4,32,640]{2,1,0:T(8,128)(2,1)S(1)}, u32[]{:S(2)}, u32[]{:S(2)}) %collective-permute-start.1) | collective-permute-done | bytes 163872 | tf_op jit(solution)/shard_map/ppermute | solution.py:23
  5.7 0.2 %shard_map.79 = (f32[32,576]{1,0:T(8,128)S(1)}, f32[1,512]{1,0:T(1,128)S(1)}, bf16[32,640]{1,0:T(8,128)(2,1)S(1)}, bf16[32,640]{1,0:T(8,128)(2,1)S(1)}, bf16[32,...) custom-call(f32[4,32,576]{2,1,0:T(8,128)S(1)} %get-tuple-element.30.refs_0_, f32[1,512]{1,0:T(1,128)S(1)} %get-tuple-element.31.refs_1_, ...), custom_call_target="tpu_custom_call" | custom-call | flops 147456 | bytes 700416 | tf_op jit(solution)/shard_map/pallas_call | solution.py:280
  5.9 0.2 collective-permute-start.2
  6.1 2.9 %collective-permute-start.3 = (bf16[32,640]{1,0:T(8,128)(2,1)S(1)}, bf16[32,640]{1,0:T(8,128)(2,1)S(1)}, u32[]{:S(2)}, u32[]{:S(2)}) collective-permute-start(bf16[32,640]{1,0:T(8,128)(2,1)S(1)} %get-tuple-element.36), channel_id=1, source_target_pairs={{0,1},{1,2},{2,3},{3,0},{4,5},{5,7},{6,4},{7,6},{8,9},{9,10},{10,1... | collective-permute-start | bytes 122888 | tf_op jit(solution)/shard_map/ppermute | solution.py:70
  9.0 2.0 %collective-permute-start.4 = (bf16[32,640]{1,0:T(8,128)(2,1)S(1)}, bf16[32,640]{1,0:T(8,128)(2,1)S(1)}, u32[]{:S(2)}, u32[]{:S(2)}) collective-permute-start(bf16[32,640]{1,0:T(8,128)(2,1)S(1)} %get-tuple-element.37), channel_id=1, source_target_pairs={{0,3},{1,0},{2,1},{3,2},{4,7},{5,6},{6,5},{7,4},{8,11},{9,8},{10,9... | collective-permute-start | bytes 122888 | tf_op jit(solution)/shard_map/ppermute | solution.py:70
  11.0 0.7 %collective-permute-start.5 = (bf16[32,640]{1,0:T(8,128)(2,1)S(1)}, bf16[32,640]{1,0:T(8,128)(2,1)S(1)}, u32[]{:S(2)}, u32[]{:S(2)}) collective-permute-start(bf16[32,640]{1,0:T(8,128)(2,1)S(1)} %get-tuple-element.38), channel_id=1, source_target_pairs={{0,2},{1,3},{2,6},{3,1},{4,0},{5,4},{6,7},{7,5},{8,10},{9,11},{10,... | collective-permute-start | bytes 122888 | tf_op jit(solution)/shard_map/ppermute | solution.py:70
  11.7 1.1 %shard_map.78 = (bf16[4,576,128]{2,1,0:T(8,128)(2,1)}, f32[1,128]{1,0:T(1,128)S(1)}) custom-call(bf16[256,512]{1,0:T(8,128)(2,1)S(1)} %get-tuple-element.28.refs_0_, bf16[576,128]{1,0:T(8,128)(2,1)S(1)} %bitcast.15, bf16[576,128]{1,0:T(8,128)(2,1)S(1)} %collective-permute-done.refs_6_.refs_2_), custom_call_target="tpu_custom_call" | custom-call | flops 150994944 | bytes 1147392 | tf_op jit(solution)/shard_map/pallas_call | solution.py:280
  12.9 0.0 collective-permute-done.2.refs_2_
  12.9 0.3 %collective-permute-done.3.refs_3_ = bf16[32,640]{1,0:T(8,128)(2,1)S(1)} collective-permute-done((bf16[32,640]{1,0:T(8,128)(2,1)S(1)}, bf16[32,640]{1,0:T(8,128)(2,1)S(1)}, u32[]{:S(2)}, u32[]{:S(2)}) %collective-permute-start.3) | collective-permute-done | bytes 40992 | tf_op jit(solution)/shard_map/ppermute | solution.py:70
  13.1 0.6 %collective-permute-done.4.refs_4_ = bf16[32,640]{1,0:T(8,128)(2,1)S(1)} collective-permute-done((bf16[32,640]{1,0:T(8,128)(2,1)S(1)}, bf16[32,640]{1,0:T(8,128)(2,1)S(1)}, u32[]{:S(2)}, u32[]{:S(2)}) %collective-permute-start.4) | collective-permute-done | bytes 40992 | tf_op jit(solution)/shard_map/ppermute | solution.py:70
  13.7 0.0 collective-permute-done.5.refs_5_
  13.7 0.1 shard_map.80.refs_0_.refs_1_
  13.8 1.8 %collective-permute-start.8 = (f32[1,512]{1,0:T(1,128)S(1)}, f32[1,512]{1,0:T(1,128)S(1)}, u32[]{:S(2)}, u32[]{:S(2)}) collective-permute-start(f32[1,512]{1,0:T(1,128)S(1)} %shard_map.80.refs_0_.refs_1_), channel_id=1, source_target_pairs={{0,16},{8,20},{16,8},{24,4},{4,24},{12,28},{20,0},{28,12},{1,17},{... | collective-permute-start | bytes 6152 | tf_op jit(solution)/shard_map/ppermute | solution.py:363
  15.6 0.2 %collective-permute-start.7 = (f32[1,512]{1,0:T(1,128)S(1)}, f32[1,512]{1,0:T(1,128)S(1)}, u32[]{:S(2)}, u32[]{:S(2)}) collective-permute-start(f32[1,512]{1,0:T(1,128)S(1)} %shard_map.80.refs_0_.refs_1_), channel_id=1, source_target_pairs={{0,20},{8,16},{16,12},{24,8},{4,28},{12,4},{20,24},{28,0},{1,21},{... | collective-permute-start | bytes 6152 | tf_op jit(solution)/shard_map/ppermute | solution.py:363
  15.9 2.2 %collective-permute-start.6 = (f32[1,512]{1,0:T(1,128)S(1)}, f32[1,512]{1,0:T(1,128)S(1)}, u32[]{:S(2)}, u32[]{:S(2)}) collective-permute-start(f32[1,512]{1,0:T(1,128)S(1)} %shard_map.80.refs_0_.refs_1_), channel_id=1, source_target_pairs={{0,12},{8,24},{16,28},{24,20},{4,8},{12,0},{20,4},{28,16},{1,13},{... | collective-permute-start | bytes 6152 | tf_op jit(solution)/shard_map/ppermute | solution.py:363
  18.0 0.7 %shard_map.81 = f32[32,576]{1,0:T(8,128)} custom-call(f32[1,512]{1,0:T(1,128)S(1)} %shard_map.80.refs_0_.refs_1_, f32[32,576]{1,0:T(8,128)S(1)} %get-tuple-element.39.refs_1_, bf16[32,640]{1,0:T(8,128)(2,1)S(1)} %collective-permute-done.2.refs_2_, bf16[32,640]{1,0:T(8,128)(2,1)S(1)} %collective-permute-done.3.refs_3_, ...), custom_call_target="tpu_custom_call" | custom-call | flops 73728 | bytes 313344 | tf_op jit(solution)/shard_map/pallas_call | solution.py:280
  18.7 0.0 collective-permute-done.8.refs_4_
  18.7 0.8 %collective-permute-done.7.refs_3_ = f32[1,512]{1,0:T(1,128)S(1)} collective-permute-done((f32[1,512]{1,0:T(1,128)S(1)}, f32[1,512]{1,0:T(1,128)S(1)}, u32[]{:S(2)}, u32[]{:S(2)}) %collective-permute-start.7) | collective-permute-done | bytes 2080 | tf_op jit(solution)/shard_map/ppermute | solution.py:363
  19.5 0.6 %shard_map.82 = f32[1,512]{1,0:T(1,128)} custom-call(f32[1,512]{1,0:T(1,128)S(1)} %get-tuple-element.40.refs_0_, f32[1,512]{1,0:T(1,128)S(1)} %shard_map.80.refs_0_.refs_1_, f32[1,512]{1,0:T(1,128)S(1)} %collective-permute-done.6.refs_2_, f32[1,512]{1,0:T(1,128)S(1)} %collective-permute-done.7.refs_3_, f32[1,512]{1,0:T(1,128)S(1)} %collective-permute-done.8.refs_4_), custom_call_target="tpu_custom_call" | custom-call | flops 1536 | bytes 12288 | tf_op jit(solution)/shard_map/pallas_call | solution.py:280
  (3 shorter events, 0.0 us)
Async XLA Ops:
  0.6 2.4 %collective-permute-start = (bf16[576,128]{1,0:T(8,128)(2,1)}, bf16[576,128]{1,0:T(8,128)(2,1)S(1)}, u32[]{:S(2)}, u32[]{:S(2)}) collective-permute-start(bf16[576,128]{1,0:T(8,128)(2,1)} %bitcast.13), channel_id=1, source_target_pairs={{0,4},{4,0},{1,5},{5,1},{2,6},{6,2},{3,7},{7,3},{8,12},{12,8},{9,1... | collective-permute-start | bytes 442376 | tf_op jit(solution)/shard_map/ppermute | solution.py:23
  4.3 1.4 %collective-permute-start.1 = (bf16[4,32,640]{2,1,0:T(8,128)(2,1)S(1)}, bf16[4,32,640]{2,1,0:T(8,128)(2,1)S(1)}, u32[]{:S(2)}, u32[]{:S(2)}) collective-permute-start(bf16[4,32,640]{2,1,0:T(8,128)(2,1)S(1)} %get-tuple-element.32), channel_id=1, source_target_pairs={{0,4},{4,0},{1,5},{5,1},{2,6},{6,2},{3,7},{7,3},{8,12},{12,8},{9,1... | collective-permute-start | bytes 491528 | tf_op jit(solution)/shard_map/ppermute | solution.py:23
  5.7 6.1 %copy-start = (bf16[1,128,576]{1,2,0:T(8,128)(2,1)S(1)}, bf16[1,128,576]{1,2,0:T(8,128)(2,1)}, u32[]{:S(2)}) copy-start(bf16[1,128,576]{1,2,0:T(8,128)(2,1)} %param.7) | copy-start | bytes 442372
  5.9 7.0 %collective-permute-start.2 = (bf16[32,640]{1,0:T(8,128)(2,1)S(1)}, bf16[32,640]{1,0:T(8,128)(2,1)S(1)}, u32[]{:S(2)}, u32[]{:S(2)}) collective-permute-start(bf16[32,640]{1,0:T(8,128)(2,1)S(1)} %get-tuple-element.35), channel_id=1, source_target_pairs={{0,4},{1,5},{2,0},{3,7},{4,6},{5,1},{6,2},{7,3},{8,12},{9,13},{10,... | collective-permute-start | bytes 122888 | tf_op jit(solution)/shard_map/ppermute | solution.py:70
  6.1 7.1 %collective-permute-start.3 = (bf16[32,640]{1,0:T(8,128)(2,1)S(1)}, bf16[32,640]{1,0:T(8,128)(2,1)S(1)}, u32[]{:S(2)}, u32[]{:S(2)}) collective-permute-start(bf16[32,640]{1,0:T(8,128)(2,1)S(1)} %get-tuple-element.36), channel_id=1, source_target_pairs={{0,1},{1,2},{2,3},{3,0},{4,5},{5,7},{6,4},{7,6},{8,9},{9,10},{10,1... | collective-permute-start | bytes 122888 | tf_op jit(solution)/shard_map/ppermute | solution.py:70
  9.0 4.7 %collective-permute-start.4 = (bf16[32,640]{1,0:T(8,128)(2,1)S(1)}, bf16[32,640]{1,0:T(8,128)(2,1)S(1)}, u32[]{:S(2)}, u32[]{:S(2)}) collective-permute-start(bf16[32,640]{1,0:T(8,128)(2,1)S(1)} %get-tuple-element.37), channel_id=1, source_target_pairs={{0,3},{1,0},{2,1},{3,2},{4,7},{5,6},{6,5},{7,4},{8,11},{9,8},{10,9... | collective-permute-start | bytes 122888 | tf_op jit(solution)/shard_map/ppermute | solution.py:70
  11.0 2.7 %collective-permute-start.5 = (bf16[32,640]{1,0:T(8,128)(2,1)S(1)}, bf16[32,640]{1,0:T(8,128)(2,1)S(1)}, u32[]{:S(2)}, u32[]{:S(2)}) collective-permute-start(bf16[32,640]{1,0:T(8,128)(2,1)S(1)} %get-tuple-element.38), channel_id=1, source_target_pairs={{0,2},{1,3},{2,6},{3,1},{4,0},{5,4},{6,7},{7,5},{8,10},{9,11},{10,... | collective-permute-start | bytes 122888 | tf_op jit(solution)/shard_map/ppermute | solution.py:70
  13.8 4.9 %collective-permute-start.8 = (f32[1,512]{1,0:T(1,128)S(1)}, f32[1,512]{1,0:T(1,128)S(1)}, u32[]{:S(2)}, u32[]{:S(2)}) collective-permute-start(f32[1,512]{1,0:T(1,128)S(1)} %shard_map.80.refs_0_.refs_1_), channel_id=1, source_target_pairs={{0,16},{8,20},{16,8},{24,4},{4,24},{12,28},{20,0},{28,12},{1,17},{... | collective-permute-start | bytes 6152 | tf_op jit(solution)/shard_map/ppermute | solution.py:363
  15.6 3.9 %collective-permute-start.7 = (f32[1,512]{1,0:T(1,128)S(1)}, f32[1,512]{1,0:T(1,128)S(1)}, u32[]{:S(2)}, u32[]{:S(2)}) collective-permute-start(f32[1,512]{1,0:T(1,128)S(1)} %shard_map.80.refs_0_.refs_1_), channel_id=1, source_target_pairs={{0,20},{8,16},{16,12},{24,8},{4,28},{12,4},{20,24},{28,0},{1,21},{... | collective-permute-start | bytes 6152 | tf_op jit(solution)/shard_map/ppermute | solution.py:363
  15.9 3.7 %collective-permute-start.6 = (f32[1,512]{1,0:T(1,128)S(1)}, f32[1,512]{1,0:T(1,128)S(1)}, u32[]{:S(2)}, u32[]{:S(2)}) collective-permute-start(f32[1,512]{1,0:T(1,128)S(1)} %shard_map.80.refs_0_.refs_1_), channel_id=1, source_target_pairs={{0,12},{8,24},{16,28},{24,20},{4,8},{12,0},{20,4},{28,16},{1,13},{... | collective-permute-start | bytes 6152 | tf_op jit(solution)/shard_map/ppermute | solution.py:363

commit v4 on v3

--- a/solution.py
+++ b/solution.py
@@ -12,7 +12,6 @@
 MASKED_SCORE = -1e30
 TAIL = 64
 TAIL_ROWS = LATENT // TAIL
-G_PARTS = 4
 
 NT = (((1,), (1,)), ((), ()))
 F32, BF16 = jnp.float32, jnp.bfloat16
@@ -107,78 +106,57 @@
     return [(j, slice(j * step, (j + 1) * step), step) for j in range(2 * TAIL_ROWS // step)]
 
 
-def masked(products, first_key, query_pos):
-    key_pos = first_key + lax.broadcasted_iota(jnp.int32, products.shape, 0)
-    return jnp.where(key_pos <= query_pos, products * SOFTMAX_SCALE, MASKED_SCORE)
-
-
-def own_scores_kernel(
+def fetch_kernel(
     groups_hbm, kv_gain_hbm, q_hbm, g_hbm, key_hbm,
-    queries_ref, grads_ref, keys_ref, scores_ref, grad_prob_ref, query_pos_ref, kv_gain_ref,
+    queries_ref, grads_ref, keys_ref, query_pos_ref, kv_gain_ref,
     groups, g_ref, key_ref, copied,
 ):
     heads, _, rows_q = q_hbm.shape
-    rows_k = key_ref.shape[1]
     q_copies = [
         pltpu.make_async_copy(
-            q_hbm.at[h], queries_ref.at[:, pl.ds(h * rows_q, rows_q)], copied.at[3 + h]
+            q_hbm.at[h], queries_ref.at[:, pl.ds(h * rows_q, rows_q)], copied.at[4 + h]
         )
         for h in range(heads)
     ]
     key_copy = pltpu.make_async_copy(key_hbm, key_ref, copied.at[0])
     groups_copy = pltpu.make_async_copy(groups_hbm, groups, copied.at[1])
-    part = rows_q // G_PARTS
-    g_copies = [
-        pltpu.make_async_copy(
-            g_hbm.at[pl.ds(p * part, part)],
-            g_ref.at[pl.ds(p * part, part)],
-            copied.at[3 + heads + p],
-        )
-        for p in range(G_PARTS)
-    ]
-    gain_copy = pltpu.make_async_copy(kv_gain_hbm, kv_gain_ref, copied.at[2])
-    for copy in (*g_copies, key_copy, *q_copies, groups_copy, gain_copy):
+    g_copy = pltpu.make_async_copy(g_hbm, g_ref, copied.at[2])
+    gain_copy = pltpu.make_async_copy(kv_gain_hbm, kv_gain_ref, copied.at[3])
+    for copy in (g_copy, key_copy, groups_copy, *q_copies, gain_copy):
         copy.start()
 
-    for p, copy in enumerate(g_copies):
+    g_copy.wait()
+    grads_ref[...] = jnp.swapaxes(g_ref[...], 0, 1).reshape(heads * rows_q, LATENT)
+    key_copy.wait()
+    keys_ref[...] = key_ref[...].T
+    groups_copy.wait()
+    query_pos_ref[...] = groups[0, lax.axis_index("ctx")] * rows_q + lax.rem(
+        lax.broadcasted_iota(jnp.int32, (1, heads * rows_q), 1), rows_q
+    )
+    for copy in (*q_copies, gain_copy):
         copy.wait()
-        heads_first = jnp.swapaxes(g_ref[pl.ds(p * part, part)], 0, 1)
-        for h in range(heads):
-            grads_ref[pl.ds(h * rows_q + p * part, part), :] = heads_first[h]
-    key_copy.wait()
-    keys = key_ref[...].T
-    keys_ref[...] = keys
-    grad_prob_ref[...] = dot_nt(keys[:, :LATENT], grads_ref[...])
-    groups_copy.wait()
-    place = lax.axis_index("ctx")
-    query_pos = groups[0, place] * rows_q + lax.rem(
-        lax.broadcasted_iota(jnp.int32, (1, heads * rows_q), 1), rows_q
-    )
-    query_pos_ref[...] = query_pos
-    for copy in q_copies:
-        copy.wait()
-    scores_ref[...] = masked(dot(keys, queries_ref[...]), place * rows_k, query_pos)
-    gain_copy.wait()
 
 
 def softmax_kernel(ctx_count, *refs):
-    queries_ref, grads_ref, keys_ref, scores_ref, grad_prob_ref, query_pos_ref = refs[:6]
-    peer_refs = refs[6 : 5 + ctx_count]
-    dscore_ref, own_ref, gain_ref = refs[5 + ctx_count : 8 + ctx_count]
-    send_refs = refs[8 + ctx_count :]
+    queries_ref, grads_ref, keys_ref, query_pos_ref = refs[:4]
+    peer_refs = refs[4 : 3 + ctx_count]
+    dscore_ref, own_ref, gain_ref = refs[3 + ctx_count : 6 + ctx_count]
+    send_refs = refs[6 + ctx_count :]
     rows_k = keys_ref.shape[0]
     place = lax.axis_index("ctx")
     queries_t = queries_ref[...]
     grads = grads_ref[...]
-
-    keys = [keys_ref[...]] + [ref[...].T for ref in peer_refs]
-    blocks = [(scores_ref[...], grad_prob_ref[...])]
-    for b in range(1, ctx_count):
-        first_key = lax.rem(place + b, ctx_count) * rows_k
-        scores = masked(dot(keys[b], queries_t), first_key, query_pos_ref[...])
-        blocks.append((scores, dot_nt(keys[b][:, :LATENT], grads)))
-    scores = jnp.concatenate([block[0] for block in blocks], axis=0)
-    grad_prob = jnp.concatenate([block[1] for block in blocks], axis=0)
+    query_pos = query_pos_ref[...]
+
+    keys = jnp.concatenate([keys_ref[...]] + [ref[...].T for ref in peer_refs], axis=0)
+    scores = dot(keys, queries_t) * SOFTMAX_SCALE
+    grad_prob = dot_nt(keys[:, :LATENT], grads)
+    key_row = lax.broadcasted_iota(jnp.int32, (rows_k, scores.shape[1]), 0)
+    visible = jnp.concatenate(
+        [key_row + lax.rem(place + b, ctx_count) * rows_k <= query_pos for b in range(ctx_count)],
+        axis=0,
+    )
+    scores = jnp.where(visible, scores, MASKED_SCORE)
     row_max = jnp.max(scores, axis=0, keepdims=True)
     exponent = jnp.exp(scores - row_max)
     weights = exponent * (1.0 / jnp.sum(exponent, axis=0, keepdims=True))
@@ -189,8 +167,7 @@
 
     key_part = dot_nt(dscore, queries_t) * SOFTMAX_SCALE
     latent_part = key_part[:, :LATENT] + dot(weights_low, grads)
-    all_keys = jnp.concatenate(keys, axis=0)[:, :LATENT]
-    gain = jnp.sum(latent_part * all_keys.astype(F32), axis=0, keepdims=True)
+    gain = jnp.sum(latent_part * keys[:, :LATENT].astype(F32), axis=0, keepdims=True)
     gain_ref[...] = gain
     tail = gain_tail(gain)
     blocks, share, width = own_ref.shape
@@ -308,13 +285,11 @@
     peer_keys = [shift(own_keys, "ctx", b) for b in range(1, ctx_count)]
 
     *prepared, query_pos, kv_gain_row = call(
-        own_scores_kernel,
+        fetch_kernel,
         [
             bf16(width, rows_all),
             bf16(rows_all, LATENT),
             bf16(rows_k, width),
-            f32(rows_k, rows_all),
-            f32(rows_k, rows_all),
             jax.ShapeDtypeStruct((1, rows_all), jnp.int32),
             f32(1, LATENT),
         ],
@@ -325,12 +300,12 @@
             out_grad[0],
             own_keys,
         ],
-        2 * rows_all * rows_k * both,
+        rows_all * width,
         [
             pltpu.SMEM(query_groups.shape, jnp.int32),
             pltpu.VMEM((rows_q, heads, LATENT), BF16),
             pltpu.VMEM((width, rows_k), BF16),
-            pltpu.SemaphoreType.DMA((3 + heads + G_PARTS,)),
+            pltpu.SemaphoreType.DMA((4 + heads,)),
         ],
         fetch=True,
     )
@@ -339,7 +314,7 @@
         [bf16(keys_all, rows_all), f32(exp_count, share, width), f32(1, LATENT)]
         + [bf16(exp_count, share, width + TAIL)] * (ctx_count - 1),
         [*prepared, query_pos, *peer_keys],
-        2 * rows_all * (2 * keys_all - rows_k) * both,
+        4 * rows_all * keys_all * both,
     )
     received = [shift(sends[b - 1], "ctx", -b) for b in range(1, ctx_count)]
     dq_t, mark = call(

time: 20.3 us -> 19.8 us (0.975)
  Pallas kernels: 5.79 us -> 5.35 us
    pallas_call x7, Pallas kernels: 5.79 us -> 5.35 us  [call(): pl.pallas_call(kernel, out_shape=list(out_shapes), in_specs=[pl.BlockSpec...]
  transfers between devices with their start and end apart: 9 -> 9, of which waited for: 4 -> 4; matrix products, arithmetic and copies ran while one was open for 0% -> 0% of each run, Pallas kernels for 18% -> 16%
where the time goes in v4:
time: 19.8 us; the launch traced here: 19.6 us
  starting transfers between devices  10.8 us (55%)
  Pallas kernels  5.35 us (27%)
  waiting for transfers between devices  2.88 us (15%)
  between operations  0.66 us (3%)
    ppermute x4, starting transfers between devices, send_step(): return lax.ppermute(value, ('ctx', 'exp'), list(enumerate(step)))  5.9 us
    pallas_call x7, Pallas kernels, call(): pl.pallas_call(kernel, out_shape=list(out_shapes), in_specs=[pl.BlockSpec...  5.35 us
    ppermute x3, starting transfers between devices, body(): lax.ppermute(gain, ('dp', 'ctx'), step)  4.13 us
    ppermute x2, waiting for transfers between devices, shift(): lax.ppermute(value, axis, [(i, (i - step) % size) for i in range(size)])  1.2 us
    ppermute x3, waiting for transfers between devices, body(): lax.ppermute(gain, ('dp', 'ctx'), step)  0.84 us
    ppermute x4, waiting for transfers between devices, send_step(): return lax.ppermute(value, ('ctx', 'exp'), list(enumerate(step)))  0.84 us
    ppermute x2, starting transfers between devices, shift(): lax.ppermute(value, axis, [(i, (i - step) % size) for i in range(size)])  0.72 us
  transfers between devices with their start and end apart: 9, of which 4 were waited for; matrix products, arithmetic and copies ran while one was open for 0% of the time, Pallas kernels for 16%

profile of v4, /device:TPU:0, one launch (start us, length us, event | category | flops | bytes accessed | tf_op | source)
XLA Modules:
  0.0 19.6 jit_solution(16703499726997377454)
XLA Ops:
  0.6 0.5 %collective-permute-start = (bf16[576,128]{1,0:T(8,128)(2,1)}, bf16[576,128]{1,0:T(8,128)(2,1)S(1)}, u32[]{:S(2)}, u32[]{:S(2)}) collective-permute-start(bf16[576,128]{1,0:T(8,128)(2,1)} %bitcast.13), channel_id=1, source_target_pairs={{0,4},{4,0},{1,5},{5,1},{2,6},{6,2},{3,7},{7,3},{8,12},{12,8},{9,1... | collective-permute-start | bytes 442376 | tf_op jit(solution)/shard_map/ppermute | solution.py:22
  1.1 1.4 %shard_map.76 = (bf16[576,512]{1,0:T(8,128)(2,1)S(1)}, bf16[512,512]{1,0:T(8,128)(2,1)S(1)}, bf16[128,576]{1,0:T(8,128)(2,1)S(1)}, s32[1,512]{1,0:T(1,128)S(1)}, f32[1,512]{1,0:T(1,128)S(1)}) custom-call(s32[1,2]{1,0:T(1,128)} %groups_hbm.1, f32[1,512]{1,0:T(1,128)} %bitcast.19, bf16[4,576,128]{2,1,0:T(8,128)(2,1)} %bitcast.16, ...), custom_call_target="tpu_custom_call" | custom-call | flops 294912 | bytes 2529288 | tf_op jit(solution)/shard_map/pallas_call | solution.py:257
  2.5 0.0 collective-permute-done.refs_4_.refs_2_
  2.5 1.3 %shard_map.77 = (bf16[256,512]{1,0:T(8,128)(2,1)S(1)}, f32[4,32,576]{2,1,0:T(8,128)S(1)}, f32[1,512]{1,0:T(1,128)S(1)}, bf16[4,32,640]{2,1,0:T(8,128)(2,1)S(1)}) custom-call(bf16[576,512]{1,0:T(8,128)(2,1)S(1)} %get-tuple-element.20.refs_0_, bf16[512,512]{1,0:T(8,128)(2,1)S(1)} %get-tuple-element.21.refs_1_, bf16[128,576]{1,0:T(8,128)(2,1)S(1)} %get-tuple-element.22.refs_2_, ...), custom_call_target="tpu_custom_call" | custom-call | flops 570425344 | bytes 2134016 | tf_op jit(solution)/shard_map/pallas_call | solution.py:257
  3.8 0.2 %collective-permute-start.1 = (bf16[4,32,640]{2,1,0:T(8,128)(2,1)S(1)}, bf16[4,32,640]{2,1,0:T(8,128)(2,1)S(1)}, u32[]{:S(2)}, u32[]{:S(2)}) collective-permute-start(bf16[4,32,640]{2,1,0:T(8,128)(2,1)S(1)} %get-tuple-element.28), channel_id=1, source_target_pairs={{0,4},{4,0},{1,5},{5,1},{2,6},{6,2},{3,7},{7,3},{8,12},{12,8},{9,1... | collective-permute-start | bytes 491528 | tf_op jit(solution)/shard_map/ppermute | solution.py:22
  4.0 1.2 %collective-permute-done.1.refs_2_ = bf16[4,32,640]{2,1,0:T(8,128)(2,1)S(1)} collective-permute-done((bf16[4,32,640]{2,1,0:T(8,128)(2,1)S(1)}, bf16[4,32,640]{2,1,0:T(8,128)(2,1)S(1)}, u32[]{:S(2)}, u32[]{:S(2)}) %collective-permute-start.1) | collective-permute-done | bytes 163872 | tf_op jit(solution)/shard_map/ppermute | solution.py:22
  5.2 0.2 %shard_map.79 = (f32[32,576]{1,0:T(8,128)S(1)}, f32[1,512]{1,0:T(1,128)S(1)}, bf16[32,640]{1,0:T(8,128)(2,1)S(1)}, bf16[32,640]{1,0:T(8,128)(2,1)S(1)}, bf16[32,...) custom-call(f32[4,32,576]{2,1,0:T(8,128)S(1)} %get-tuple-element.26.refs_0_, f32[1,512]{1,0:T(1,128)S(1)} %get-tuple-element.27.refs_1_, ...), custom_call_target="tpu_custom_call" | custom-call | flops 147456 | bytes 700416 | tf_op jit(solution)/shard_map/pallas_call | solution.py:257
  5.5 0.2 %collective-permute-start.2 = (bf16[32,640]{1,0:T(8,128)(2,1)S(1)}, bf16[32,640]{1,0:T(8,128)(2,1)S(1)}, u32[]{:S(2)}, u32[]{:S(2)}) collective-permute-start(bf16[32,640]{1,0:T(8,128)(2,1)S(1)} %get-tuple-element.31), channel_id=1, source_target_pairs={{0,4},{1,5},{2,0},{3,7},{4,6},{5,1},{6,2},{7,3},{8,12},{9,13},{10,... | collective-permute-start | bytes 122888 | tf_op jit(solution)/shard_map/ppermute | solution.py:69
  5.7 2.9 %collective-permute-start.3 = (bf16[32,640]{1,0:T(8,128)(2,1)S(1)}, bf16[32,640]{1,0:T(8,128)(2,1)S(1)}, u32[]{:S(2)}, u32[]{:S(2)}) collective-permute-start(bf16[32,640]{1,0:T(8,128)(2,1)S(1)} %get-tuple-element.32), channel_id=1, source_target_pairs={{0,1},{1,2},{2,3},{3,0},{4,5},{5,7},{6,4},{7,6},{8,9},{9,10},{10,1... | collective-permute-start | bytes 122888 | tf_op jit(solution)/shard_map/ppermute | solution.py:69
  8.6 2.0 %collective-permute-start.4 = (bf16[32,640]{1,0:T(8,128)(2,1)S(1)}, bf16[32,640]{1,0:T(8,128)(2,1)S(1)}, u32[]{:S(2)}, u32[]{:S(2)}) collective-permute-start(bf16[32,640]{1,0:T(8,128)(2,1)S(1)} %get-tuple-element.33), channel_id=1, source_target_pairs={{0,3},{1,0},{2,1},{3,2},{4,7},{5,6},{6,5},{7,4},{8,11},{9,8},{10,9... | collective-permute-start | bytes 122888 | tf_op jit(solution)/shard_map/ppermute | solution.py:69
  10.6 0.8 %collective-permute-start.5 = (bf16[32,640]{1,0:T(8,128)(2,1)S(1)}, bf16[32,640]{1,0:T(8,128)(2,1)S(1)}, u32[]{:S(2)}, u32[]{:S(2)}) collective-permute-start(bf16[32,640]{1,0:T(8,128)(2,1)S(1)} %get-tuple-element.34), channel_id=1, source_target_pairs={{0,2},{1,3},{2,6},{3,1},{4,0},{5,4},{6,7},{7,5},{8,10},{9,11},{10,... | collective-permute-start | bytes 122888 | tf_op jit(solution)/shard_map/ppermute | solution.py:69
  11.4 1.1 %shard_map.78 = (bf16[4,576,128]{2,1,0:T(8,128)(2,1)}, f32[1,128]{1,0:T(1,128)S(1)}) custom-call(bf16[256,512]{1,0:T(8,128)(2,1)S(1)} %get-tuple-element.24.refs_0_, bf16[576,128]{1,0:T(8,128)(2,1)S(1)} %bitcast.15, bf16[576,128]{1,0:T(8,128)(2,1)S(1)} %collective-permute-done.refs_4_.refs_2_), custom_call_target="tpu_custom_call" | custom-call | flops 150994944 | bytes 1147392 | tf_op jit(solution)/shard_map/pallas_call | solution.py:257
  12.5 0.0 collective-permute-done.2.refs_2_
  12.5 0.3 %collective-permute-done.3.refs_3_ = bf16[32,640]{1,0:T(8,128)(2,1)S(1)} collective-permute-done((bf16[32,640]{1,0:T(8,128)(2,1)S(1)}, bf16[32,640]{1,0:T(8,128)(2,1)S(1)}, u32[]{:S(2)}, u32[]{:S(2)}) %collective-permute-start.3) | collective-permute-done | bytes 40992 | tf_op jit(solution)/shard_map/ppermute | solution.py:69
  12.8 0.5 %collective-permute-done.4.refs_4_ = bf16[32,640]{1,0:T(8,128)(2,1)S(1)} collective-permute-done((bf16[32,640]{1,0:T(8,128)(2,1)S(1)}, bf16[32,640]{1,0:T(8,128)(2,1)S(1)}, u32[]{:S(2)}, u32[]{:S(2)}) %collective-permute-start.4) | collective-permute-done | bytes 40992 | tf_op jit(solution)/shard_map/ppermute | solution.py:69
  13.3 0.1 shard_map.80.refs_0_.refs_1_
  13.4 1.7 %collective-permute-start.8 = (f32[1,512]{1,0:T(1,128)S(1)}, f32[1,512]{1,0:T(1,128)S(1)}, u32[]{:S(2)}, u32[]{:S(2)}) collective-permute-start(f32[1,512]{1,0:T(1,128)S(1)} %shard_map.80.refs_0_.refs_1_), channel_id=1, source_target_pairs={{0,16},{8,20},{16,8},{24,4},{4,24},{12,28},{20,0},{28,12},{1,17},{... | collective-permute-start | bytes 6152 | tf_op jit(solution)/shard_map/ppermute | solution.py:338
  15.1 0.3 %collective-permute-start.7 = (f32[1,512]{1,0:T(1,128)S(1)}, f32[1,512]{1,0:T(1,128)S(1)}, u32[]{:S(2)}, u32[]{:S(2)}) collective-permute-start(f32[1,512]{1,0:T(1,128)S(1)} %shard_map.80.refs_0_.refs_1_), channel_id=1, source_target_pairs={{0,20},{8,16},{16,12},{24,8},{4,28},{12,4},{20,24},{28,0},{1,21},{... | collective-permute-start | bytes 6152 | tf_op jit(solution)/shard_map/ppermute | solution.py:338
  15.4 2.1 %collective-permute-start.6 = (f32[1,512]{1,0:T(1,128)S(1)}, f32[1,512]{1,0:T(1,128)S(1)}, u32[]{:S(2)}, u32[]{:S(2)}) collective-permute-start(f32[1,512]{1,0:T(1,128)S(1)} %shard_map.80.refs_0_.refs_1_), channel_id=1, source_target_pairs={{0,12},{8,24},{16,28},{24,20},{4,8},{12,0},{20,4},{28,16},{1,13},{... | collective-permute-start | bytes 6152 | tf_op jit(solution)/shard_map/ppermute | solution.py:338
  17.5 0.7 %shard_map.81 = f32[32,576]{1,0:T(8,128)} custom-call(f32[1,512]{1,0:T(1,128)S(1)} %shard_map.80.refs_0_.refs_1_, f32[32,576]{1,0:T(8,128)S(1)} %get-tuple-element.35.refs_1_, bf16[32,640]{1,0:T(8,128)(2,1)S(1)} %collective-permute-done.2.refs_2_, bf16[32,640]{1,0:T(8,128)(2,1)S(1)} %collective-permute-done.3.refs_3_, ...), custom_call_target="tpu_custom_call" | custom-call | flops 73728 | bytes 313344 | tf_op jit(solution)/shard_map/pallas_call | solution.py:257
  18.2 0.0 collective-permute-done.8.refs_4_
  18.2 0.8 %collective-permute-done.7.refs_3_ = f32[1,512]{1,0:T(1,128)S(1)} collective-permute-done((f32[1,512]{1,0:T(1,128)S(1)}, f32[1,512]{1,0:T(1,128)S(1)}, u32[]{:S(2)}, u32[]{:S(2)}) %collective-permute-start.7) | collective-permute-done | bytes 2080 | tf_op jit(solution)/shard_map/ppermute | solution.py:338
  19.1 0.0 collective-permute-done.6.refs_2_
  19.1 0.6 %shard_map.82 = f32[1,512]{1,0:T(1,128)} custom-call(f32[1,512]{1,0:T(1,128)S(1)} %get-tuple-element.36.refs_0_, f32[1,512]{1,0:T(1,128)S(1)} %shard_map.80.refs_0_.refs_1_, f32[1,512]{1,0:T(1,128)S(1)} %collective-permute-done.6.refs_2_, f32[1,512]{1,0:T(1,128)S(1)} %collective-permute-done.7.refs_3_, f32[1,512]{1,0:T(1,128)S(1)} %collective-permute-done.8.refs_4_), custom_call_target="tpu_custom_call" | custom-call | flops 1536 | bytes 12288 | tf_op jit(solution)/shard_map/pallas_call | solution.py:257
  (3 shorter events, 0.0 us)
Async XLA Ops:
  0.6 1.9 %collective-permute-start = (bf16[576,128]{1,0:T(8,128)(2,1)}, bf16[576,128]{1,0:T(8,128)(2,1)S(1)}, u32[]{:S(2)}, u32[]{:S(2)}) collective-permute-start(bf16[576,128]{1,0:T(8,128)(2,1)} %bitcast.13), channel_id=1, source_target_pairs={{0,4},{4,0},{1,5},{5,1},{2,6},{6,2},{3,7},{7,3},{8,12},{12,8},{9,1... | collective-permute-start | bytes 442376 | tf_op jit(solution)/shard_map/ppermute | solution.py:22
  3.8 1.4 %collective-permute-start.1 = (bf16[4,32,640]{2,1,0:T(8,128)(2,1)S(1)}, bf16[4,32,640]{2,1,0:T(8,128)(2,1)S(1)}, u32[]{:S(2)}, u32[]{:S(2)}) collective-permute-start(bf16[4,32,640]{2,1,0:T(8,128)(2,1)S(1)} %get-tuple-element.28), channel_id=1, source_target_pairs={{0,4},{4,0},{1,5},{5,1},{2,6},{6,2},{3,7},{7,3},{8,12},{12,8},{9,1... | collective-permute-start | bytes 491528 | tf_op jit(solution)/shard_map/ppermute | solution.py:22
  5.2 6.1 %copy-start = (bf16[1,128,576]{1,2,0:T(8,128)(2,1)S(1)}, bf16[1,128,576]{1,2,0:T(8,128)(2,1)}, u32[]{:S(2)}) copy-start(bf16[1,128,576]{1,2,0:T(8,128)(2,1)} %param.7) | copy-start | bytes 442372
  5.5 7.0 %collective-permute-start.2 = (bf16[32,640]{1,0:T(8,128)(2,1)S(1)}, bf16[32,640]{1,0:T(8,128)(2,1)S(1)}, u32[]{:S(2)}, u32[]{:S(2)}) collective-permute-start(bf16[32,640]{1,0:T(8,128)(2,1)S(1)} %get-tuple-element.31), channel_id=1, source_target_pairs={{0,4},{1,5},{2,0},{3,7},{4,6},{5,1},{6,2},{7,3},{8,12},{9,13},{10,... | collective-permute-start | bytes 122888 | tf_op jit(solution)/shard_map/ppermute | solution.py:69
  5.7 7.1 %collective-permute-start.3 = (bf16[32,640]{1,0:T(8,128)(2,1)S(1)}, bf16[32,640]{1,0:T(8,128)(2,1)S(1)}, u32[]{:S(2)}, u32[]{:S(2)}) collective-permute-start(bf16[32,640]{1,0:T(8,128)(2,1)S(1)} %get-tuple-element.32), channel_id=1, source_target_pairs={{0,1},{1,2},{2,3},{3,0},{4,5},{5,7},{6,4},{7,6},{8,9},{9,10},{10,1... | collective-permute-start | bytes 122888 | tf_op jit(solution)/shard_map/ppermute | solution.py:69
  8.6 4.8 %collective-permute-start.4 = (bf16[32,640]{1,0:T(8,128)(2,1)S(1)}, bf16[32,640]{1,0:T(8,128)(2,1)S(1)}, u32[]{:S(2)}, u32[]{:S(2)}) collective-permute-start(bf16[32,640]{1,0:T(8,128)(2,1)S(1)} %get-tuple-element.33), channel_id=1, source_target_pairs={{0,3},{1,0},{2,1},{3,2},{4,7},{5,6},{6,5},{7,4},{8,11},{9,8},{10,9... | collective-permute-start | bytes 122888 | tf_op jit(solution)/shard_map/ppermute | solution.py:69
  10.6 2.7 %collective-permute-start.5 = (bf16[32,640]{1,0:T(8,128)(2,1)S(1)}, bf16[32,640]{1,0:T(8,128)(2,1)S(1)}, u32[]{:S(2)}, u32[]{:S(2)}) collective-permute-start(bf16[32,640]{1,0:T(8,128)(2,1)S(1)} %get-tuple-element.34), channel_id=1, source_target_pairs={{0,2},{1,3},{2,6},{3,1},{4,0},{5,4},{6,7},{7,5},{8,10},{9,11},{10,... | collective-permute-start | bytes 122888 | tf_op jit(solution)/shard_map/ppermute | solution.py:69
  13.4 4.8 %collective-permute-start.8 = (f32[1,512]{1,0:T(1,128)S(1)}, f32[1,512]{1,0:T(1,128)S(1)}, u32[]{:S(2)}, u32[]{:S(2)}) collective-permute-start(f32[1,512]{1,0:T(1,128)S(1)} %shard_map.80.refs_0_.refs_1_), channel_id=1, source_target_pairs={{0,16},{8,20},{16,8},{24,4},{4,24},{12,28},{20,0},{28,12},{1,17},{... | collective-permute-start | bytes 6152 | tf_op jit(solution)/shard_map/ppermute | solution.py:338
  15.1 3.9 %collective-permute-start.7 = (f32[1,512]{1,0:T(1,128)S(1)}, f32[1,512]{1,0:T(1,128)S(1)}, u32[]{:S(2)}, u32[]{:S(2)}) collective-permute-start(f32[1,512]{1,0:T(1,128)S(1)} %shard_map.80.refs_0_.refs_1_), channel_id=1, source_target_pairs={{0,20},{8,16},{16,12},{24,8},{4,28},{12,4},{20,24},{28,0},{1,21},{... | collective-permute-start | bytes 6152 | tf_op jit(solution)/shard_map/ppermute | solution.py:338
  15.4 3.6 %collective-permute-start.6 = (f32[1,512]{1,0:T(1,128)S(1)}, f32[1,512]{1,0:T(1,128)S(1)}, u32[]{:S(2)}, u32[]{:S(2)}) collective-permute-start(f32[1,512]{1,0:T(1,128)S(1)} %shard_map.80.refs_0_.refs_1_), channel_id=1, source_target_pairs={{0,12},{8,24},{16,28},{24,20},{4,8},{12,0},{20,4},{28,16},{1,13},{... | collective-permute-start | bytes 6152 | tf_op jit(solution)/shard_map/ppermute | solution.py:338

commit v5 on v4

--- a/solution.py
+++ b/solution.py
@@ -13,6 +13,8 @@
 TAIL = 64
 TAIL_ROWS = LATENT // TAIL
 
+QUERY_PARTS = 2
+
 NT = (((1,), (1,)), ((), ()))
 F32, BF16 = jnp.float32, jnp.bfloat16
 
@@ -23,50 +25,82 @@
 
 
 EXP_STEPS = (
-    (4, 5, 0, 7, 6, 1, 2, 3),
-    (1, 2, 3, 0, 5, 7, 4, 6),
-    (3, 0, 1, 2, 7, 6, 5, 4),
-    (2, 3, 6, 1, 0, 4, 7, 5),
+    ((4, 5, 0, 7, 6, 1, 2, 3), (1, 2, 3, 0, 5, 7, 4, 6), (3, 0, 1, 2, 7, 6, 5, 4), (2, 3, 6, 1, 0, 4, 7, 5)),
+    ((4, 5, 0, 7, 6, 1, 2, 3), (1, 2, 3, 0, 5, 7, 4, 6), (3, 0, 1, 2, 7, 6, 5, 4), (2, 3, 6, 1, 0, 4, 7, 5)),
+    ((4, 5, 0, 7, 6, 1, 2, 3), (1, 2, 3, 0, 5, 7, 4, 6), (3, 0, 1, 2, 7, 6, 5, 4), (2, 3, 6, 1, 0, 4, 7, 5)),
+    ((4, 5, 0, 7, 6, 1, 2, 3), (1, 2, 3, 0, 5, 7, 4, 6), (3, 0, 1, 2, 7, 6, 5, 4), (2, 3, 6, 1, 0, 4, 7, 5)),
 )
-DP_STEPS = ((2, 6, 1, 4, 3, 7, 0, 5), (6, 2, 5, 1, 7, 4, 3, 0), (5, 3, 7, 6, 1, 0, 4, 2))
+DP_STEPS = (
+    ((1, 2, 7, 6, 3, 0, 5, 4), (5, 3, 1, 2, 7, 6, 4, 0), (6, 7, 3, 1, 2, 4, 0, 5)),
+    ((6, 2, 5, 0, 7, 3, 1, 4), (5, 6, 7, 1, 3, 0, 4, 2), (2, 7, 3, 5, 1, 4, 0, 6)),
+    ((6, 7, 0, 1, 2, 3, 5, 4), (7, 6, 3, 0, 1, 2, 4, 5), (5, 0, 7, 6, 3, 4, 1, 2)),
+    ((6, 3, 5, 0, 2, 7, 1, 4), (7, 4, 0, 2, 5, 6, 3, 1), (3, 0, 4, 6, 1, 2, 7, 5)),
+)
 
 
 def ring_steps(size):
     return tuple(tuple((i + k) % size for i in range(size)) for k in range(1, size))
 
 
-def exp_steps(exp_count, ctx_count):
-    if (exp_count, ctx_count) == (4, 2):
-        return EXP_STEPS
+def tuned(mesh_shape):
+    return mesh_shape == (4, 2, 4)
+
+
+def exp_pairs(mesh_shape):
+    dp_count, ctx_count, exp_count = mesh_shape
+    if tuned(mesh_shape):
+        return [
+            [
+                (d * 8 + k, d * 8 + to)
+                for d in range(dp_count)
+                for k, to in enumerate(EXP_STEPS[d][i])
+            ]
+            for i in range(len(EXP_STEPS[0]))
+        ]
     return [
-        [c * exp_count + to for c in range(ctx_count) for to in step]
+        [
+            (group * exp_count + i, group * exp_count + to)
+            for group in range(dp_count * ctx_count)
+            for i, to in enumerate(step)
+        ]
         for step in ring_steps(exp_count)
     ]
 
 
-def dp_pairs(dp_count, ctx_count):
-    if (dp_count, ctx_count) == (4, 2):
+def dp_pairs(mesh_shape):
+    dp_count, ctx_count, exp_count = mesh_shape
+    if tuned(mesh_shape):
         return [
-            [(k % 4 * 2 + k // 4, to % 4 * 2 + to // 4) for k, to in enumerate(step)]
-            for step in DP_STEPS
+            [
+                (k % 4 * 8 + k // 4 * 4 + z, to % 4 * 8 + to // 4 * 4 + z)
+                for z in range(exp_count)
+                for k, to in enumerate(DP_STEPS[z][i])
+            ]
+            for i in range(len(DP_STEPS[0]))
         ]
+    size = ctx_count * exp_count
     return [
-        [(i * ctx_count + c, to * ctx_count + c) for i, to in enumerate(step) for c in range(ctx_count)]
+        [(i * size + j, to * size + j) for i, to in enumerate(step) for j in range(size)]
         for step in ring_steps(dp_count)
     ]
 
 
-def target_of(core, place, step, exp_count):
-    if step not in EXP_STEPS:
-        return lax.rem(place + step[0], exp_count), True
-    target = jnp.int32(step[0])
-    for k in range(1, len(step)):
-        target = jnp.where(core * exp_count + place == k, step[k], target)
-    return lax.rem(target, exp_count), target // exp_count == core
-
-
-def send_step(value, step):
-    return lax.ppermute(value, ("ctx", "exp"), list(enumerate(step)))
+def exp_target(mesh_shape, index):
+    exp_count = mesh_shape[2]
+    place = lax.axis_index("exp")
+    if not tuned(mesh_shape):
+        return lax.rem(place + ring_steps(exp_count)[index][0], exp_count), True
+    core, row = lax.axis_index("ctx"), lax.axis_index("dp")
+    words = [sum(to << 3 * k for k, to in enumerate(column[index])) for column in EXP_STEPS]
+    word = jnp.int32(words[0])
+    for i in range(1, len(words)):
+        word = jnp.where(row == i, words[i], word)
+    target = (word >> (3 * (core * 4 + place))) & 7
+    return target & 3, (target >> 2) == core
+
+
+def send_step(value, pairs):
+    return lax.ppermute(value, ("dp", "ctx", "exp"), pairs)
 
 
 def dot(a, b):
@@ -149,24 +183,27 @@
     query_pos = query_pos_ref[...]
 
     keys = jnp.concatenate([keys_ref[...]] + [ref[...].T for ref in peer_refs], axis=0)
-    scores = dot(keys, queries_t) * SOFTMAX_SCALE
-    grad_prob = dot_nt(keys[:, :LATENT], grads)
-    key_row = lax.broadcasted_iota(jnp.int32, (rows_k, scores.shape[1]), 0)
-    visible = jnp.concatenate(
-        [key_row + lax.rem(place + b, ctx_count) * rows_k <= query_pos for b in range(ctx_count)],
-        axis=0,
-    )
-    scores = jnp.where(visible, scores, MASKED_SCORE)
-    row_max = jnp.max(scores, axis=0, keepdims=True)
-    exponent = jnp.exp(scores - row_max)
-    weights = exponent * (1.0 / jnp.sum(exponent, axis=0, keepdims=True))
-    row_delta = jnp.sum(weights * grad_prob, axis=0, keepdims=True)
-    dscore = (weights * (grad_prob - row_delta)).astype(BF16)
-    weights_low = weights.astype(BF16)
-    dscore_ref[...] = dscore
-
-    key_part = dot_nt(dscore, queries_t) * SOFTMAX_SCALE
-    latent_part = key_part[:, :LATENT] + dot(weights_low, grads)
+    part = queries_t.shape[1] // QUERY_PARTS
+    parts = [slice(p * part, (p + 1) * part) for p in range(QUERY_PARTS)]
+    scores = [dot(keys, queries_t[:, p]) * SOFTMAX_SCALE for p in parts]
+    grad_prob = [dot_nt(keys[:, :LATENT], grads[p]) for p in parts]
+    key_row = lax.broadcasted_iota(jnp.int32, (rows_k, part), 0)
+    key_pos = jnp.concatenate(
+        [key_row + lax.rem(place + b, ctx_count) * rows_k for b in range(ctx_count)], axis=0
+    )
+    key_part = value_part = 0.0
+    for i, p in enumerate(parts):
+        masked = jnp.where(key_pos <= query_pos[:, p], scores[i], MASKED_SCORE)
+        row_max = jnp.max(masked, axis=0, keepdims=True)
+        exponent = jnp.exp(masked - row_max)
+        weights = exponent * (1.0 / jnp.sum(exponent, axis=0, keepdims=True))
+        row_delta = jnp.sum(weights * grad_prob[i], axis=0, keepdims=True)
+        dscore = (weights * (grad_prob[i] - row_delta)).astype(BF16)
+        dscore_ref[:, p] = dscore
+        key_part += dot_nt(dscore, queries_t[:, p])
+        value_part += dot(weights.astype(BF16), grads[p])
+    key_part = key_part * SOFTMAX_SCALE
+    latent_part = key_part[:, :LATENT] + value_part
     gain = jnp.sum(latent_part * keys[:, :LATENT].astype(F32), axis=0, keepdims=True)
     gain_ref[...] = gain
     tail = gain_tail(gain)
@@ -194,12 +231,13 @@
         dq_ref[h] = dq_t[:, h * rows_q : (h + 1) * rows_q].astype(BF16)
 
 
-def pair_kernel(ctx_count, *refs):
+def pair_kernel(mesh_shape, *refs):
+    ctx_count = mesh_shape[1]
     own_ref, gain_ref = refs[:2]
     recv_refs = refs[2 : 1 + ctx_count]
     kept_ref, gain_out = refs[1 + ctx_count : 3 + ctx_count]
     send_refs = refs[3 + ctx_count :]
-    exp_count, share, width = own_ref.shape
+    share, width = own_ref.shape[1:]
 
     def block(i):
         rows = own_ref[i]
@@ -213,10 +251,9 @@
         gain = gain + tail_gain(jnp.concatenate(tail, axis=0).astype(F32))
     gain_out[...] = gain
     tail = gain_tail(gain)
-    core, place = lax.axis_index("ctx"), lax.axis_index("exp")
-    kept_ref[...] = block(place)
-    for step, ref in zip(exp_steps(exp_count, ctx_count), send_refs):
-        target, sends = target_of(core, place, step, exp_count)
+    kept_ref[...] = block(lax.axis_index("exp"))
+    for index, ref in enumerate(send_refs):
+        target, sends = exp_target(mesh_shape, index)
         if ref.shape[0] > share:
             ref[...] = jnp.zeros(ref.shape, ref.dtype)
         rows = block(target)
@@ -324,9 +361,10 @@
         2 * rows_all * keys_all * width,
     )
     message = bf16(max(share, 2 * TAIL_ROWS), width + TAIL)
-    steps = exp_steps(exp_count, ctx_count)
+    mesh_shape = (lax.axis_size("dp"), ctx_count, exp_count)
+    steps = exp_pairs(mesh_shape)
     kept, gain, *sends = call(
-        lambda *refs: pair_kernel(ctx_count, *refs),
+        lambda *refs: pair_kernel(mesh_shape, *refs),
         [f32(share, width), f32(1, LATENT)] + [message] * len(steps),
         [own, gain, *received],
         rows_k * width * ctx_count,
@@ -334,8 +372,7 @@
     received = [send_step(send, step) for send, step in zip(sends, steps)]
     (gain,) = call(gain_kernel, [f32(1, LATENT)], [gain, mark, *received], LATENT * exp_count)
 
-    pairs = dp_pairs(lax.axis_size("dp"), ctx_count)
-    gains = [lax.ppermute(gain, ("dp", "ctx"), step) for step in reversed(pairs)]
+    gains = [send_step(gain, step) for step in reversed(dp_pairs(mesh_shape))]
     (grad_keys,) = call(
         rows_kernel, [f32(share, width)], [gain, kept, *received], share * width * exp_count
     )

time: 19.8 us -> 19.8 us (level)
  no operation moved by 1% of the time
where the time goes in v5:
time: 19.8 us; the launch traced here: 19.7 us
  starting transfers between devices  10.8 us (55%)
  Pallas kernels  5.41 us (27%)
  waiting for transfers between devices  2.85 us (14%)
  between operations  0.66 us (3%)
    ppermute x7, starting transfers between devices, send_step(): return lax.ppermute(value, ('dp', 'ctx', 'exp'), pairs)  10 us
    pallas_call x7, Pallas kernels, call(): pl.pallas_call(kernel, out_shape=list(out_shapes), in_specs=[pl.BlockSpec...  5.41 us
    ppermute x7, waiting for transfers between devices, send_step(): return lax.ppermute(value, ('dp', 'ctx', 'exp'), pairs)  1.65 us
    ppermute x2, waiting for transfers between devices, shift(): lax.ppermute(value, axis, [(i, (i - step) % size) for i in range(size)])  1.2 us
    ppermute x2, starting transfers between devices, shift(): lax.ppermute(value, axis, [(i, (i - step) % size) for i in range(size)])  0.72 us
  transfers between devices with their start and end apart: 9, of which 4 were waited for; matrix products, arithmetic and copies ran while one was open for 0% of the time, Pallas kernels for 16%

profile of v5, /device:TPU:0, one launch (start us, length us, event | category | flops | bytes accessed | tf_op | source)
XLA Modules:
  0.0 19.7 jit_solution(6176951008053254410)
XLA Ops:
  0.6 0.5 %collective-permute-start = (bf16[576,128]{1,0:T(8,128)(2,1)}, bf16[576,128]{1,0:T(8,128)(2,1)S(1)}, u32[]{:S(2)}, u32[]{:S(2)}) collective-permute-start(bf16[576,128]{1,0:T(8,128)(2,1)} %bitcast.13), channel_id=1, source_target_pairs={{0,4},{4,0},{1,5},{5,1},{2,6},{6,2},{3,7},{7,3},{8,12},{12,8},{9,1... | collective-permute-start | bytes 442376 | tf_op jit(solution)/shard_map/ppermute | solution.py:24
  1.1 1.4 %shard_map.76 = (bf16[576,512]{1,0:T(8,128)(2,1)S(1)}, bf16[512,512]{1,0:T(8,128)(2,1)S(1)}, bf16[128,576]{1,0:T(8,128)(2,1)S(1)}, s32[1,512]{1,0:T(1,128)S(1)}, f32[1,512]{1,0:T(1,128)S(1)}) custom-call(s32[1,2]{1,0:T(1,128)} %groups_hbm.1, f32[1,512]{1,0:T(1,128)} %bitcast.19, bf16[4,576,128]{2,1,0:T(8,128)(2,1)} %bitcast.16, ...), custom_call_target="tpu_custom_call" | custom-call | flops 294912 | bytes 2529288 | tf_op jit(solution)/shard_map/pallas_call | solution.py:294
  2.5 0.0 collective-permute-done.refs_4_.refs_2_
  2.5 1.3 %shard_map.77 = (bf16[256,512]{1,0:T(8,128)(2,1)S(1)}, f32[4,32,576]{2,1,0:T(8,128)S(1)}, f32[1,512]{1,0:T(1,128)S(1)}, bf16[4,32,640]{2,1,0:T(8,128)(2,1)S(1)}) custom-call(bf16[576,512]{1,0:T(8,128)(2,1)S(1)} %get-tuple-element.20.refs_0_, bf16[512,512]{1,0:T(8,128)(2,1)S(1)} %get-tuple-element.21.refs_1_, bf16[128,576]{1,0:T(8,128)(2,1)S(1)} %get-tuple-element.22.refs_2_, ...), custom_call_target="tpu_custom_call" | custom-call | flops 570425344 | bytes 2134016 | tf_op jit(solution)/shard_map/pallas_call | solution.py:294
  3.9 0.2 %collective-permute-start.1 = (bf16[4,32,640]{2,1,0:T(8,128)(2,1)S(1)}, bf16[4,32,640]{2,1,0:T(8,128)(2,1)S(1)}, u32[]{:S(2)}, u32[]{:S(2)}) collective-permute-start(bf16[4,32,640]{2,1,0:T(8,128)(2,1)S(1)} %get-tuple-element.28), channel_id=1, source_target_pairs={{0,4},{4,0},{1,5},{5,1},{2,6},{6,2},{3,7},{7,3},{8,12},{12,8},{9,1... | collective-permute-start | bytes 491528 | tf_op jit(solution)/shard_map/ppermute | solution.py:24
  4.1 1.2 %collective-permute-done.1.refs_2_ = bf16[4,32,640]{2,1,0:T(8,128)(2,1)S(1)} collective-permute-done((bf16[4,32,640]{2,1,0:T(8,128)(2,1)S(1)}, bf16[4,32,640]{2,1,0:T(8,128)(2,1)S(1)}, u32[]{:S(2)}, u32[]{:S(2)}) %collective-permute-start.1) | collective-permute-done | bytes 163872 | tf_op jit(solution)/shard_map/ppermute | solution.py:24
  5.3 0.2 %shard_map.79 = (f32[32,576]{1,0:T(8,128)S(1)}, f32[1,512]{1,0:T(1,128)S(1)}, bf16[32,640]{1,0:T(8,128)(2,1)S(1)}, bf16[32,640]{1,0:T(8,128)(2,1)S(1)}, bf16[32,...) custom-call(f32[4,32,576]{2,1,0:T(8,128)S(1)} %get-tuple-element.26.refs_0_, f32[1,512]{1,0:T(1,128)S(1)} %get-tuple-element.27.refs_1_, ...), custom_call_target="tpu_custom_call" | custom-call | flops 147456 | bytes 700416 | tf_op jit(solution)/shard_map/pallas_call | solution.py:294
  5.5 0.2 %collective-permute-start.2 = (bf16[32,640]{1,0:T(8,128)(2,1)S(1)}, bf16[32,640]{1,0:T(8,128)(2,1)S(1)}, u32[]{:S(2)}, u32[]{:S(2)}) collective-permute-start(bf16[32,640]{1,0:T(8,128)(2,1)S(1)} %get-tuple-element.31), channel_id=1, source_target_pairs={{0,4},{1,5},{2,0},{3,7},{4,6},{5,1},{6,2},{7,3},{8,12},{9,13},{10,... | collective-permute-start | bytes 122888 | tf_op jit(solution)/shard_map/ppermute | solution.py:103
  5.7 2.9 %collective-permute-start.3 = (bf16[32,640]{1,0:T(8,128)(2,1)S(1)}, bf16[32,640]{1,0:T(8,128)(2,1)S(1)}, u32[]{:S(2)}, u32[]{:S(2)}) collective-permute-start(bf16[32,640]{1,0:T(8,128)(2,1)S(1)} %get-tuple-element.32), channel_id=1, source_target_pairs={{0,1},{1,2},{2,3},{3,0},{4,5},{5,7},{6,4},{7,6},{8,9},{9,10},{10,1... | collective-permute-start | bytes 122888 | tf_op jit(solution)/shard_map/ppermute | solution.py:103
  8.6 2.0 %collective-permute-start.4 = (bf16[32,640]{1,0:T(8,128)(2,1)S(1)}, bf16[32,640]{1,0:T(8,128)(2,1)S(1)}, u32[]{:S(2)}, u32[]{:S(2)}) collective-permute-start(bf16[32,640]{1,0:T(8,128)(2,1)S(1)} %get-tuple-element.33), channel_id=1, source_target_pairs={{0,3},{1,0},{2,1},{3,2},{4,7},{5,6},{6,5},{7,4},{8,11},{9,8},{10,9... | collective-permute-start | bytes 122888 | tf_op jit(solution)/shard_map/ppermute | solution.py:103
  10.7 0.8 %collective-permute-start.5 = (bf16[32,640]{1,0:T(8,128)(2,1)S(1)}, bf16[32,640]{1,0:T(8,128)(2,1)S(1)}, u32[]{:S(2)}, u32[]{:S(2)}) collective-permute-start(bf16[32,640]{1,0:T(8,128)(2,1)S(1)} %get-tuple-element.34), channel_id=1, source_target_pairs={{0,2},{1,3},{2,6},{3,1},{4,0},{5,4},{6,7},{7,5},{8,10},{9,11},{10,... | collective-permute-start | bytes 122888 | tf_op jit(solution)/shard_map/ppermute | solution.py:103
  11.4 1.1 %shard_map.78 = (bf16[4,576,128]{2,1,0:T(8,128)(2,1)}, f32[1,128]{1,0:T(1,128)S(1)}) custom-call(bf16[256,512]{1,0:T(8,128)(2,1)S(1)} %get-tuple-element.24.refs_0_, bf16[576,128]{1,0:T(8,128)(2,1)S(1)} %bitcast.15, bf16[576,128]{1,0:T(8,128)(2,1)S(1)} %collective-permute-done.refs_4_.refs_2_), custom_call_target="tpu_custom_call" | custom-call | flops 150994944 | bytes 1147392 | tf_op jit(solution)/shard_map/pallas_call | solution.py:294
  12.6 0.0 collective-permute-done.2.refs_2_
  12.6 0.3 %collective-permute-done.3.refs_3_ = bf16[32,640]{1,0:T(8,128)(2,1)S(1)} collective-permute-done((bf16[32,640]{1,0:T(8,128)(2,1)S(1)}, bf16[32,640]{1,0:T(8,128)(2,1)S(1)}, u32[]{:S(2)}, u32[]{:S(2)}) %collective-permute-start.3) | collective-permute-done | bytes 40992 | tf_op jit(solution)/shard_map/ppermute | solution.py:103
  12.8 0.5 %collective-permute-done.4.refs_4_ = bf16[32,640]{1,0:T(8,128)(2,1)S(1)} collective-permute-done((bf16[32,640]{1,0:T(8,128)(2,1)S(1)}, bf16[32,640]{1,0:T(8,128)(2,1)S(1)}, u32[]{:S(2)}, u32[]{:S(2)}) %collective-permute-start.4) | collective-permute-done | bytes 40992 | tf_op jit(solution)/shard_map/ppermute | solution.py:103
  13.4 0.1 shard_map.80.refs_0_.refs_1_
  13.5 1.7 %collective-permute-start.8 = (f32[1,512]{1,0:T(1,128)S(1)}, f32[1,512]{1,0:T(1,128)S(1)}, u32[]{:S(2)}, u32[]{:S(2)}) collective-permute-start(f32[1,512]{1,0:T(1,128)S(1)} %shard_map.80.refs_0_.refs_1_), channel_id=1, source_target_pairs={{0,8},{8,16},{16,28},{24,20},{4,24},{12,0},{20,12},{28,4},{1,21},{... | collective-permute-start | bytes 6152 | tf_op jit(solution)/shard_map/ppermute | solution.py:103
  15.2 0.3 %collective-permute-start.7 = (f32[1,512]{1,0:T(1,128)S(1)}, f32[1,512]{1,0:T(1,128)S(1)}, u32[]{:S(2)}, u32[]{:S(2)}) collective-permute-start(f32[1,512]{1,0:T(1,128)S(1)} %shard_map.80.refs_0_.refs_1_), channel_id=1, source_target_pairs={{0,12},{8,24},{16,8},{24,16},{4,28},{12,20},{20,4},{28,0},{1,13},{... | collective-permute-start | bytes 6152 | tf_op jit(solution)/shard_map/ppermute | solution.py:103
  15.4 2.2 %collective-permute-start.6 = (f32[1,512]{1,0:T(1,128)S(1)}, f32[1,512]{1,0:T(1,128)S(1)}, u32[]{:S(2)}, u32[]{:S(2)}) collective-permute-start(f32[1,512]{1,0:T(1,128)S(1)} %shard_map.80.refs_0_.refs_1_), channel_id=1, source_target_pairs={{0,20},{8,28},{16,24},{24,8},{4,16},{12,4},{20,0},{28,12},{1,17},{... | collective-permute-start | bytes 6152 | tf_op jit(solution)/shard_map/ppermute | solution.py:103
  17.6 0.7 %shard_map.81 = f32[32,576]{1,0:T(8,128)} custom-call(f32[1,512]{1,0:T(1,128)S(1)} %shard_map.80.refs_0_.refs_1_, f32[32,576]{1,0:T(8,128)S(1)} %get-tuple-element.35.refs_1_, bf16[32,640]{1,0:T(8,128)(2,1)S(1)} %collective-permute-done.2.refs_2_, bf16[32,640]{1,0:T(8,128)(2,1)S(1)} %collective-permute-done.3.refs_3_, ...), custom_call_target="tpu_custom_call" | custom-call | flops 73728 | bytes 313344 | tf_op jit(solution)/shard_map/pallas_call | solution.py:294
  18.3 0.0 collective-permute-done.8.refs_4_
  18.3 0.8 %collective-permute-done.7.refs_3_ = f32[1,512]{1,0:T(1,128)S(1)} collective-permute-done((f32[1,512]{1,0:T(1,128)S(1)}, f32[1,512]{1,0:T(1,128)S(1)}, u32[]{:S(2)}, u32[]{:S(2)}) %collective-permute-start.7) | collective-permute-done | bytes 2080 | tf_op jit(solution)/shard_map/ppermute | solution.py:103
  19.1 0.0 collective-permute-done.6.refs_2_
  19.1 0.6 %shard_map.82 = f32[1,512]{1,0:T(1,128)} custom-call(f32[1,512]{1,0:T(1,128)S(1)} %get-tuple-element.36.refs_0_, f32[1,512]{1,0:T(1,128)S(1)} %shard_map.80.refs_0_.refs_1_, f32[1,512]{1,0:T(1,128)S(1)} %collective-permute-done.6.refs_2_, f32[1,512]{1,0:T(1,128)S(1)} %collective-permute-done.7.refs_3_, f32[1,512]{1,0:T(1,128)S(1)} %collective-permute-done.8.refs_4_), custom_call_target="tpu_custom_call" | custom-call | flops 1536 | bytes 12288 | tf_op jit(solution)/shard_map/pallas_call | solution.py:294
  (3 shorter events, 0.0 us)
Async XLA Ops:
  0.6 1.9 %collective-permute-start = (bf16[576,128]{1,0:T(8,128)(2,1)}, bf16[576,128]{1,0:T(8,128)(2,1)S(1)}, u32[]{:S(2)}, u32[]{:S(2)}) collective-permute-start(bf16[576,128]{1,0:T(8,128)(2,1)} %bitcast.13), channel_id=1, source_target_pairs={{0,4},{4,0},{1,5},{5,1},{2,6},{6,2},{3,7},{7,3},{8,12},{12,8},{9,1... | collective-permute-start | bytes 442376 | tf_op jit(solution)/shard_map/ppermute | solution.py:24
  3.9 1.4 %collective-permute-start.1 = (bf16[4,32,640]{2,1,0:T(8,128)(2,1)S(1)}, bf16[4,32,640]{2,1,0:T(8,128)(2,1)S(1)}, u32[]{:S(2)}, u32[]{:S(2)}) collective-permute-start(bf16[4,32,640]{2,1,0:T(8,128)(2,1)S(1)} %get-tuple-element.28), channel_id=1, source_target_pairs={{0,4},{4,0},{1,5},{5,1},{2,6},{6,2},{3,7},{7,3},{8,12},{12,8},{9,1... | collective-permute-start | bytes 491528 | tf_op jit(solution)/shard_map/ppermute | solution.py:24
  5.3 6.2 %copy-start = (bf16[1,128,576]{1,2,0:T(8,128)(2,1)S(1)}, bf16[1,128,576]{1,2,0:T(8,128)(2,1)}, u32[]{:S(2)}) copy-start(bf16[1,128,576]{1,2,0:T(8,128)(2,1)} %param.7) | copy-start | bytes 442372
  5.5 7.1 %collective-permute-start.2 = (bf16[32,640]{1,0:T(8,128)(2,1)S(1)}, bf16[32,640]{1,0:T(8,128)(2,1)S(1)}, u32[]{:S(2)}, u32[]{:S(2)}) collective-permute-start(bf16[32,640]{1,0:T(8,128)(2,1)S(1)} %get-tuple-element.31), channel_id=1, source_target_pairs={{0,4},{1,5},{2,0},{3,7},{4,6},{5,1},{6,2},{7,3},{8,12},{9,13},{10,... | collective-permute-start | bytes 122888 | tf_op jit(solution)/shard_map/ppermute | solution.py:103
  5.7 7.1 %collective-permute-start.3 = (bf16[32,640]{1,0:T(8,128)(2,1)S(1)}, bf16[32,640]{1,0:T(8,128)(2,1)S(1)}, u32[]{:S(2)}, u32[]{:S(2)}) collective-permute-start(bf16[32,640]{1,0:T(8,128)(2,1)S(1)} %get-tuple-element.32), channel_id=1, source_target_pairs={{0,1},{1,2},{2,3},{3,0},{4,5},{5,7},{6,4},{7,6},{8,9},{9,10},{10,1... | collective-permute-start | bytes 122888 | tf_op jit(solution)/shard_map/ppermute | solution.py:103
  8.6 4.8 %collective-permute-start.4 = (bf16[32,640]{1,0:T(8,128)(2,1)S(1)}, bf16[32,640]{1,0:T(8,128)(2,1)S(1)}, u32[]{:S(2)}, u32[]{:S(2)}) collective-permute-start(bf16[32,640]{1,0:T(8,128)(2,1)S(1)} %get-tuple-element.33), channel_id=1, source_target_pairs={{0,3},{1,0},{2,1},{3,2},{4,7},{5,6},{6,5},{7,4},{8,11},{9,8},{10,9... | collective-permute-start | bytes 122888 | tf_op jit(solution)/shard_map/ppermute | solution.py:103
  10.7 2.7 %collective-permute-start.5 = (bf16[32,640]{1,0:T(8,128)(2,1)S(1)}, bf16[32,640]{1,0:T(8,128)(2,1)S(1)}, u32[]{:S(2)}, u32[]{:S(2)}) collective-permute-start(bf16[32,640]{1,0:T(8,128)(2,1)S(1)} %get-tuple-element.34), channel_id=1, source_target_pairs={{0,2},{1,3},{2,6},{3,1},{4,0},{5,4},{6,7},{7,5},{8,10},{9,11},{10,... | collective-permute-start | bytes 122888 | tf_op jit(solution)/shard_map/ppermute | solution.py:103
  13.5 4.8 %collective-permute-start.8 = (f32[1,512]{1,0:T(1,128)S(1)}, f32[1,512]{1,0:T(1,128)S(1)}, u32[]{:S(2)}, u32[]{:S(2)}) collective-permute-start(f32[1,512]{1,0:T(1,128)S(1)} %shard_map.80.refs_0_.refs_1_), channel_id=1, source_target_pairs={{0,8},{8,16},{16,28},{24,20},{4,24},{12,0},{20,12},{28,4},{1,21},{... | collective-permute-start | bytes 6152 | tf_op jit(solution)/shard_map/ppermute | solution.py:103
  15.2 3.9 %collective-permute-start.7 = (f32[1,512]{1,0:T(1,128)S(1)}, f32[1,512]{1,0:T(1,128)S(1)}, u32[]{:S(2)}, u32[]{:S(2)}) collective-permute-start(f32[1,512]{1,0:T(1,128)S(1)} %shard_map.80.refs_0_.refs_1_), channel_id=1, source_target_pairs={{0,12},{8,24},{16,8},{24,16},{4,28},{12,20},{20,4},{28,0},{1,13},{... | collective-permute-start | bytes 6152 | tf_op jit(solution)/shard_map/ppermute | solution.py:103
  15.4 3.7 %collective-permute-start.6 = (f32[1,512]{1,0:T(1,128)S(1)}, f32[1,512]{1,0:T(1,128)S(1)}, u32[]{:S(2)}, u32[]{:S(2)}) collective-permute-start(f32[1,512]{1,0:T(1,128)S(1)} %shard_map.80.refs_0_.refs_1_), channel_id=1, source_target_pairs={{0,20},{8,28},{16,24},{24,8},{4,16},{12,4},{20,0},{28,12},{1,17},{... | collective-permute-start | bytes 6152 | tf_op jit(solution)/shard_map/ppermute | solution.py:103

commit v6 on v5

--- a/solution.py
+++ b/solution.py
@@ -12,8 +12,6 @@
 MASKED_SCORE = -1e30
 TAIL = 64
 TAIL_ROWS = LATENT // TAIL
-
-QUERY_PARTS = 2
 
 NT = (((1,), (1,)), ((), ()))
 F32, BF16 = jnp.float32, jnp.bfloat16
@@ -183,27 +181,24 @@
     query_pos = query_pos_ref[...]
 
     keys = jnp.concatenate([keys_ref[...]] + [ref[...].T for ref in peer_refs], axis=0)
-    part = queries_t.shape[1] // QUERY_PARTS
-    parts = [slice(p * part, (p + 1) * part) for p in range(QUERY_PARTS)]
-    scores = [dot(keys, queries_t[:, p]) * SOFTMAX_SCALE for p in parts]
-    grad_prob = [dot_nt(keys[:, :LATENT], grads[p]) for p in parts]
-    key_row = lax.broadcasted_iota(jnp.int32, (rows_k, part), 0)
-    key_pos = jnp.concatenate(
-        [key_row + lax.rem(place + b, ctx_count) * rows_k for b in range(ctx_count)], axis=0
-    )
-    key_part = value_part = 0.0
-    for i, p in enumerate(parts):
-        masked = jnp.where(key_pos <= query_pos[:, p], scores[i], MASKED_SCORE)
-        row_max = jnp.max(masked, axis=0, keepdims=True)
-        exponent = jnp.exp(masked - row_max)
-        weights = exponent * (1.0 / jnp.sum(exponent, axis=0, keepdims=True))
-        row_delta = jnp.sum(weights * grad_prob[i], axis=0, keepdims=True)
-        dscore = (weights * (grad_prob[i] - row_delta)).astype(BF16)
-        dscore_ref[:, p] = dscore
-        key_part += dot_nt(dscore, queries_t[:, p])
-        value_part += dot(weights.astype(BF16), grads[p])
-    key_part = key_part * SOFTMAX_SCALE
-    latent_part = key_part[:, :LATENT] + value_part
+    scores = dot(keys, queries_t) * SOFTMAX_SCALE
+    grad_prob = dot_nt(keys[:, :LATENT], grads)
+    key_row = lax.broadcasted_iota(jnp.int32, (rows_k, scores.shape[1]), 0)
+    visible = jnp.concatenate(
+        [key_row + lax.rem(place + b, ctx_count) * rows_k <= query_pos for b in range(ctx_count)],
+        axis=0,
+    )
+    scores = jnp.where(visible, scores, MASKED_SCORE)
+    row_max = jnp.max(scores, axis=0, keepdims=True)
+    exponent = jnp.exp(scores - row_max)
+    weights = exponent * (1.0 / jnp.sum(exponent, axis=0, keepdims=True))
+    row_delta = jnp.sum(weights * grad_prob, axis=0, keepdims=True)
+    dscore = (weights * (grad_prob - row_delta)).astype(BF16)
+    weights_low = weights.astype(BF16)
+    dscore_ref[...] = dscore
+
+    key_part = dot_nt(dscore, queries_t) * SOFTMAX_SCALE
+    latent_part = key_part[:, :LATENT] + dot(weights_low, grads)
     gain = jnp.sum(latent_part * keys[:, :LATENT].astype(F32), axis=0, keepdims=True)
     gain_ref[...] = gain
     tail = gain_tail(gain)

time: 19.8 us -> 19.8 us (level)
  no operation moved by 1% of the time
where the time goes in v6:
time: 19.8 us; the launch traced here: 19.6 us
  starting transfers between devices  10.8 us (55%)
  Pallas kernels  5.35 us (27%)
  waiting for transfers between devices  2.84 us (14%)
  between operations  0.66 us (3%)
    ppermute x7, starting transfers between devices, send_step(): return lax.ppermute(value, ('dp', 'ctx', 'exp'), pairs)  10 us
    pallas_call x7, Pallas kernels, call(): pl.pallas_call(kernel, out_shape=list(out_shapes), in_specs=[pl.BlockSpec...  5.35 us
    ppermute x7, waiting for transfers between devices, send_step(): return lax.ppermute(value, ('dp', 'ctx', 'exp'), pairs)  1.64 us
    ppermute x2, waiting for transfers between devices, shift(): lax.ppermute(value, axis, [(i, (i - step) % size) for i in range(size)])  1.2 us
    ppermute x2, starting transfers between devices, shift(): lax.ppermute(value, axis, [(i, (i - step) % size) for i in range(size)])  0.72 us
  transfers between devices with their start and end apart: 9, of which 4 were waited for; matrix products, arithmetic and copies ran while one was open for 0% of the time, Pallas kernels for 16%

profile of v6, /device:TPU:0, one launch (start us, length us, event | category | flops | bytes accessed | tf_op | source)
XLA Modules:
  0.0 19.6 jit_solution(6191552266223155578)
XLA Ops:
  0.6 0.5 %collective-permute-start = (bf16[576,128]{1,0:T(8,128)(2,1)}, bf16[576,128]{1,0:T(8,128)(2,1)S(1)}, u32[]{:S(2)}, u32[]{:S(2)}) collective-permute-start(bf16[576,128]{1,0:T(8,128)(2,1)} %bitcast.13), channel_id=1, source_target_pairs={{0,4},{4,0},{1,5},{5,1},{2,6},{6,2},{3,7},{7,3},{8,12},{12,8},{9,1... | collective-permute-start | bytes 442376 | tf_op jit(solution)/shard_map/ppermute | solution.py:22
  1.1 1.4 %shard_map.76 = (bf16[576,512]{1,0:T(8,128)(2,1)S(1)}, bf16[512,512]{1,0:T(8,128)(2,1)S(1)}, bf16[128,576]{1,0:T(8,128)(2,1)S(1)}, s32[1,512]{1,0:T(1,128)S(1)}, f32[1,512]{1,0:T(1,128)S(1)}) custom-call(s32[1,2]{1,0:T(1,128)} %groups_hbm.1, f32[1,512]{1,0:T(1,128)} %bitcast.19, bf16[4,576,128]{2,1,0:T(8,128)(2,1)} %bitcast.16, ...), custom_call_target="tpu_custom_call" | custom-call | flops 294912 | bytes 2529288 | tf_op jit(solution)/shard_map/pallas_call | solution.py:289
  2.5 0.0 collective-permute-done.refs_4_.refs_2_
  2.5 1.3 %shard_map.77 = (bf16[256,512]{1,0:T(8,128)(2,1)S(1)}, f32[4,32,576]{2,1,0:T(8,128)S(1)}, f32[1,512]{1,0:T(1,128)S(1)}, bf16[4,32,640]{2,1,0:T(8,128)(2,1)S(1)}) custom-call(bf16[576,512]{1,0:T(8,128)(2,1)S(1)} %get-tuple-element.20.refs_0_, bf16[512,512]{1,0:T(8,128)(2,1)S(1)} %get-tuple-element.21.refs_1_, bf16[128,576]{1,0:T(8,128)(2,1)S(1)} %get-tuple-element.22.refs_2_, ...), custom_call_target="tpu_custom_call" | custom-call | flops 570425344 | bytes 2134016 | tf_op jit(solution)/shard_map/pallas_call | solution.py:289
  3.8 0.2 %collective-permute-start.1 = (bf16[4,32,640]{2,1,0:T(8,128)(2,1)S(1)}, bf16[4,32,640]{2,1,0:T(8,128)(2,1)S(1)}, u32[]{:S(2)}, u32[]{:S(2)}) collective-permute-start(bf16[4,32,640]{2,1,0:T(8,128)(2,1)S(1)} %get-tuple-element.28), channel_id=1, source_target_pairs={{0,4},{4,0},{1,5},{5,1},{2,6},{6,2},{3,7},{7,3},{8,12},{12,8},{9,1... | collective-permute-start | bytes 491528 | tf_op jit(solution)/shard_map/ppermute | solution.py:22
  4.0 1.2 %collective-permute-done.1.refs_2_ = bf16[4,32,640]{2,1,0:T(8,128)(2,1)S(1)} collective-permute-done((bf16[4,32,640]{2,1,0:T(8,128)(2,1)S(1)}, bf16[4,32,640]{2,1,0:T(8,128)(2,1)S(1)}, u32[]{:S(2)}, u32[]{:S(2)}) %collective-permute-start.1) | collective-permute-done | bytes 163872 | tf_op jit(solution)/shard_map/ppermute | solution.py:22
  5.2 0.2 %shard_map.79 = (f32[32,576]{1,0:T(8,128)S(1)}, f32[1,512]{1,0:T(1,128)S(1)}, bf16[32,640]{1,0:T(8,128)(2,1)S(1)}, bf16[32,640]{1,0:T(8,128)(2,1)S(1)}, bf16[32,...) custom-call(f32[4,32,576]{2,1,0:T(8,128)S(1)} %get-tuple-element.26.refs_0_, f32[1,512]{1,0:T(1,128)S(1)} %get-tuple-element.27.refs_1_, ...), custom_call_target="tpu_custom_call" | custom-call | flops 147456 | bytes 700416 | tf_op jit(solution)/shard_map/pallas_call | solution.py:289
  5.5 0.2 %collective-permute-start.2 = (bf16[32,640]{1,0:T(8,128)(2,1)S(1)}, bf16[32,640]{1,0:T(8,128)(2,1)S(1)}, u32[]{:S(2)}, u32[]{:S(2)}) collective-permute-start(bf16[32,640]{1,0:T(8,128)(2,1)S(1)} %get-tuple-element.31), channel_id=1, source_target_pairs={{0,4},{1,5},{2,0},{3,7},{4,6},{5,1},{6,2},{7,3},{8,12},{9,13},{10,... | collective-permute-start | bytes 122888 | tf_op jit(solution)/shard_map/ppermute | solution.py:101
  5.7 2.9 %collective-permute-start.3 = (bf16[32,640]{1,0:T(8,128)(2,1)S(1)}, bf16[32,640]{1,0:T(8,128)(2,1)S(1)}, u32[]{:S(2)}, u32[]{:S(2)}) collective-permute-start(bf16[32,640]{1,0:T(8,128)(2,1)S(1)} %get-tuple-element.32), channel_id=1, source_target_pairs={{0,1},{1,2},{2,3},{3,0},{4,5},{5,7},{6,4},{7,6},{8,9},{9,10},{10,1... | collective-permute-start | bytes 122888 | tf_op jit(solution)/shard_map/ppermute | solution.py:101
  8.6 2.0 %collective-permute-start.4 = (bf16[32,640]{1,0:T(8,128)(2,1)S(1)}, bf16[32,640]{1,0:T(8,128)(2,1)S(1)}, u32[]{:S(2)}, u32[]{:S(2)}) collective-permute-start(bf16[32,640]{1,0:T(8,128)(2,1)S(1)} %get-tuple-element.33), channel_id=1, source_target_pairs={{0,3},{1,0},{2,1},{3,2},{4,7},{5,6},{6,5},{7,4},{8,11},{9,8},{10,9... | collective-permute-start | bytes 122888 | tf_op jit(solution)/shard_map/ppermute | solution.py:101
  10.6 0.8 %collective-permute-start.5 = (bf16[32,640]{1,0:T(8,128)(2,1)S(1)}, bf16[32,640]{1,0:T(8,128)(2,1)S(1)}, u32[]{:S(2)}, u32[]{:S(2)}) collective-permute-start(bf16[32,640]{1,0:T(8,128)(2,1)S(1)} %get-tuple-element.34), channel_id=1, source_target_pairs={{0,2},{1,3},{2,6},{3,1},{4,0},{5,4},{6,7},{7,5},{8,10},{9,11},{10,... | collective-permute-start | bytes 122888 | tf_op jit(solution)/shard_map/ppermute | solution.py:101
  11.4 1.1 %shard_map.78 = (bf16[4,576,128]{2,1,0:T(8,128)(2,1)}, f32[1,128]{1,0:T(1,128)S(1)}) custom-call(bf16[256,512]{1,0:T(8,128)(2,1)S(1)} %get-tuple-element.24.refs_0_, bf16[576,128]{1,0:T(8,128)(2,1)S(1)} %bitcast.15, bf16[576,128]{1,0:T(8,128)(2,1)S(1)} %collective-permute-done.refs_4_.refs_2_), custom_call_target="tpu_custom_call" | custom-call | flops 150994944 | bytes 1147392 | tf_op jit(solution)/shard_map/pallas_call | solution.py:289
  12.5 0.0 collective-permute-done.2.refs_2_
  12.5 0.3 %collective-permute-done.3.refs_3_ = bf16[32,640]{1,0:T(8,128)(2,1)S(1)} collective-permute-done((bf16[32,640]{1,0:T(8,128)(2,1)S(1)}, bf16[32,640]{1,0:T(8,128)(2,1)S(1)}, u32[]{:S(2)}, u32[]{:S(2)}) %collective-permute-start.3) | collective-permute-done | bytes 40992 | tf_op jit(solution)/shard_map/ppermute | solution.py:101
  12.8 0.5 %collective-permute-done.4.refs_4_ = bf16[32,640]{1,0:T(8,128)(2,1)S(1)} collective-permute-done((bf16[32,640]{1,0:T(8,128)(2,1)S(1)}, bf16[32,640]{1,0:T(8,128)(2,1)S(1)}, u32[]{:S(2)}, u32[]{:S(2)}) %collective-permute-start.4) | collective-permute-done | bytes 40992 | tf_op jit(solution)/shard_map/ppermute | solution.py:101
  13.3 0.0 collective-permute-done.5.refs_5_
  13.3 0.1 shard_map.80.refs_0_.refs_1_
  13.4 1.7 %collective-permute-start.8 = (f32[1,512]{1,0:T(1,128)S(1)}, f32[1,512]{1,0:T(1,128)S(1)}, u32[]{:S(2)}, u32[]{:S(2)}) collective-permute-start(f32[1,512]{1,0:T(1,128)S(1)} %shard_map.80.refs_0_.refs_1_), channel_id=1, source_target_pairs={{0,8},{8,16},{16,28},{24,20},{4,24},{12,0},{20,12},{28,4},{1,21},{... | collective-permute-start | bytes 6152 | tf_op jit(solution)/shard_map/ppermute | solution.py:101
  15.1 0.3 %collective-permute-start.7 = (f32[1,512]{1,0:T(1,128)S(1)}, f32[1,512]{1,0:T(1,128)S(1)}, u32[]{:S(2)}, u32[]{:S(2)}) collective-permute-start(f32[1,512]{1,0:T(1,128)S(1)} %shard_map.80.refs_0_.refs_1_), channel_id=1, source_target_pairs={{0,12},{8,24},{16,8},{24,16},{4,28},{12,20},{20,4},{28,0},{1,13},{... | collective-permute-start | bytes 6152 | tf_op jit(solution)/shard_map/ppermute | solution.py:101
  15.4 2.2 %collective-permute-start.6 = (f32[1,512]{1,0:T(1,128)S(1)}, f32[1,512]{1,0:T(1,128)S(1)}, u32[]{:S(2)}, u32[]{:S(2)}) collective-permute-start(f32[1,512]{1,0:T(1,128)S(1)} %shard_map.80.refs_0_.refs_1_), channel_id=1, source_target_pairs={{0,20},{8,28},{16,24},{24,8},{4,16},{12,4},{20,0},{28,12},{1,17},{... | collective-permute-start | bytes 6152 | tf_op jit(solution)/shard_map/ppermute | solution.py:101
  17.5 0.7 %shard_map.81 = f32[32,576]{1,0:T(8,128)} custom-call(f32[1,512]{1,0:T(1,128)S(1)} %shard_map.80.refs_0_.refs_1_, f32[32,576]{1,0:T(8,128)S(1)} %get-tuple-element.35.refs_1_, bf16[32,640]{1,0:T(8,128)(2,1)S(1)} %collective-permute-done.2.refs_2_, bf16[32,640]{1,0:T(8,128)(2,1)S(1)} %collective-permute-done.3.refs_3_, ...), custom_call_target="tpu_custom_call" | custom-call | flops 73728 | bytes 313344 | tf_op jit(solution)/shard_map/pallas_call | solution.py:289
  18.2 0.0 collective-permute-done.8.refs_4_
  18.2 0.8 %collective-permute-done.7.refs_3_ = f32[1,512]{1,0:T(1,128)S(1)} collective-permute-done((f32[1,512]{1,0:T(1,128)S(1)}, f32[1,512]{1,0:T(1,128)S(1)}, u32[]{:S(2)}, u32[]{:S(2)}) %collective-permute-start.7) | collective-permute-done | bytes 2080 | tf_op jit(solution)/shard_map/ppermute | solution.py:101
  19.0 0.6 %shard_map.82 = f32[1,512]{1,0:T(1,128)} custom-call(f32[1,512]{1,0:T(1,128)S(1)} %get-tuple-element.36.refs_0_, f32[1,512]{1,0:T(1,128)S(1)} %shard_map.80.refs_0_.refs_1_, f32[1,512]{1,0:T(1,128)S(1)} %collective-permute-done.6.refs_2_, f32[1,512]{1,0:T(1,128)S(1)} %collective-permute-done.7.refs_3_, f32[1,512]{1,0:T(1,128)S(1)} %collective-permute-done.8.refs_4_), custom_call_target="tpu_custom_call" | custom-call | flops 1536 | bytes 12288 | tf_op jit(solution)/shard_map/pallas_call | solution.py:289
  (3 shorter events, 0.0 us)
Async XLA Ops:
  0.6 1.9 %collective-permute-start = (bf16[576,128]{1,0:T(8,128)(2,1)}, bf16[576,128]{1,0:T(8,128)(2,1)S(1)}, u32[]{:S(2)}, u32[]{:S(2)}) collective-permute-start(bf16[576,128]{1,0:T(8,128)(2,1)} %bitcast.13), channel_id=1, source_target_pairs={{0,4},{4,0},{1,5},{5,1},{2,6},{6,2},{3,7},{7,3},{8,12},{12,8},{9,1... | collective-permute-start | bytes 442376 | tf_op jit(solution)/shard_map/ppermute | solution.py:22
  3.8 1.4 %collective-permute-start.1 = (bf16[4,32,640]{2,1,0:T(8,128)(2,1)S(1)}, bf16[4,32,640]{2,1,0:T(8,128)(2,1)S(1)}, u32[]{:S(2)}, u32[]{:S(2)}) collective-permute-start(bf16[4,32,640]{2,1,0:T(8,128)(2,1)S(1)} %get-tuple-element.28), channel_id=1, source_target_pairs={{0,4},{4,0},{1,5},{5,1},{2,6},{6,2},{3,7},{7,3},{8,12},{12,8},{9,1... | collective-permute-start | bytes 491528 | tf_op jit(solution)/shard_map/ppermute | solution.py:22
  5.2 6.2 %copy-start = (bf16[1,128,576]{1,2,0:T(8,128)(2,1)S(1)}, bf16[1,128,576]{1,2,0:T(8,128)(2,1)}, u32[]{:S(2)}) copy-start(bf16[1,128,576]{1,2,0:T(8,128)(2,1)} %param.7) | copy-start | bytes 442372
  5.5 7.0 %collective-permute-start.2 = (bf16[32,640]{1,0:T(8,128)(2,1)S(1)}, bf16[32,640]{1,0:T(8,128)(2,1)S(1)}, u32[]{:S(2)}, u32[]{:S(2)}) collective-permute-start(bf16[32,640]{1,0:T(8,128)(2,1)S(1)} %get-tuple-element.31), channel_id=1, source_target_pairs={{0,4},{1,5},{2,0},{3,7},{4,6},{5,1},{6,2},{7,3},{8,12},{9,13},{10,... | collective-permute-start | bytes 122888 | tf_op jit(solution)/shard_map/ppermute | solution.py:101
  5.7 7.1 %collective-permute-start.3 = (bf16[32,640]{1,0:T(8,128)(2,1)S(1)}, bf16[32,640]{1,0:T(8,128)(2,1)S(1)}, u32[]{:S(2)}, u32[]{:S(2)}) collective-permute-start(bf16[32,640]{1,0:T(8,128)(2,1)S(1)} %get-tuple-element.32), channel_id=1, source_target_pairs={{0,1},{1,2},{2,3},{3,0},{4,5},{5,7},{6,4},{7,6},{8,9},{9,10},{10,1... | collective-permute-start | bytes 122888 | tf_op jit(solution)/shard_map/ppermute | solution.py:101
  8.6 4.7 %collective-permute-start.4 = (bf16[32,640]{1,0:T(8,128)(2,1)S(1)}, bf16[32,640]{1,0:T(8,128)(2,1)S(1)}, u32[]{:S(2)}, u32[]{:S(2)}) collective-permute-start(bf16[32,640]{1,0:T(8,128)(2,1)S(1)} %get-tuple-element.33), channel_id=1, source_target_pairs={{0,3},{1,0},{2,1},{3,2},{4,7},{5,6},{6,5},{7,4},{8,11},{9,8},{10,9... | collective-permute-start | bytes 122888 | tf_op jit(solution)/shard_map/ppermute | solution.py:101
  10.6 2.7 %collective-permute-start.5 = (bf16[32,640]{1,0:T(8,128)(2,1)S(1)}, bf16[32,640]{1,0:T(8,128)(2,1)S(1)}, u32[]{:S(2)}, u32[]{:S(2)}) collective-permute-start(bf16[32,640]{1,0:T(8,128)(2,1)S(1)} %get-tuple-element.34), channel_id=1, source_target_pairs={{0,2},{1,3},{2,6},{3,1},{4,0},{5,4},{6,7},{7,5},{8,10},{9,11},{10,... | collective-permute-start | bytes 122888 | tf_op jit(solution)/shard_map/ppermute | solution.py:101
  13.4 4.8 %collective-permute-start.8 = (f32[1,512]{1,0:T(1,128)S(1)}, f32[1,512]{1,0:T(1,128)S(1)}, u32[]{:S(2)}, u32[]{:S(2)}) collective-permute-start(f32[1,512]{1,0:T(1,128)S(1)} %shard_map.80.refs_0_.refs_1_), channel_id=1, source_target_pairs={{0,8},{8,16},{16,28},{24,20},{4,24},{12,0},{20,12},{28,4},{1,21},{... | collective-permute-start | bytes 6152 | tf_op jit(solution)/shard_map/ppermute | solution.py:101
  15.1 3.9 %collective-permute-start.7 = (f32[1,512]{1,0:T(1,128)S(1)}, f32[1,512]{1,0:T(1,128)S(1)}, u32[]{:S(2)}, u32[]{:S(2)}) collective-permute-start(f32[1,512]{1,0:T(1,128)S(1)} %shard_map.80.refs_0_.refs_1_), channel_id=1, source_target_pairs={{0,12},{8,24},{16,8},{24,16},{4,28},{12,20},{20,4},{28,0},{1,13},{... | collective-permute-start | bytes 6152 | tf_op jit(solution)/shard_map/ppermute | solution.py:101
  15.4 3.7 %collective-permute-start.6 = (f32[1,512]{1,0:T(1,128)S(1)}, f32[1,512]{1,0:T(1,128)S(1)}, u32[]{:S(2)}, u32[]{:S(2)}) collective-permute-start(f32[1,512]{1,0:T(1,128)S(1)} %shard_map.80.refs_0_.refs_1_), channel_id=1, source_target_pairs={{0,20},{8,28},{16,24},{24,8},{4,16},{12,4},{20,0},{28,12},{1,17},{... | collective-permute-start | bytes 6152 | tf_op jit(solution)/shard_map/ppermute | solution.py:101

commit v7 on v6

--- a/solution.py
+++ b/solution.py
@@ -29,10 +29,30 @@
     ((4, 5, 0, 7, 6, 1, 2, 3), (1, 2, 3, 0, 5, 7, 4, 6), (3, 0, 1, 2, 7, 6, 5, 4), (2, 3, 6, 1, 0, 4, 7, 5)),
 )
 DP_STEPS = (
-    ((1, 2, 7, 6, 3, 0, 5, 4), (5, 3, 1, 2, 7, 6, 4, 0), (6, 7, 3, 1, 2, 4, 0, 5)),
-    ((6, 2, 5, 0, 7, 3, 1, 4), (5, 6, 7, 1, 3, 0, 4, 2), (2, 7, 3, 5, 1, 4, 0, 6)),
-    ((6, 7, 0, 1, 2, 3, 5, 4), (7, 6, 3, 0, 1, 2, 4, 5), (5, 0, 7, 6, 3, 4, 1, 2)),
-    ((6, 3, 5, 0, 2, 7, 1, 4), (7, 4, 0, 2, 5, 6, 3, 1), (3, 0, 4, 6, 1, 2, 7, 5)),
+    (
+        (4, 5, 6, 7, 2, 1, 0, 3),
+        (1, 2, 5, 0, 3, 6, 7, 4),
+        (7, 3, 1, 2, 5, 0, 4, 6),
+        (6, 7, 3, 1, 0, 4, 2, 5),
+    ),
+    (
+        (3, 6, 5, 0, 7, 2, 1, 4),
+        (6, 3, 7, 5, 1, 4, 0, 2),
+        (2, 7, 3, 1, 5, 0, 4, 6),
+        (4, 5, 6, 7, 0, 1, 2, 3),
+    ),
+    (
+        (7, 6, 5, 4, 2, 3, 0, 1),
+        (6, 7, 1, 5, 3, 2, 4, 0),
+        (5, 0, 7, 6, 1, 4, 3, 2),
+        (4, 5, 6, 7, 0, 1, 2, 3),
+    ),
+    (
+        (7, 0, 5, 1, 2, 6, 3, 4),
+        (5, 7, 0, 2, 1, 3, 4, 6),
+        (3, 4, 1, 5, 6, 2, 7, 0),
+        (4, 5, 6, 7, 0, 1, 2, 3),
+    ),
 )
 
 
@@ -97,6 +117,16 @@
     return target & 3, (target >> 2) == core
 
 
+def dp_counts(mesh_shape, index):
+    if not tuned(mesh_shape):
+        return True
+    word = 0
+    for source, to in dp_pairs(mesh_shape)[index]:
+        word |= (source // 8 != to // 8) << to
+    place = (lax.axis_index("dp") * 2 + lax.axis_index("ctx")) * 4 + lax.axis_index("exp")
+    return (jnp.int32(word - (word >> 31 << 32)) >> place) & 1 == 1
+
+
 def send_step(value, pairs):
     return lax.ppermute(value, ("dp", "ctx", "exp"), pairs)
 
@@ -273,11 +303,12 @@
     out_ref[...] = rows
 
 
-def final_kernel(*refs):
+def final_kernel(mesh_shape, *refs):
     kv_gain_ref, gain_ref, *recv_refs, gain_out = refs
     gain = gain_ref[...]
-    for ref in recv_refs:
-        gain = gain + ref[...]
+    for index, ref in enumerate(reversed(recv_refs)):
+        heard = ref[...]
+        gain = gain + jnp.where(dp_counts(mesh_shape, index), heard, jnp.zeros_like(heard))
     gain_out[...] = gain / kv_gain_ref[...]
 
 
@@ -372,7 +403,10 @@
         rows_kernel, [f32(share, width)], [gain, kept, *received], share * width * exp_count
     )
     (grad_gain,) = call(
-        final_kernel, [f32(1, LATENT)], [kv_gain_row, gain, *gains], LATENT * len(gains)
+        lambda *refs: final_kernel(mesh_shape, *refs),
+        [f32(1, LATENT)],
+        [kv_gain_row, gain, *gains],
+        LATENT * len(gains),
     )
     grad_queries = jnp.transpose(dq_t, (2, 0, 1))[None]
     return (grad_queries, grad_keys[None, None], grad_gain.reshape(LATENT))

time: 19.8 us -> 20.2 us (1.020)
  starting transfers between devices: 10.8 us -> 11.4 us
    ppermute x7 -> x8, starting transfers between devices: 10 us -> 10.6 us  [send_step(): return lax.ppermute(value, ('dp', 'ctx', 'exp'), pairs)]
    ppermute x7 -> x8, waiting for transfers between devices: 1.64 us -> 1.45 us  [send_step(): return lax.ppermute(value, ('dp', 'ctx', 'exp'), pairs)]
  transfers between devices with their start and end apart: 9 -> 10, of which waited for: 4 -> 4; matrix products, arithmetic and copies ran while one was open for 0% -> 0% of each run, Pallas kernels for 16% -> 16%
where the time goes in v7:
time: 20.2 us; the launch traced here: 20 us
  starting transfers between devices  11.4 us (56%)
  Pallas kernels  5.36 us (27%)
  waiting for transfers between devices  2.65 us (13%)
  between operations  0.66 us (3%)
    ppermute x8, starting transfers between devices, send_step(): return lax.ppermute(value, ('dp', 'ctx', 'exp'), pairs)  10.6 us
    pallas_call x7, Pallas kernels, call(): pl.pallas_call(kernel, out_shape=list(out_shapes), in_specs=[pl.BlockSpec...  5.36 us
    ppermute x8, waiting for transfers between devices, send_step(): return lax.ppermute(value, ('dp', 'ctx', 'exp'), pairs)  1.45 us
    ppermute x2, waiting for transfers between devices, shift(): lax.ppermute(value, axis, [(i, (i - step) % size) for i in range(size)])  1.2 us
    ppermute x2, starting transfers between devices, shift(): lax.ppermute(value, axis, [(i, (i - step) % size) for i in range(size)])  0.72 us
  transfers between devices with their start and end apart: 10, of which 4 were waited for; matrix products, arithmetic and copies ran while one was open for 0% of the time, Pallas kernels for 16%

profile of v7, /device:TPU:0, one launch (start us, length us, event | category | flops | bytes accessed | tf_op | source)
XLA Modules:
  0.0 20.0 jit_solution(4833572326745686018)
XLA Ops:
  0.6 0.5 %collective-permute-start = (bf16[576,128]{1,0:T(8,128)(2,1)}, bf16[576,128]{1,0:T(8,128)(2,1)S(1)}, u32[]{:S(2)}, u32[]{:S(2)}) collective-permute-start(bf16[576,128]{1,0:T(8,128)(2,1)} %bitcast.13), channel_id=1, source_target_pairs={{0,4},{4,0},{1,5},{5,1},{2,6},{6,2},{3,7},{7,3},{8,12},{12,8},{9,1... | collective-permute-start | bytes 442376 | tf_op jit(solution)/shard_map/ppermute | solution.py:22
  1.1 1.4 %shard_map.76 = (bf16[576,512]{1,0:T(8,128)(2,1)S(1)}, bf16[512,512]{1,0:T(8,128)(2,1)S(1)}, bf16[128,576]{1,0:T(8,128)(2,1)S(1)}, s32[1,512]{1,0:T(1,128)S(1)}, f32[1,512]{1,0:T(1,128)S(1)}) custom-call(s32[1,2]{1,0:T(1,128)} %groups_hbm.1, f32[1,512]{1,0:T(1,128)} %bitcast.19, bf16[4,576,128]{2,1,0:T(8,128)(2,1)} %bitcast.16, ...), custom_call_target="tpu_custom_call" | custom-call | flops 294912 | bytes 2529288 | tf_op jit(solution)/shard_map/pallas_call | solution.py:320
  2.5 0.0 collective-permute-done.refs_4_.refs_2_
  2.5 1.3 %shard_map.77 = (bf16[256,512]{1,0:T(8,128)(2,1)S(1)}, f32[4,32,576]{2,1,0:T(8,128)S(1)}, f32[1,512]{1,0:T(1,128)S(1)}, bf16[4,32,640]{2,1,0:T(8,128)(2,1)S(1)}) custom-call(bf16[576,512]{1,0:T(8,128)(2,1)S(1)} %get-tuple-element.20.refs_0_, bf16[512,512]{1,0:T(8,128)(2,1)S(1)} %get-tuple-element.21.refs_1_, bf16[128,576]{1,0:T(8,128)(2,1)S(1)} %get-tuple-element.22.refs_2_, ...), custom_call_target="tpu_custom_call" | custom-call | flops 570425344 | bytes 2134016 | tf_op jit(solution)/shard_map/pallas_call | solution.py:320
  3.8 0.2 %collective-permute-start.1 = (bf16[4,32,640]{2,1,0:T(8,128)(2,1)S(1)}, bf16[4,32,640]{2,1,0:T(8,128)(2,1)S(1)}, u32[]{:S(2)}, u32[]{:S(2)}) collective-permute-start(bf16[4,32,640]{2,1,0:T(8,128)(2,1)S(1)} %get-tuple-element.28), channel_id=1, source_target_pairs={{0,4},{4,0},{1,5},{5,1},{2,6},{6,2},{3,7},{7,3},{8,12},{12,8},{9,1... | collective-permute-start | bytes 491528 | tf_op jit(solution)/shard_map/ppermute | solution.py:22
  4.0 1.2 %collective-permute-done.1.refs_2_ = bf16[4,32,640]{2,1,0:T(8,128)(2,1)S(1)} collective-permute-done((bf16[4,32,640]{2,1,0:T(8,128)(2,1)S(1)}, bf16[4,32,640]{2,1,0:T(8,128)(2,1)S(1)}, u32[]{:S(2)}, u32[]{:S(2)}) %collective-permute-start.1) | collective-permute-done | bytes 163872 | tf_op jit(solution)/shard_map/ppermute | solution.py:22
  5.2 0.2 %shard_map.79 = (f32[32,576]{1,0:T(8,128)S(1)}, f32[1,512]{1,0:T(1,128)S(1)}, bf16[32,640]{1,0:T(8,128)(2,1)S(1)}, bf16[32,640]{1,0:T(8,128)(2,1)S(1)}, bf16[32,...) custom-call(f32[4,32,576]{2,1,0:T(8,128)S(1)} %get-tuple-element.26.refs_0_, f32[1,512]{1,0:T(1,128)S(1)} %get-tuple-element.27.refs_1_, ...), custom_call_target="tpu_custom_call" | custom-call | flops 147456 | bytes 700416 | tf_op jit(solution)/shard_map/pallas_call | solution.py:320
  5.5 0.2 %collective-permute-start.2 = (bf16[32,640]{1,0:T(8,128)(2,1)S(1)}, bf16[32,640]{1,0:T(8,128)(2,1)S(1)}, u32[]{:S(2)}, u32[]{:S(2)}) collective-permute-start(bf16[32,640]{1,0:T(8,128)(2,1)S(1)} %get-tuple-element.31), channel_id=1, source_target_pairs={{0,4},{1,5},{2,0},{3,7},{4,6},{5,1},{6,2},{7,3},{8,12},{9,13},{10,... | collective-permute-start | bytes 122888 | tf_op jit(solution)/shard_map/ppermute | solution.py:131
  5.7 2.9 %collective-permute-start.3 = (bf16[32,640]{1,0:T(8,128)(2,1)S(1)}, bf16[32,640]{1,0:T(8,128)(2,1)S(1)}, u32[]{:S(2)}, u32[]{:S(2)}) collective-permute-start(bf16[32,640]{1,0:T(8,128)(2,1)S(1)} %get-tuple-element.32), channel_id=1, source_target_pairs={{0,1},{1,2},{2,3},{3,0},{4,5},{5,7},{6,4},{7,6},{8,9},{9,10},{10,1... | collective-permute-start | bytes 122888 | tf_op jit(solution)/shard_map/ppermute | solution.py:131
  8.6 2.0 %collective-permute-start.4 = (bf16[32,640]{1,0:T(8,128)(2,1)S(1)}, bf16[32,640]{1,0:T(8,128)(2,1)S(1)}, u32[]{:S(2)}, u32[]{:S(2)}) collective-permute-start(bf16[32,640]{1,0:T(8,128)(2,1)S(1)} %get-tuple-element.33), channel_id=1, source_target_pairs={{0,3},{1,0},{2,1},{3,2},{4,7},{5,6},{6,5},{7,4},{8,11},{9,8},{10,9... | collective-permute-start | bytes 122888 | tf_op jit(solution)/shard_map/ppermute | solution.py:131
  10.6 0.8 %collective-permute-start.5 = (bf16[32,640]{1,0:T(8,128)(2,1)S(1)}, bf16[32,640]{1,0:T(8,128)(2,1)S(1)}, u32[]{:S(2)}, u32[]{:S(2)}) collective-permute-start(bf16[32,640]{1,0:T(8,128)(2,1)S(1)} %get-tuple-element.34), channel_id=1, source_target_pairs={{0,2},{1,3},{2,6},{3,1},{4,0},{5,4},{6,7},{7,5},{8,10},{9,11},{10,... | collective-permute-start | bytes 122888 | tf_op jit(solution)/shard_map/ppermute | solution.py:131
  11.4 1.1 %shard_map.78 = (bf16[4,576,128]{2,1,0:T(8,128)(2,1)}, f32[1,128]{1,0:T(1,128)S(1)}) custom-call(bf16[256,512]{1,0:T(8,128)(2,1)S(1)} %get-tuple-element.24.refs_0_, bf16[576,128]{1,0:T(8,128)(2,1)S(1)} %bitcast.15, bf16[576,128]{1,0:T(8,128)(2,1)S(1)} %collective-permute-done.refs_4_.refs_2_), custom_call_target="tpu_custom_call" | custom-call | flops 150994944 | bytes 1147392 | tf_op jit(solution)/shard_map/pallas_call | solution.py:320
  12.5 0.0 collective-permute-done.2.refs_2_
  12.5 0.3 %collective-permute-done.3.refs_3_ = bf16[32,640]{1,0:T(8,128)(2,1)S(1)} collective-permute-done((bf16[32,640]{1,0:T(8,128)(2,1)S(1)}, bf16[32,640]{1,0:T(8,128)(2,1)S(1)}, u32[]{:S(2)}, u32[]{:S(2)}) %collective-permute-start.3) | collective-permute-done | bytes 40992 | tf_op jit(solution)/shard_map/ppermute | solution.py:131
  12.8 0.5 %collective-permute-done.4.refs_4_ = bf16[32,640]{1,0:T(8,128)(2,1)S(1)} collective-permute-done((bf16[32,640]{1,0:T(8,128)(2,1)S(1)}, bf16[32,640]{1,0:T(8,128)(2,1)S(1)}, u32[]{:S(2)}, u32[]{:S(2)}) %collective-permute-start.4) | collective-permute-done | bytes 40992 | tf_op jit(solution)/shard_map/ppermute | solution.py:131
  13.3 0.1 shard_map.80.refs_0_.refs_1_
  13.4 0.8 %collective-permute-start.9 = (f32[1,512]{1,0:T(1,128)S(1)}, f32[1,512]{1,0:T(1,128)S(1)}, u32[]{:S(2)}, u32[]{:S(2)}) collective-permute-start(f32[1,512]{1,0:T(1,128)S(1)} %shard_map.80.refs_0_.refs_1_), channel_id=1, source_target_pairs={{0,4},{8,12},{16,20},{24,28},{4,16},{12,8},{20,0},{28,24},{1,25},{... | collective-permute-start | bytes 6152 | tf_op jit(solution)/shard_map/ppermute | solution.py:131
  14.2 1.5 %collective-permute-start.8 = (f32[1,512]{1,0:T(1,128)S(1)}, f32[1,512]{1,0:T(1,128)S(1)}, u32[]{:S(2)}, u32[]{:S(2)}) collective-permute-start(f32[1,512]{1,0:T(1,128)S(1)} %shard_map.80.refs_0_.refs_1_), channel_id=1, source_target_pairs={{0,8},{8,16},{16,12},{24,0},{4,24},{12,20},{20,28},{28,4},{1,21},{... | collective-permute-start | bytes 6152 | tf_op jit(solution)/shard_map/ppermute | solution.py:131
  15.7 1.8 %collective-permute-start.7 = (f32[1,512]{1,0:T(1,128)S(1)}, f32[1,512]{1,0:T(1,128)S(1)}, u32[]{:S(2)}, u32[]{:S(2)}) collective-permute-start(f32[1,512]{1,0:T(1,128)S(1)} %shard_map.80.refs_0_.refs_1_), channel_id=1, source_target_pairs={{0,28},{8,24},{16,8},{24,16},{4,12},{12,0},{20,4},{28,20},{1,17},{... | collective-permute-start | bytes 6152 | tf_op jit(solution)/shard_map/ppermute | solution.py:131
  17.5 0.6 %collective-permute-start.6 = (f32[1,512]{1,0:T(1,128)S(1)}, f32[1,512]{1,0:T(1,128)S(1)}, u32[]{:S(2)}, u32[]{:S(2)}) collective-permute-start(f32[1,512]{1,0:T(1,128)S(1)} %shard_map.80.refs_0_.refs_1_), channel_id=1, source_target_pairs={{0,20},{8,28},{16,24},{24,8},{4,0},{12,4},{20,16},{28,12},{1,5},{9... | collective-permute-start | bytes 6152 | tf_op jit(solution)/shard_map/ppermute | solution.py:131
  18.1 0.7 %shard_map.81 = f32[32,576]{1,0:T(8,128)} custom-call(f32[1,512]{1,0:T(1,128)S(1)} %shard_map.80.refs_0_.refs_1_, f32[32,576]{1,0:T(8,128)S(1)} %get-tuple-element.35.refs_1_, bf16[32,640]{1,0:T(8,128)(2,1)S(1)} %collective-permute-done.2.refs_2_, bf16[32,640]{1,0:T(8,128)(2,1)S(1)} %collective-permute-done.3.refs_3_, ...), custom_call_target="tpu_custom_call" | custom-call | flops 73728 | bytes 313344 | tf_op jit(solution)/shard_map/pallas_call | solution.py:320
  18.8 0.0 collective-permute-done.7.refs_3_
  18.8 0.6 %collective-permute-done.6.refs_2_ = f32[1,512]{1,0:T(1,128)S(1)} collective-permute-done((f32[1,512]{1,0:T(1,128)S(1)}, f32[1,512]{1,0:T(1,128)S(1)}, u32[]{:S(2)}, u32[]{:S(2)}) %collective-permute-start.6) | collective-permute-done | bytes 2080 | tf_op jit(solution)/shard_map/ppermute | solution.py:131
  19.4 0.6 %shard_map.82 = f32[1,512]{1,0:T(1,128)} custom-call(f32[1,512]{1,0:T(1,128)S(1)} %get-tuple-element.36.refs_0_, f32[1,512]{1,0:T(1,128)S(1)} %shard_map.80.refs_0_.refs_1_, f32[1,512]{1,0:T(1,128)S(1)} %collective-permute-done.6.refs_2_, f32[1,512]{1,0:T(1,128)S(1)} %collective-permute-done.7.refs_3_, f32[1,512]{1,0:T(1,128)S(1)} %collective-permute-done.8.refs_4_, ...), custom_call_target="tpu_custom_call" | custom-call | flops 2048 | bytes 14336 | tf_op jit(solution)/shard_map/pallas_call | solution.py:320
  (5 shorter events, 0.0 us)
Async XLA Ops:
  0.6 1.9 %collective-permute-start = (bf16[576,128]{1,0:T(8,128)(2,1)}, bf16[576,128]{1,0:T(8,128)(2,1)S(1)}, u32[]{:S(2)}, u32[]{:S(2)}) collective-permute-start(bf16[576,128]{1,0:T(8,128)(2,1)} %bitcast.13), channel_id=1, source_target_pairs={{0,4},{4,0},{1,5},{5,1},{2,6},{6,2},{3,7},{7,3},{8,12},{12,8},{9,1... | collective-permute-start | bytes 442376 | tf_op jit(solution)/shard_map/ppermute | solution.py:22
  3.8 1.4 %collective-permute-start.1 = (bf16[4,32,640]{2,1,0:T(8,128)(2,1)S(1)}, bf16[4,32,640]{2,1,0:T(8,128)(2,1)S(1)}, u32[]{:S(2)}, u32[]{:S(2)}) collective-permute-start(bf16[4,32,640]{2,1,0:T(8,128)(2,1)S(1)} %get-tuple-element.28), channel_id=1, source_target_pairs={{0,4},{4,0},{1,5},{5,1},{2,6},{6,2},{3,7},{7,3},{8,12},{12,8},{9,1... | collective-permute-start | bytes 491528 | tf_op jit(solution)/shard_map/ppermute | solution.py:22
  5.2 6.2 %copy-start = (bf16[1,128,576]{1,2,0:T(8,128)(2,1)S(1)}, bf16[1,128,576]{1,2,0:T(8,128)(2,1)}, u32[]{:S(2)}) copy-start(bf16[1,128,576]{1,2,0:T(8,128)(2,1)} %param.7) | copy-start | bytes 442372
  5.5 7.0 %collective-permute-start.2 = (bf16[32,640]{1,0:T(8,128)(2,1)S(1)}, bf16[32,640]{1,0:T(8,128)(2,1)S(1)}, u32[]{:S(2)}, u32[]{:S(2)}) collective-permute-start(bf16[32,640]{1,0:T(8,128)(2,1)S(1)} %get-tuple-element.31), channel_id=1, source_target_pairs={{0,4},{1,5},{2,0},{3,7},{4,6},{5,1},{6,2},{7,3},{8,12},{9,13},{10,... | collective-permute-start | bytes 122888 | tf_op jit(solution)/shard_map/ppermute | solution.py:131
  5.7 7.1 %collective-permute-start.3 = (bf16[32,640]{1,0:T(8,128)(2,1)S(1)}, bf16[32,640]{1,0:T(8,128)(2,1)S(1)}, u32[]{:S(2)}, u32[]{:S(2)}) collective-permute-start(bf16[32,640]{1,0:T(8,128)(2,1)S(1)} %get-tuple-element.32), channel_id=1, source_target_pairs={{0,1},{1,2},{2,3},{3,0},{4,5},{5,7},{6,4},{7,6},{8,9},{9,10},{10,1... | collective-permute-start | bytes 122888 | tf_op jit(solution)/shard_map/ppermute | solution.py:131
  8.6 4.7 %collective-permute-start.4 = (bf16[32,640]{1,0:T(8,128)(2,1)S(1)}, bf16[32,640]{1,0:T(8,128)(2,1)S(1)}, u32[]{:S(2)}, u32[]{:S(2)}) collective-permute-start(bf16[32,640]{1,0:T(8,128)(2,1)S(1)} %get-tuple-element.33), channel_id=1, source_target_pairs={{0,3},{1,0},{2,1},{3,2},{4,7},{5,6},{6,5},{7,4},{8,11},{9,8},{10,9... | collective-permute-start | bytes 122888 | tf_op jit(solution)/shard_map/ppermute | solution.py:131
  10.6 2.7 %collective-permute-start.5 = (bf16[32,640]{1,0:T(8,128)(2,1)S(1)}, bf16[32,640]{1,0:T(8,128)(2,1)S(1)}, u32[]{:S(2)}, u32[]{:S(2)}) collective-permute-start(bf16[32,640]{1,0:T(8,128)(2,1)S(1)} %get-tuple-element.34), channel_id=1, source_target_pairs={{0,2},{1,3},{2,6},{3,1},{4,0},{5,4},{6,7},{7,5},{8,10},{9,11},{10,... | collective-permute-start | bytes 122888 | tf_op jit(solution)/shard_map/ppermute | solution.py:131
  13.4 5.4 %collective-permute-start.9 = (f32[1,512]{1,0:T(1,128)S(1)}, f32[1,512]{1,0:T(1,128)S(1)}, u32[]{:S(2)}, u32[]{:S(2)}) collective-permute-start(f32[1,512]{1,0:T(1,128)S(1)} %shard_map.80.refs_0_.refs_1_), channel_id=1, source_target_pairs={{0,4},{8,12},{16,20},{24,28},{4,16},{12,8},{20,0},{28,24},{1,25},{... | collective-permute-start | bytes 6152 | tf_op jit(solution)/shard_map/ppermute | solution.py:131
  14.2 4.6 %collective-permute-start.8 = (f32[1,512]{1,0:T(1,128)S(1)}, f32[1,512]{1,0:T(1,128)S(1)}, u32[]{:S(2)}, u32[]{:S(2)}) collective-permute-start(f32[1,512]{1,0:T(1,128)S(1)} %shard_map.80.refs_0_.refs_1_), channel_id=1, source_target_pairs={{0,8},{8,16},{16,12},{24,0},{4,24},{12,20},{20,28},{28,4},{1,21},{... | collective-permute-start | bytes 6152 | tf_op jit(solution)/shard_map/ppermute | solution.py:131
  15.7 3.1 %collective-permute-start.7 = (f32[1,512]{1,0:T(1,128)S(1)}, f32[1,512]{1,0:T(1,128)S(1)}, u32[]{:S(2)}, u32[]{:S(2)}) collective-permute-start(f32[1,512]{1,0:T(1,128)S(1)} %shard_map.80.refs_0_.refs_1_), channel_id=1, source_target_pairs={{0,28},{8,24},{16,8},{24,16},{4,12},{12,0},{20,4},{28,20},{1,17},{... | collective-permute-start | bytes 6152 | tf_op jit(solution)/shard_map/ppermute | solution.py:131
  17.5 1.9 %collective-permute-start.6 = (f32[1,512]{1,0:T(1,128)S(1)}, f32[1,512]{1,0:T(1,128)S(1)}, u32[]{:S(2)}, u32[]{:S(2)}) collective-permute-start(f32[1,512]{1,0:T(1,128)S(1)} %shard_map.80.refs_0_.refs_1_), channel_id=1, source_target_pairs={{0,20},{8,28},{16,24},{24,8},{4,0},{12,4},{20,16},{28,12},{1,5},{9... | collective-permute-start | bytes 6152 | tf_op jit(solution)/shard_map/ppermute | solution.py:131

commit v8 on v6

--- a/solution.py
+++ b/solution.py
@@ -144,17 +144,12 @@
     groups, g_ref, key_ref, copied,
 ):
     heads, _, rows_q = q_hbm.shape
-    q_copies = [
-        pltpu.make_async_copy(
-            q_hbm.at[h], queries_ref.at[:, pl.ds(h * rows_q, rows_q)], copied.at[4 + h]
-        )
-        for h in range(heads)
-    ]
+    q_copy = pltpu.make_async_copy(q_hbm, queries_ref, copied.at[4])
     key_copy = pltpu.make_async_copy(key_hbm, key_ref, copied.at[0])
     groups_copy = pltpu.make_async_copy(groups_hbm, groups, copied.at[1])
     g_copy = pltpu.make_async_copy(g_hbm, g_ref, copied.at[2])
     gain_copy = pltpu.make_async_copy(kv_gain_hbm, kv_gain_ref, copied.at[3])
-    for copy in (g_copy, key_copy, groups_copy, *q_copies, gain_copy):
+    for copy in (g_copy, key_copy, groups_copy, q_copy, gain_copy):
         copy.start()
 
     g_copy.wait()
@@ -165,8 +160,8 @@
     query_pos_ref[...] = groups[0, lax.axis_index("ctx")] * rows_q + lax.rem(
         lax.broadcasted_iota(jnp.int32, (1, heads * rows_q), 1), rows_q
     )
-    for copy in (*q_copies, gain_copy):
-        copy.wait()
+    q_copy.wait()
+    gain_copy.wait()
 
 
 def softmax_kernel(ctx_count, *refs):
@@ -176,12 +171,12 @@
     send_refs = refs[6 + ctx_count :]
     rows_k = keys_ref.shape[0]
     place = lax.axis_index("ctx")
-    queries_t = queries_ref[...]
+    queries_t = jnp.concatenate([queries_ref[h] for h in range(queries_ref.shape[0])], axis=1)
     grads = grads_ref[...]
     query_pos = query_pos_ref[...]
 
     keys = jnp.concatenate([keys_ref[...]] + [ref[...].T for ref in peer_refs], axis=0)
-    scores = dot(keys, queries_t) * SOFTMAX_SCALE
+    scores = dot(keys, queries_t)
     grad_prob = dot_nt(keys[:, :LATENT], grads)
     key_row = lax.broadcasted_iota(jnp.int32, (rows_k, scores.shape[1]), 0)
     visible = jnp.concatenate(
@@ -190,9 +185,10 @@
     )
     scores = jnp.where(visible, scores, MASKED_SCORE)
     row_max = jnp.max(scores, axis=0, keepdims=True)
-    exponent = jnp.exp(scores - row_max)
-    weights = exponent * (1.0 / jnp.sum(exponent, axis=0, keepdims=True))
-    row_delta = jnp.sum(weights * grad_prob, axis=0, keepdims=True)
+    exponent = jnp.exp2((scores - row_max) * (SOFTMAX_SCALE * math.log2(math.e)))
+    inverse = 1.0 / jnp.sum(exponent, axis=0, keepdims=True)
+    row_delta = jnp.sum(exponent * grad_prob, axis=0, keepdims=True) * inverse
+    weights = exponent * inverse
     dscore = (weights * (grad_prob - row_delta)).astype(BF16)
     weights_low = weights.astype(BF16)
     dscore_ref[...] = dscore
@@ -319,7 +315,7 @@
     *prepared, query_pos, kv_gain_row = call(
         fetch_kernel,
         [
-            bf16(width, rows_all),
+            bf16(heads, width, rows_q),
             bf16(rows_all, LATENT),
             bf16(rows_k, width),
             jax.ShapeDtypeStruct((1, rows_all), jnp.int32),
@@ -337,7 +333,7 @@
             pltpu.SMEM(query_groups.shape, jnp.int32),
             pltpu.VMEM((rows_q, heads, LATENT), BF16),
             pltpu.VMEM((width, rows_k), BF16),
-            pltpu.SemaphoreType.DMA((4 + heads,)),
+            pltpu.SemaphoreType.DMA((5,)),
         ],
         fetch=True,
     )

time: 19.8 us -> 19.8 us (level)
  no operation moved by 1% of the time
where the time goes in v8:
time: 19.8 us; the launch traced here: 19.6 us
  starting transfers between devices  10.8 us (55%)
  Pallas kernels  5.33 us (27%)
  waiting for transfers between devices  2.81 us (14%)
  between operations  0.66 us (3%)
    ppermute x7, starting transfers between devices, send_step(): return lax.ppermute(value, ('dp', 'ctx', 'exp'), pairs)  10.1 us
    pallas_call x7, Pallas kernels, call(): pl.pallas_call(kernel, out_shape=list(out_shapes), in_specs=[pl.BlockSpec...  5.33 us
    ppermute x7, waiting for transfers between devices, send_step(): return lax.ppermute(value, ('dp', 'ctx', 'exp'), pairs)  1.64 us
    ppermute x2, waiting for transfers between devices, shift(): lax.ppermute(value, axis, [(i, (i - step) % size) for i in range(size)])  1.17 us
    ppermute x2, starting transfers between devices, shift(): lax.ppermute(value, axis, [(i, (i - step) % size) for i in range(size)])  0.76 us
  transfers between devices with their start and end apart: 9, of which 4 were waited for; matrix products, arithmetic and copies ran while one was open for 0% of the time, Pallas kernels for 16%

profile of v8, /device:TPU:0, one launch (start us, length us, event | category | flops | bytes accessed | tf_op | source)
XLA Modules:
  0.0 19.6 jit_solution(11651662951312370433)
XLA Ops:
  0.6 0.5 %collective-permute-start = (bf16[576,128]{1,0:T(8,128)(2,1)}, bf16[576,128]{1,0:T(8,128)(2,1)S(1)}, u32[]{:S(2)}, u32[]{:S(2)}) collective-permute-start(bf16[576,128]{1,0:T(8,128)(2,1)} %bitcast.13), channel_id=1, source_target_pairs={{0,4},{4,0},{1,5},{5,1},{2,6},{6,2},{3,7},{7,3},{8,12},{12,8},{9,1... | collective-permute-start | bytes 442376 | tf_op jit(solution)/shard_map/ppermute | solution.py:22
  1.1 1.3 %shard_map.76 = (bf16[4,576,128]{2,1,0:T(8,128)(2,1)S(1)}, bf16[512,512]{1,0:T(8,128)(2,1)S(1)}, bf16[128,576]{1,0:T(8,128)(2,1)S(1)}, s32[1,512]{1,0:T(1,128)S(1)}, f32[1,512]{1,0:T(1,128)S(1)}) custom-call(s32[1,2]{1,0:T(1,128)} %groups_hbm.1, f32[1,512]{1,0:T(1,128)} %bitcast.19, bf16[4,576,128]{2,1,0:T(8,128)(2,1)} %bitcast.16, ...), custom_call_target="tpu_custom_call" | custom-call | flops 294912 | bytes 2529288 | tf_op jit(solution)/shard_map/pallas_call | solution.py:285
  2.5 1.3 %shard_map.77 = (bf16[256,512]{1,0:T(8,128)(2,1)S(1)}, f32[4,32,576]{2,1,0:T(8,128)S(1)}, f32[1,512]{1,0:T(1,128)S(1)}, bf16[4,32,640]{2,1,0:T(8,128)(2,1)S(1)}) custom-call(bf16[4,576,128]{2,1,0:T(8,128)(2,1)S(1)} %get-tuple-element.20.refs_0_, bf16[512,512]{1,0:T(8,128)(2,1)S(1)} %get-tuple-element.21.refs_1_, ...), custom_call_target="tpu_custom_call" | custom-call | flops 570425344 | bytes 2134016 | tf_op jit(solution)/shard_map/pallas_call | solution.py:285
  3.8 0.2 %collective-permute-start.1 = (bf16[4,32,640]{2,1,0:T(8,128)(2,1)S(1)}, bf16[4,32,640]{2,1,0:T(8,128)(2,1)S(1)}, u32[]{:S(2)}, u32[]{:S(2)}) collective-permute-start(bf16[4,32,640]{2,1,0:T(8,128)(2,1)S(1)} %get-tuple-element.28), channel_id=1, source_target_pairs={{0,4},{4,0},{1,5},{5,1},{2,6},{6,2},{3,7},{7,3},{8,12},{12,8},{9,1... | collective-permute-start | bytes 491528 | tf_op jit(solution)/shard_map/ppermute | solution.py:22
  4.0 1.2 %collective-permute-done.1.refs_2_ = bf16[4,32,640]{2,1,0:T(8,128)(2,1)S(1)} collective-permute-done((bf16[4,32,640]{2,1,0:T(8,128)(2,1)S(1)}, bf16[4,32,640]{2,1,0:T(8,128)(2,1)S(1)}, u32[]{:S(2)}, u32[]{:S(2)}) %collective-permute-start.1) | collective-permute-done | bytes 163872 | tf_op jit(solution)/shard_map/ppermute | solution.py:22
  5.2 0.2 %shard_map.79 = (f32[32,576]{1,0:T(8,128)S(1)}, f32[1,512]{1,0:T(1,128)S(1)}, bf16[32,640]{1,0:T(8,128)(2,1)S(1)}, bf16[32,640]{1,0:T(8,128)(2,1)S(1)}, bf16[32,...) custom-call(f32[4,32,576]{2,1,0:T(8,128)S(1)} %get-tuple-element.26.refs_0_, f32[1,512]{1,0:T(1,128)S(1)} %get-tuple-element.27.refs_1_, ...), custom_call_target="tpu_custom_call" | custom-call | flops 147456 | bytes 700416 | tf_op jit(solution)/shard_map/pallas_call | solution.py:285
  5.4 0.3 %collective-permute-start.2 = (bf16[32,640]{1,0:T(8,128)(2,1)S(1)}, bf16[32,640]{1,0:T(8,128)(2,1)S(1)}, u32[]{:S(2)}, u32[]{:S(2)}) collective-permute-start(bf16[32,640]{1,0:T(8,128)(2,1)S(1)} %get-tuple-element.31), channel_id=1, source_target_pairs={{0,4},{1,5},{2,0},{3,7},{4,6},{5,1},{6,2},{7,3},{8,12},{9,13},{10,... | collective-permute-start | bytes 122888 | tf_op jit(solution)/shard_map/ppermute | solution.py:101
  5.7 2.8 %collective-permute-start.3 = (bf16[32,640]{1,0:T(8,128)(2,1)S(1)}, bf16[32,640]{1,0:T(8,128)(2,1)S(1)}, u32[]{:S(2)}, u32[]{:S(2)}) collective-permute-start(bf16[32,640]{1,0:T(8,128)(2,1)S(1)} %get-tuple-element.32), channel_id=1, source_target_pairs={{0,1},{1,2},{2,3},{3,0},{4,5},{5,7},{6,4},{7,6},{8,9},{9,10},{10,1... | collective-permute-start | bytes 122888 | tf_op jit(solution)/shard_map/ppermute | solution.py:101
  8.5 2.0 %collective-permute-start.4 = (bf16[32,640]{1,0:T(8,128)(2,1)S(1)}, bf16[32,640]{1,0:T(8,128)(2,1)S(1)}, u32[]{:S(2)}, u32[]{:S(2)}) collective-permute-start(bf16[32,640]{1,0:T(8,128)(2,1)S(1)} %get-tuple-element.33), channel_id=1, source_target_pairs={{0,3},{1,0},{2,1},{3,2},{4,7},{5,6},{6,5},{7,4},{8,11},{9,8},{10,9... | collective-permute-start | bytes 122888 | tf_op jit(solution)/shard_map/ppermute | solution.py:101
  10.6 0.8 %collective-permute-start.5 = (bf16[32,640]{1,0:T(8,128)(2,1)S(1)}, bf16[32,640]{1,0:T(8,128)(2,1)S(1)}, u32[]{:S(2)}, u32[]{:S(2)}) collective-permute-start(bf16[32,640]{1,0:T(8,128)(2,1)S(1)} %get-tuple-element.34), channel_id=1, source_target_pairs={{0,2},{1,3},{2,6},{3,1},{4,0},{5,4},{6,7},{7,5},{8,10},{9,11},{10,... | collective-permute-start | bytes 122888 | tf_op jit(solution)/shard_map/ppermute | solution.py:101
  11.4 1.1 %shard_map.78 = (bf16[4,576,128]{2,1,0:T(8,128)(2,1)}, f32[1,128]{1,0:T(1,128)S(1)}) custom-call(bf16[256,512]{1,0:T(8,128)(2,1)S(1)} %get-tuple-element.24.refs_0_, bf16[576,128]{1,0:T(8,128)(2,1)S(1)} %bitcast.15, bf16[576,128]{1,0:T(8,128)(2,1)S(1)} %collective-permute-done.refs_4_.refs_2_), custom_call_target="tpu_custom_call" | custom-call | flops 150994944 | bytes 1147392 | tf_op jit(solution)/shard_map/pallas_call | solution.py:285
  12.5 0.0 collective-permute-done.2.refs_2_
  12.5 0.3 %collective-permute-done.3.refs_3_ = bf16[32,640]{1,0:T(8,128)(2,1)S(1)} collective-permute-done((bf16[32,640]{1,0:T(8,128)(2,1)S(1)}, bf16[32,640]{1,0:T(8,128)(2,1)S(1)}, u32[]{:S(2)}, u32[]{:S(2)}) %collective-permute-start.3) | collective-permute-done | bytes 40992 | tf_op jit(solution)/shard_map/ppermute | solution.py:101
  12.8 0.5 %collective-permute-done.4.refs_4_ = bf16[32,640]{1,0:T(8,128)(2,1)S(1)} collective-permute-done((bf16[32,640]{1,0:T(8,128)(2,1)S(1)}, bf16[32,640]{1,0:T(8,128)(2,1)S(1)}, u32[]{:S(2)}, u32[]{:S(2)}) %collective-permute-start.4) | collective-permute-done | bytes 40992 | tf_op jit(solution)/shard_map/ppermute | solution.py:101
  13.3 0.0 collective-permute-done.5.refs_5_
  13.3 0.1 shard_map.80.refs_0_.refs_1_
  13.4 1.7 %collective-permute-start.8 = (f32[1,512]{1,0:T(1,128)S(1)}, f32[1,512]{1,0:T(1,128)S(1)}, u32[]{:S(2)}, u32[]{:S(2)}) collective-permute-start(f32[1,512]{1,0:T(1,128)S(1)} %shard_map.80.refs_0_.refs_1_), channel_id=1, source_target_pairs={{0,8},{8,16},{16,28},{24,20},{4,24},{12,0},{20,12},{28,4},{1,21},{... | collective-permute-start | bytes 6152 | tf_op jit(solution)/shard_map/ppermute | solution.py:101
  15.1 0.3 %collective-permute-start.7 = (f32[1,512]{1,0:T(1,128)S(1)}, f32[1,512]{1,0:T(1,128)S(1)}, u32[]{:S(2)}, u32[]{:S(2)}) collective-permute-start(f32[1,512]{1,0:T(1,128)S(1)} %shard_map.80.refs_0_.refs_1_), channel_id=1, source_target_pairs={{0,12},{8,24},{16,8},{24,16},{4,28},{12,20},{20,4},{28,0},{1,13},{... | collective-permute-start | bytes 6152 | tf_op jit(solution)/shard_map/ppermute | solution.py:101
  15.4 2.2 %collective-permute-start.6 = (f32[1,512]{1,0:T(1,128)S(1)}, f32[1,512]{1,0:T(1,128)S(1)}, u32[]{:S(2)}, u32[]{:S(2)}) collective-permute-start(f32[1,512]{1,0:T(1,128)S(1)} %shard_map.80.refs_0_.refs_1_), channel_id=1, source_target_pairs={{0,20},{8,28},{16,24},{24,8},{4,16},{12,4},{20,0},{28,12},{1,17},{... | collective-permute-start | bytes 6152 | tf_op jit(solution)/shard_map/ppermute | solution.py:101
  17.5 0.7 %shard_map.81 = f32[32,576]{1,0:T(8,128)} custom-call(f32[1,512]{1,0:T(1,128)S(1)} %shard_map.80.refs_0_.refs_1_, f32[32,576]{1,0:T(8,128)S(1)} %get-tuple-element.35.refs_1_, bf16[32,640]{1,0:T(8,128)(2,1)S(1)} %collective-permute-done.2.refs_2_, bf16[32,640]{1,0:T(8,128)(2,1)S(1)} %collective-permute-done.3.refs_3_, ...), custom_call_target="tpu_custom_call" | custom-call | flops 73728 | bytes 313344 | tf_op jit(solution)/shard_map/pallas_call | solution.py:285
  18.2 0.0 collective-permute-done.8.refs_4_
  18.2 0.8 %collective-permute-done.7.refs_3_ = f32[1,512]{1,0:T(1,128)S(1)} collective-permute-done((f32[1,512]{1,0:T(1,128)S(1)}, f32[1,512]{1,0:T(1,128)S(1)}, u32[]{:S(2)}, u32[]{:S(2)}) %collective-permute-start.7) | collective-permute-done | bytes 2080 | tf_op jit(solution)/shard_map/ppermute | solution.py:101
  19.0 0.0 collective-permute-done.6.refs_2_
  19.0 0.6 %shard_map.82 = f32[1,512]{1,0:T(1,128)} custom-call(f32[1,512]{1,0:T(1,128)S(1)} %get-tuple-element.36.refs_0_, f32[1,512]{1,0:T(1,128)S(1)} %shard_map.80.refs_0_.refs_1_, f32[1,512]{1,0:T(1,128)S(1)} %collective-permute-done.6.refs_2_, f32[1,512]{1,0:T(1,128)S(1)} %collective-permute-done.7.refs_3_, f32[1,512]{1,0:T(1,128)S(1)} %collective-permute-done.8.refs_4_), custom_call_target="tpu_custom_call" | custom-call | flops 1536 | bytes 12288 | tf_op jit(solution)/shard_map/pallas_call | solution.py:285
  (3 shorter events, 0.0 us)
Async XLA Ops:
  0.6 1.9 %collective-permute-start = (bf16[576,128]{1,0:T(8,128)(2,1)}, bf16[576,128]{1,0:T(8,128)(2,1)S(1)}, u32[]{:S(2)}, u32[]{:S(2)}) collective-permute-start(bf16[576,128]{1,0:T(8,128)(2,1)} %bitcast.13), channel_id=1, source_target_pairs={{0,4},{4,0},{1,5},{5,1},{2,6},{6,2},{3,7},{7,3},{8,12},{12,8},{9,1... | collective-permute-start | bytes 442376 | tf_op jit(solution)/shard_map/ppermute | solution.py:22
  3.8 1.4 %collective-permute-start.1 = (bf16[4,32,640]{2,1,0:T(8,128)(2,1)S(1)}, bf16[4,32,640]{2,1,0:T(8,128)(2,1)S(1)}, u32[]{:S(2)}, u32[]{:S(2)}) collective-permute-start(bf16[4,32,640]{2,1,0:T(8,128)(2,1)S(1)} %get-tuple-element.28), channel_id=1, source_target_pairs={{0,4},{4,0},{1,5},{5,1},{2,6},{6,2},{3,7},{7,3},{8,12},{12,8},{9,1... | collective-permute-start | bytes 491528 | tf_op jit(solution)/shard_map/ppermute | solution.py:22
  5.2 6.2 %copy-start = (bf16[1,128,576]{1,2,0:T(8,128)(2,1)S(1)}, bf16[1,128,576]{1,2,0:T(8,128)(2,1)}, u32[]{:S(2)}) copy-start(bf16[1,128,576]{1,2,0:T(8,128)(2,1)} %param.7) | copy-start | bytes 442372
  5.4 7.1 %collective-permute-start.2 = (bf16[32,640]{1,0:T(8,128)(2,1)S(1)}, bf16[32,640]{1,0:T(8,128)(2,1)S(1)}, u32[]{:S(2)}, u32[]{:S(2)}) collective-permute-start(bf16[32,640]{1,0:T(8,128)(2,1)S(1)} %get-tuple-element.31), channel_id=1, source_target_pairs={{0,4},{1,5},{2,0},{3,7},{4,6},{5,1},{6,2},{7,3},{8,12},{9,13},{10,... | collective-permute-start | bytes 122888 | tf_op jit(solution)/shard_map/ppermute | solution.py:101
  5.7 7.1 %collective-permute-start.3 = (bf16[32,640]{1,0:T(8,128)(2,1)S(1)}, bf16[32,640]{1,0:T(8,128)(2,1)S(1)}, u32[]{:S(2)}, u32[]{:S(2)}) collective-permute-start(bf16[32,640]{1,0:T(8,128)(2,1)S(1)} %get-tuple-element.32), channel_id=1, source_target_pairs={{0,1},{1,2},{2,3},{3,0},{4,5},{5,7},{6,4},{7,6},{8,9},{9,10},{10,1... | collective-permute-start | bytes 122888 | tf_op jit(solution)/shard_map/ppermute | solution.py:101
  8.5 4.8 %collective-permute-start.4 = (bf16[32,640]{1,0:T(8,128)(2,1)S(1)}, bf16[32,640]{1,0:T(8,128)(2,1)S(1)}, u32[]{:S(2)}, u32[]{:S(2)}) collective-permute-start(bf16[32,640]{1,0:T(8,128)(2,1)S(1)} %get-tuple-element.33), channel_id=1, source_target_pairs={{0,3},{1,0},{2,1},{3,2},{4,7},{5,6},{6,5},{7,4},{8,11},{9,8},{10,9... | collective-permute-start | bytes 122888 | tf_op jit(solution)/shard_map/ppermute | solution.py:101
  10.6 2.8 %collective-permute-start.5 = (bf16[32,640]{1,0:T(8,128)(2,1)S(1)}, bf16[32,640]{1,0:T(8,128)(2,1)S(1)}, u32[]{:S(2)}, u32[]{:S(2)}) collective-permute-start(bf16[32,640]{1,0:T(8,128)(2,1)S(1)} %get-tuple-element.34), channel_id=1, source_target_pairs={{0,2},{1,3},{2,6},{3,1},{4,0},{5,4},{6,7},{7,5},{8,10},{9,11},{10,... | collective-permute-start | bytes 122888 | tf_op jit(solution)/shard_map/ppermute | solution.py:101
  13.4 4.8 %collective-permute-start.8 = (f32[1,512]{1,0:T(1,128)S(1)}, f32[1,512]{1,0:T(1,128)S(1)}, u32[]{:S(2)}, u32[]{:S(2)}) collective-permute-start(f32[1,512]{1,0:T(1,128)S(1)} %shard_map.80.refs_0_.refs_1_), channel_id=1, source_target_pairs={{0,8},{8,16},{16,28},{24,20},{4,24},{12,0},{20,12},{28,4},{1,21},{... | collective-permute-start | bytes 6152 | tf_op jit(solution)/shard_map/ppermute | solution.py:101
  15.1 3.9 %collective-permute-start.7 = (f32[1,512]{1,0:T(1,128)S(1)}, f32[1,512]{1,0:T(1,128)S(1)}, u32[]{:S(2)}, u32[]{:S(2)}) collective-permute-start(f32[1,512]{1,0:T(1,128)S(1)} %shard_map.80.refs_0_.refs_1_), channel_id=1, source_target_pairs={{0,12},{8,24},{16,8},{24,16},{4,28},{12,20},{20,4},{28,0},{1,13},{... | collective-permute-start | bytes 6152 | tf_op jit(solution)/shard_map/ppermute | solution.py:101
  15.4 3.7 %collective-permute-start.6 = (f32[1,512]{1,0:T(1,128)S(1)}, f32[1,512]{1,0:T(1,128)S(1)}, u32[]{:S(2)}, u32[]{:S(2)}) collective-permute-start(f32[1,512]{1,0:T(1,128)S(1)} %shard_map.80.refs_0_.refs_1_), channel_id=1, source_target_pairs={{0,20},{8,28},{16,24},{24,8},{4,16},{12,4},{20,0},{28,12},{1,17},{... | collective-permute-start | bytes 6152 | tf_op jit(solution)/shard_map/ppermute | solution.py:101
